TPU v7x, 256 devices: a whole 4x4x8 slice. The times are simulated.
256 devices in a mesh: row: 32 (over z, y), col: 8 (over x, core).
Axes of the slice: x: 4, y: 4, z: 8, core: 2. Of those that a mesh axis runs over, the one named last changes fastest.
Arguments:
- tokens: bfloat16 [256, 12288], P('col', 'row'), may hold values from -6 to 6
- grad_out: bfloat16 [256, 12288], P('col', 'row'), may hold values from -1 to 1
- up_weight: bfloat16 [12288, 24576], P('row', 'col'), may hold values from -0.0546875 to 0.0546875
- down_weight: bfloat16 [24576, 12288], P('col', 'row'), may hold values from -0.0390625 to 0.0390625
Outputs:
- grad_in: bfloat16 [256, 12288], P('col', 'row')
- grad_up: bfloat16 [12288, 24576], P('row', 'col')
- grad_down: bfloat16 [24576, 12288], P('col', 'row')
All inputs are finite; a program needn't handle non-finite values.
Results may differ from a plain program's by a relative error of at most 0.0049.
Values may be sent and summed in bfloat16 or wider, within the bound.
No kernel may reach another device: no remote copies, remote signals or barrier semaphores. Data moves between devices by JAX's collectives and lax.ppermute only.
A program may use at most 64 MiB of HBM per device.

v0:
```python
import jax
import jax.numpy as jnp
from jax import lax
from jax.sharding import PartitionSpec as P


def contract(left, right, left_dim, right_dim):
    return lax.dot_general(
        left, right, (((left_dim,), (right_dim,)), ((), ())), preferred_element_type=jnp.float32
    )


def gelu_tanh(values):
    return jax.nn.gelu(values, approximate=True)


def gelu_slope(values):
    return jax.jvp(gelu_tanh, (values,), (jnp.ones_like(values),))[1]


def shards(tokens, grad_out, up_weight, down_weight):
    tok_cols, grad_cols = (
        lax.all_gather(tokens, "col", axis=0, tiled=True),
        lax.all_gather(grad_out, "col", axis=0, tiled=True),
    )
    hidden_cols = up_weight.shape[1]
    tok_rows = tok_cols
    grad_rows = grad_cols
    forward_part = jnp.dot(tok_rows, up_weight, preferred_element_type=jnp.float32)
    backward_part = contract(grad_rows, down_weight, 1, 1)
    summed = lax.psum_scatter(
        jnp.concatenate([forward_part, backward_part], axis=1),
        "row",
        scatter_dimension=0,
        tiled=True,
    )
    pre_act = summed[:, :hidden_cols]
    grad_hidden = summed[:, hidden_cols:]
    hidden = gelu_tanh(pre_act).astype(jnp.bfloat16)
    grad_pre = (grad_hidden * gelu_slope(pre_act)).astype(jnp.bfloat16)
    hidden_piece = lax.all_gather(hidden, "row", axis=0, tiled=True)
    pre_piece = lax.all_gather(grad_pre, "row", axis=0, tiled=True)
    tok_rows = tok_cols
    grad_rows = grad_cols
    up_total = contract(tok_rows, pre_piece, 0, 0)
    down_total = contract(hidden_piece, grad_rows, 0, 0)
    in_total = contract(pre_piece, up_weight, 1, 1)
    grad_in = lax.psum_scatter(in_total, "col", scatter_dimension=0, tiled=True).astype(
        jnp.bfloat16
    )
    return (grad_in, up_total.astype(jnp.bfloat16), down_total.astype(jnp.bfloat16))


def solution(mesh):
    return jax.shard_map(
        shards,
        mesh=mesh,
        in_specs=(P("col", "row"), P("col", "row"), P("row", "col"), P("col", "row")),
        out_specs=(P("col", "row"), P("row", "col"), P("col", "row")),
        check_vma=False,
    )
```

profile of v0, /device:TPU:24, one launch (start us, length us, event | category | flops | bytes accessed | tf_op | source)
XLA Modules:
  0.0 465.3 jit_solution(3436880166051864134)
XLA Ops:
  7.2 0.0 copy-start
  7.2 0.0 reduce-scatter.3.cloned.1.call-start
  7.2 13.5 %all_gather.12 = bf16[256,384]{1,0:T(8,128)(2,1)S(1)} all-gather(bf16[32,384]{1,0:T(8,128)(2,1)} %param.4), channel_id=1, replica_groups=mesh['row'=32,'col'=8] {'col'}, dimensions={0}, use_global_device_ids=true | all-gather | bytes 221184 | tf_op jit(solution)/shard_map/all_gather | solution.py:23
  20.7 13.0 %all_gather.13 = bf16[256,384]{1,0:T(8,128)(2,1)S(1)} all-gather(bf16[32,384]{1,0:T(8,128)(2,1)} %param.5), channel_id=1, replica_groups=mesh['row'=32,'col'=8] {'col'}, dimensions={0}, use_global_device_ids=true | all-gather | bytes 221184 | tf_op jit(solution)/shard_map/all_gather | solution.py:24
  33.7 2.7 fusion.14
  36.4 1.0 fusion.13
  37.4 3.1 pad_maximum_fusion
  40.5 0.0 reduce-scatter.3.cloned.1.call-update
  40.5 0.0 all-gather.3.cloned.1.call-start
  40.5 226.1 %reduce-scatter.3.cloned.1.call-done = f32[8,6144]{1,0:T(8,128)} async-done(((f32[256,6144]{1,0:T(8,128)}), f32[8,6144]{1,0:T(8,128)}) %reduce-scatter.3.cloned.1.call-update) | async-done | bytes 196624 | tf_op jit(solution)/shard_map/reduce_scatter | solution.py:31
  266.7 1.6 multiply_convert_fusion
  268.3 0.0 all-gather.3.cloned.1.call-update
  268.3 0.0 all-gather.5.cloned.1.call-start
  268.4 0.7 all-gather.5.cloned.1.call-update
  269.1 0.0 reduce-scatter.5.cloned.1.call-start
  269.1 76.3 %all-gather.3.cloned.1.call-done = bf16[256,3072]{1,0:T(8,128)(2,1)} async-done(((bf16[8,3072]{1,0:T(8,128)(2,1)}), bf16[256,3072]{1,0:T(8,128)(2,1)}) %all-gather.3.cloned.1.call-update) | async-done | bytes 1572880 | tf_op jit(solution)/shard_map/all_gather | solution.py:42
  345.4 3.2 fusion.15
  348.5 0.0 reduce-scatter.5.cloned.1.call-update
  348.6 3.8 fusion
  352.4 4.3 copy.7
  356.7 66.3 %all-gather.5.cloned.1.call-done = bf16[256,3072]{1,0:T(8,128)(2,1)} async-done(((bf16[8,3072]{1,0:T(8,128)(2,1)}), bf16[256,3072]{1,0:T(8,128)(2,1)}) %all-gather.5.cloned.1.call-update) | async-done | bytes 1572880 | tf_op jit(solution)/shard_map/all_gather | solution.py:41
  423.0 3.8 convolution_convert_fusion
  426.8 30.5 %reduce-scatter.5.cloned.1.call-done = f32[32,384]{1,0:T(8,128)} async-done(((f32[256,384]{1,0:T(8,128)}), f32[32,384]{1,0:T(8,128)}) %reduce-scatter.5.cloned.1.call-update) | async-done | bytes 49168 | tf_op jit(solution)/shard_map/reduce_scatter | solution.py:48
  457.3 1.4 convert_element_type.19
  (1 shorter events, 0.0 us)
Async XLA Ops:
  7.2 29.2 %copy-start = (bf16[384,3072]{1,0:T(8,128)(2,1)S(1)}, bf16[384,3072]{1,0:T(8,128)(2,1)}, u32[]{:S(2)}) copy-start(bf16[384,3072]{1,0:T(8,128)(2,1)} %param.6) | copy-start | bytes 7077892
  7.2 259.5 %reduce-scatter.3.cloned.1.call-start = ((), (), s32[]{:S(2)}) async-start(), calls=%async_computation.2 | async-start | bytes 6488064 | tf_op jit(solution)/shard_map/reduce_scatter | solution.py:31
  40.5 304.9 %all-gather.3.cloned.1.call-start = ((), (), s32[]{:S(2)}) async-start(), calls=%async_computation.3 | async-start | bytes 1622016 | tf_op jit(solution)/shard_map/all_gather | solution.py:42
  268.3 154.6 %all-gather.5.cloned.1.call-start = ((), (), s32[]{:S(2)}) async-start(), calls=%async_computation.5 | async-start | bytes 1622016 | tf_op jit(solution)/shard_map/all_gather | solution.py:41
  269.1 188.2 %reduce-scatter.5.cloned.1.call-start = ((), (), s32[]{:S(2)}) async-start(), calls=%async_computation.4 | async-start | bytes 442368 | tf_op jit(solution)/shard_map/reduce_scatter | solution.py:48
Sparse Core Ops, SparseCore 0:
  40.6 226.0 reduce-scatter.2
  270.2 75.1 all-gather.2
  348.3 74.6 all-gather.4
  425.5 31.7 reduce-scatter.4
where the time goes:
time: 466 us; the launch traced here: 465 us
  waiting for transfers between devices  400 us (86%)
  blocking collectives  26.5 us (6%)
  matrix products  14.5 us (3%)
  between operations  13.8 us (3%)
  other arithmetic  6.15 us (1%)
    reduce_scatter x1, waiting for transfers between devices, shards(): lax.psum_scatter(jnp.concatenate([forward_part, backward_part], axis=1),...  226 us
    all_gather x1, waiting for transfers between devices, shards(): pre_piece = lax.all_gather(grad_pre, 'row', axis=0, tiled=True)  76.3 us
    all_gather x1, waiting for transfers between devices, shards(): hidden_piece = lax.all_gather(hidden, 'row', axis=0, tiled=True)  66.3 us
    reduce_scatter x1, waiting for transfers between devices, shards(): lax.psum_scatter(in_total, 'col', scatter_dimension=0, tiled=True)  30.5 us
    all_gather x1, blocking collectives, shards(): lax.all_gather(tokens, 'col', axis=0, tiled=True)  13.5 us
    dot_general x4, matrix products, contract(): lax.dot_general(left, right, (((left_dim,), (right_dim,)), ((), ())), pre...  13.5 us
    all_gather x1, blocking collectives, shards(): lax.all_gather(grad_out, 'col', axis=0, tiled=True)  13 us
  transfers between devices with their start and end apart: 4, of which 4 were waited for; matrix products, arithmetic and copies ran while one was open for 3% of the time, Pallas kernels for 0%

commit v1 on v0

v1 whole, which is shorter than its diff:
```python
import jax
import jax.numpy as jnp
from jax import lax
from jax.sharding import Mesh, PartitionSpec as P

F32, BF16 = jnp.float32, jnp.bfloat16
COL = ("x", "core")
NZ, NY, NC = 8, 4, 8
CHUNKS = 1


def contract(left, right, left_dim, right_dim):
    return lax.dot_general(
        left, right, (((left_dim,), (right_dim,)), ((), ())), preferred_element_type=F32
    )


def gelu_tanh(values):
    return jax.nn.gelu(values, approximate=True)


def gelu_slope(values):
    return jax.jvp(gelu_tanh, (values,), (jnp.ones_like(values),))[1]


def shift_y(value, by):
    return lax.ppermute(value, "y", [(i, (i + by) % NY) for i in range(NY)])


def reduce_y(pre, back):
    rows = pre.shape[0] // NY
    f = [pre[d * rows : (d + 1) * rows] for d in range(NY)]
    g = [back[d * rows : (d + 1) * rows] for d in range(NY)]
    up = shift_y(jnp.concatenate([f[2], g[1]]), 1)
    down = shift_y(jnp.concatenate([g[2], f[3]]), -1)
    up2 = shift_y((f[1].astype(F32) + up[:rows].astype(F32)).astype(BF16), 1)
    down2 = shift_y((g[3].astype(F32) + down[:rows].astype(F32)).astype(BF16), -1)
    pre_sum = f[0].astype(F32) + down[rows:].astype(F32) + up2.astype(F32)
    back_sum = g[0].astype(F32) + up[rows:].astype(F32) + down2.astype(F32)
    return pre_sum, back_sum


def reduce_z(pre, back):
    both = jnp.concatenate([pre, back], axis=1).astype(BF16)
    rows = both.shape[0] // NZ
    parts = lax.all_to_all(both.reshape(NZ, rows, -1), "z", 0, 0)
    total = parts.astype(F32).sum(axis=0)
    return total[:, : pre.shape[1]], total[:, pre.shape[1] :]


def gather_z(value):
    return lax.all_gather(value, "z", axis=0, tiled=True)


def gather_y(hidden, grad):
    rows = hidden.shape[0]
    both = jnp.concatenate([hidden, grad])
    below = shift_y(both, 1)
    above = shift_y(both, -1)
    far_hidden = shift_y(below[:rows], 1)
    far_grad = shift_y(above[rows:], -1)
    return (
        jnp.concatenate([hidden, above[:rows], far_hidden, below[:rows]]),
        jnp.concatenate([grad, above[rows:], far_grad, below[rows:]]),
    )


def shards(tokens, grad_out, up_weight, down_weight):
    width = tokens.shape[1]
    both = lax.all_gather(jnp.concatenate([tokens, grad_out], axis=1), COL, axis=0, tiled=True)
    n_tok = both.shape[0]
    block = n_tok // NY
    start = lax.axis_index("y") * block
    both = lax.dynamic_slice_in_dim(jnp.concatenate([both, both]), start, n_tok, axis=0)
    tok, grad = both[:, :width], both[:, width:]

    hidden_cols = up_weight.shape[1]
    chunk = hidden_cols // CHUNKS
    ups, downs, in_total = [], [], 0.0
    for k in range(CHUNKS):
        up_w = up_weight[:, k * chunk : (k + 1) * chunk]
        down_w = down_weight[k * chunk : (k + 1) * chunk]
        pre = jnp.dot(tok, up_w, preferred_element_type=F32).astype(BF16)
        back = contract(grad, down_w, 1, 1).astype(BF16)
        pre_act, grad_hidden = reduce_z(*reduce_y(pre, back))
        hidden = gelu_tanh(pre_act).astype(BF16)
        grad_pre = (grad_hidden * gelu_slope(pre_act)).astype(BF16)
        gathered = gather_z(jnp.concatenate([hidden, grad_pre], axis=1))
        hidden_all, pre_all = gather_y(gathered[:, :chunk], gathered[:, chunk:])
        in_total = in_total + contract(pre_all, up_w, 1, 1)
        ups.append(contract(tok, pre_all, 0, 0).astype(BF16))
        downs.append(contract(hidden_all, grad, 0, 0).astype(BF16))
    in_total = lax.dynamic_slice_in_dim(
        jnp.concatenate([in_total, in_total]), n_tok - start, n_tok, axis=0
    )
    parts = lax.all_to_all(in_total.reshape(NC, n_tok // NC, width), COL, 0, 0)
    grad_in = parts.sum(axis=0).astype(BF16)
    return grad_in, jnp.concatenate(ups, axis=1), jnp.concatenate(downs, axis=0)


def solution(mesh):
    grid = Mesh(mesh.devices.reshape(NZ, NY, 4, 2), ("z", "y", "x", "core"))
    row = ("z", "y")
    return jax.shard_map(
        shards,
        mesh=grid,
        in_specs=(P(COL, row), P(COL, row), P(row, COL), P(COL, row)),
        out_specs=(P(COL, row), P(row, COL), P(COL, row)),
        check_vma=False,
    )
```

time: 466 us -> 162 us (0.35)
  waiting for transfers between devices: 400 us -> 57 us
  blocking collectives: 26.5 us -> 67.8 us
  starting transfers between devices: 0.16 us -> 15.6 us
  between operations: 13.8 us -> 0.79 us
    reduce_scatter x2 -> x0, waiting for transfers between devices: 257 us -> none  [the longest x1 226 us: shards(): lax.psum_scatter(jnp.concatenate([forward_part, backward_part], axis=1),...]
    all_gather x2 -> x0, waiting for transfers between devices: 143 us -> none  [the longest x1 76.3 us: shards(): pre_piece = lax.all_gather(grad_pre, 'row', axis=0, tiled=True)]
    ppermute x0 -> x8, waiting for transfers between devices: none -> 55.2 us  [shift_y(): return lax.ppermute(value, 'y', [(i, (i + by) % NY) for i in range(NY)])]
    all_to_all x0 -> x1, blocking collectives: none -> 28.2 us  [reduce_z(): parts = lax.all_to_all(both.reshape(NZ, rows, -1), 'z', 0, 0)]
    all_gather x2, blocking collectives: 26.5 us -> 39.6 us  [the longest x1 26.3 us: gather_z(): return lax.all_gather(value, 'z', axis=0, tiled=True)]
    ppermute x0 -> x8, starting transfers between devices: none -> 11.9 us  [shift_y(): return lax.ppermute(value, 'y', [(i, (i + by) % NY) for i in range(NY)])]
  transfers between devices with their start and end apart: 4 -> 9, of which waited for: 4 -> 6; matrix products, arithmetic and copies ran while one was open for 3% -> 8% of each run, Pallas kernels for 0% -> 0%
where the time goes in v1:
time: 162 us
  blocking collectives  67.8 us (42%)
  waiting for transfers between devices  57 us (35%)
  starting transfers between devices  15.6 us (10%)
  matrix products  11.8 us (7%)
  other arithmetic  4.66 us (3%)
  local copies, waits for them, and re-layouts  4.17 us (3%)
    ppermute x8, waiting for transfers between devices, shift_y(): return lax.ppermute(value, 'y', [(i, (i + by) % NY) for i in range(NY)])  55.2 us
    all_to_all x1, blocking collectives, reduce_z(): parts = lax.all_to_all(both.reshape(NZ, rows, -1), 'z', 0, 0)  28.2 us
    all_gather x1, blocking collectives, gather_z(): return lax.all_gather(value, 'z', axis=0, tiled=True)  26.3 us
    all_gather x1, blocking collectives, shards(): lax.all_gather(jnp.concatenate([tokens, grad_out], axis=1), COL, axis=0,...  13.3 us
    ppermute x8, starting transfers between devices, shift_y(): return lax.ppermute(value, 'y', [(i, (i + by) % NY) for i in range(NY)])  11.9 us
    dot_general x4, matrix products, contract(): lax.dot_general(left, right, (((left_dim,), (right_dim,)), ((), ())), pre...  10.8 us
    all_to_all x1, starting transfers between devices, shards(): parts = lax.all_to_all(in_total.reshape(NC, n_tok // NC, width), COL, 0, 0)  3.69 us
  transfers between devices with their start and end apart: 9, of which 6 were waited for; matrix products, arithmetic and copies ran while one was open for 8% of the time, Pallas kernels for 0%

profile of v1, /device:TPU:24, one launch (start us, length us, event | category | flops | bytes accessed | tf_op | source)
XLA Modules:
  0.0 161.8 jit_solution(1005406971846403413)
XLA Ops:
  0.7 0.9 pad_maximum_fusion.8
  1.6 13.3 %all_gather.6 = bf16[256,768]{1,0:T(8,128)(2,1)S(1)} all-gather(bf16[32,768]{1,0:T(8,128)(2,1)S(1)} %pad_maximum_fusion.8), channel_id=1, replica_groups=mesh['z'=8,'y'=4,'x'=4,'core'=2] {'x','core'}, dimensions={0}, use_global_device_ids=true | all-gather | bytes 442368 | tf_op jit(solution)/shard_map/all_gather | solution.py:70
  15.3 2.7 %convolution_convert_fusion.2 = bf16[256,3072]{1,0:T(8,128)(2,1)S(1)} fusion(bf16[3072,384]{1,0:T(8,128)(2,1)} %param.7, bf16[256,768]{1,0:T(8,128)(2,1)S(1)} %fusion.10), kind=kOutput, calls=%fused_computation.2 | convolution fusion | flops 604766208 | bytes 4128768 | tf_op jit(solution)/shard_map/dot_general | solution.py:13
  18.0 1.0 convolution_convert_fusion.3
  19.2 1.7 %collective-permute-start.1 = (bf16[128,3072]{1,0:T(8,128)(2,1)S(1)}, bf16[128,3072]{1,0:T(8,128)(2,1)S(1)}, u32[]{:S(2)}, u32[]{:S(2)}) collective-permute-start(bf16[128,3072]{1,0:T(8,128)(2,1)S(1)} %pad_maximum_fusion.2), channel_id=1, source_target_pairs={{0,8},{8,16},{16,24},{24,0},{1,9},{9,17},{17,25},{25,1},{2,10},{10... | collective-permute-start | bytes 2359304 | tf_op jit(solution)/shard_map/ppermute | solution.py:27
  21.4 17.6 %collective-permute-done.1 = bf16[128,3072]{1,0:T(8,128)(2,1)S(1)} collective-permute-done((bf16[128,3072]{1,0:T(8,128)(2,1)S(1)}, bf16[128,3072]{1,0:T(8,128)(2,1)S(1)}, u32[]{:S(2)}, u32[]{:S(2)}) %collective-permute-start.1) | collective-permute-done | bytes 786464 | tf_op jit(solution)/shard_map/ppermute | solution.py:27
  39.1 2.9 %collective-permute-start.2 = (bf16[64,3072]{1,0:T(8,128)(2,1)S(1)}, bf16[64,3072]{1,0:T(8,128)(2,1)S(1)}, u32[]{:S(2)}, u32[]{:S(2)}) collective-permute-start(bf16[64,3072]{1,0:T(8,128)(2,1)S(1)} %add_convert_fusion.3), channel_id=1, source_target_pairs={{0,8},{8,16},{16,24},{24,0},{1,9},{9,17},{17,25},{25,1},{2,10},{10... | collective-permute-start | bytes 1179656 | tf_op jit(solution)/shard_map/ppermute | solution.py:27
  42.0 8.1 %collective-permute-done.2 = bf16[64,3072]{1,0:T(8,128)(2,1)S(1)} collective-permute-done((bf16[64,3072]{1,0:T(8,128)(2,1)S(1)}, bf16[64,3072]{1,0:T(8,128)(2,1)S(1)}, u32[]{:S(2)}, u32[]{:S(2)}) %collective-permute-start.2) | collective-permute-done | bytes 393248 | tf_op jit(solution)/shard_map/ppermute | solution.py:27
  50.8 11.2 %collective-permute-done.3 = bf16[64,3072]{1,0:T(8,128)(2,1)S(1)} collective-permute-done((bf16[64,3072]{1,0:T(8,128)(2,1)S(1)}, bf16[64,3072]{1,0:T(8,128)(2,1)S(1)}, u32[]{:S(2)}, u32[]{:S(2)}) %collective-permute-start.3) | collective-permute-done | bytes 393248 | tf_op jit(solution)/shard_map/ppermute | solution.py:27
  62.2 28.2 %all_to_all.10 = bf16[8,8,6144]{2,1,0:T(8,128)(2,1)S(1)} all-to-all(bf16[8,8,6144]{2,1,0:T(8,128)(2,1)S(1)} %pad_maximum_fusion.3), channel_id=1, replica_groups=mesh['z'=8,'y'=4,'x'=4,'core'=2] {'z'}, dimensions={0} | all-to-all | bytes 1572864 | tf_op jit(solution)/shard_map/all_to_all | solution.py:46
  90.6 26.3 %all_gather.7 = bf16[64,6144]{1,0:T(8,128)(2,1)S(1)} all-gather(bf16[8,6144]{1,0:T(8,128)(2,1)S(1)} %pad_maximum_fusion.7), channel_id=1, replica_groups=mesh['z'=8,'y'=4,'x'=4,'core'=2] {'z'}, dimensions={0}, use_global_device_ids=true | all-gather | bytes 884736 | tf_op jit(solution)/shard_map/all_gather | solution.py:52
  117.0 1.0 pad_maximum_fusion.4
  118.0 3.2 %collective-permute-start.6 = (bf16[128,3072]{1,0:T(8,128)(2,1)}, bf16[128,3072]{1,0:T(8,128)(2,1)}, u32[]{:S(2)}, u32[]{:S(2)}) collective-permute-start(bf16[128,3072]{1,0:T(8,128)(2,1)} %pad_maximum_fusion.4), channel_id=1, source_target_pairs={{0,8},{8,16},{16,24},{24,0},{1,9},{9,17},{17,25},{25,1},{2,10},{10... | collective-permute-start | bytes 2359304 | tf_op jit(solution)/shard_map/ppermute | solution.py:27
  121.2 14.5 %collective-permute-done.4 = bf16[128,3072]{1,0:T(8,128)(2,1)} collective-permute-done((bf16[128,3072]{1,0:T(8,128)(2,1)}, bf16[128,3072]{1,0:T(8,128)(2,1)}, u32[]{:S(2)}, u32[]{:S(2)}) %collective-permute-start.4) | collective-permute-done | bytes 786464 | tf_op jit(solution)/shard_map/ppermute | solution.py:27
  135.7 1.9 %fusion.33 = (bf16[64,3072]{1,0:T(8,128)(2,1)}, bf16[64,3072]{1,0:T(8,128)(2,1)S(1)}) fusion(bf16[128,3072]{1,0:T(8,128)(2,1)} %collective-permute-done.4), kind=kLoop, calls=%fused_computation.56 | loop fusion | bytes 1572864 | tf_op jit(solution)/shard_map/slice | solution.py:63
  137.6 2.1 %fusion.34 = (bf16[64,3072]{1,0:T(8,128)(2,1)}, bf16[64,3072]{1,0:T(8,128)(2,1)S(1)}) fusion(bf16[128,3072]{1,0:T(8,128)(2,1)} %collective-permute-done.6), kind=kLoop, calls=%fused_computation.57 | loop fusion | bytes 1572864 | tf_op jit(solution)/shard_map/slice | solution.py:60
  139.7 3.1 %collective-permute-start.7 = (bf16[64,3072]{1,0:T(8,128)(2,1)}, bf16[64,3072]{1,0:T(8,128)(2,1)}, u32[]{:S(2)}, u32[]{:S(2)}) collective-permute-start(bf16[64,3072]{1,0:T(8,128)(2,1)} %get-tuple-element.9), channel_id=1, source_target_pairs={{0,8},{8,16},{16,24},{24,0},{1,9},{9,17},{17,25},{25,1},{2,10},{10... | collective-permute-start | bytes 1179656 | tf_op jit(solution)/shard_map/ppermute | solution.py:27
  142.8 3.8 %collective-permute-done.5 = bf16[64,3072]{1,0:T(8,128)(2,1)S(1)} collective-permute-done((bf16[64,3072]{1,0:T(8,128)(2,1)S(1)}, bf16[64,3072]{1,0:T(8,128)(2,1)S(1)}, u32[]{:S(2)}, u32[]{:S(2)}) %collective-permute-start.5) | collective-permute-done | bytes 393248 | tf_op jit(solution)/shard_map/ppermute | solution.py:27
  146.6 1.0 fusion.11
  147.7 0.9 fusion.9
  148.5 3.7 %all-to-all-start.1 = ((f32[8,32,384]{2,1,0:T(8,128)}), f32[8,32,384]{2,1,0:T(8,128)S(1)}, u32[]{:S(2)}, u32[]{:S(2)}) async-start(f32[8,32,384]{2,1,0:T(8,128)} %bitcast.2), calls=%async_computation.1 | async-start | bytes 786432 | tf_op jit(solution)/shard_map/all_to_all | solution.py:96
  152.2 3.6 %convolution_convert_fusion.1 = bf16[384,3072]{1,0:T(8,128)(2,1)} fusion(bf16[64,3072]{1,0:T(8,128)(2,1)} %copy-done.4, bf16[64,3072]{1,0:T(8,128)(2,1)} %copy-done.5, bf16[64,3072]{1,0:T(8,128)(2,1)} %copy-done.3, bf16[64,3072]{1,0:T(8,128)(2,1)} %copy-done.1, bf16[256,768]{1,0:T(8,128)(2,1)S(1)} %fusion.10), kind=kOutput, calls=%fused_computation.1 | convolution fusion | flops 611450880 | bytes 4128768 | tf_op jit(solution)/shard_map/dot_general | solution.py:13
  155.8 3.5 %convolution_convert_fusion = bf16[3072,384]{1,0:T(8,128)(2,1)} fusion(bf16[64,3072]{1,0:T(8,128)(2,1)} %get-tuple-element.9, bf16[64,3072]{1,0:T(8,128)(2,1)} %collective-permute-done.7, bf16[64,3072]{1,0:T(8,128)(2,1)S(1)} %copy-done.2, bf16[64,3072]{1,0:T(8,128)(2,1)S(1)} %get-tuple-element.11, bf16[256,768]{1,0:T(8,128)(2,1)S(1)} %fusion.10), kind=kOutput, calls=%fused_computation | convolution fusion | flops 611450880 | bytes 4128768 | tf_op jit(solution)/shard_map/dot_general | solution.py:13
  159.4 1.8 %all-to-all-done.1 = f32[8,32,384]{2,1,0:T(8,128)S(1)} async-done(((f32[8,32,384]{2,1,0:T(8,128)}), f32[8,32,384]{2,1,0:T(8,128)S(1)}, u32[]{:S(2)}, u32[]{:S(2)}) %all-to-all-start.1) | async-done | bytes 393248 | tf_op jit(solution)/shard_map/all_to_all | solution.py:96
  (32 shorter events, 3.1 us)
Async XLA Ops:
  0.6 17.4 %copy-start = (bf16[384,3072]{1,0:T(8,128)(2,1)S(1)}, bf16[384,3072]{1,0:T(8,128)(2,1)}, u32[]{:S(2)}) copy-start(bf16[384,3072]{1,0:T(8,128)(2,1)} %param.6) | copy-start | bytes 7077892
  19.2 19.9 %collective-permute-start.1 = (bf16[128,3072]{1,0:T(8,128)(2,1)S(1)}, bf16[128,3072]{1,0:T(8,128)(2,1)S(1)}, u32[]{:S(2)}, u32[]{:S(2)}) collective-permute-start(bf16[128,3072]{1,0:T(8,128)(2,1)S(1)} %pad_maximum_fusion.2), channel_id=1, source_target_pairs={{0,8},{8,16},{16,24},{24,0},{1,9},{9,17},{17,25},{25,1},{2,10},{10... | collective-permute-start | bytes 2359304 | tf_op jit(solution)/shard_map/ppermute | solution.py:27
  20.9 21.1 %collective-permute-start = (bf16[128,3072]{1,0:T(8,128)(2,1)S(1)}, bf16[128,3072]{1,0:T(8,128)(2,1)S(1)}, u32[]{:S(2)}, u32[]{:S(2)}) collective-permute-start(bf16[128,3072]{1,0:T(8,128)(2,1)S(1)} %pad_maximum_fusion.1), channel_id=1, source_target_pairs={{0,24},{8,0},{16,8},{24,16},{1,25},{9,1},{17,9},{25,17},{2,26},{10... | collective-permute-start | bytes 2359304 | tf_op jit(solution)/shard_map/ppermute | solution.py:27
  39.1 11.0 %collective-permute-start.2 = (bf16[64,3072]{1,0:T(8,128)(2,1)S(1)}, bf16[64,3072]{1,0:T(8,128)(2,1)S(1)}, u32[]{:S(2)}, u32[]{:S(2)}) collective-permute-start(bf16[64,3072]{1,0:T(8,128)(2,1)S(1)} %add_convert_fusion.3), channel_id=1, source_target_pairs={{0,8},{8,16},{16,24},{24,0},{1,9},{9,17},{17,25},{25,1},{2,10},{10... | collective-permute-start | bytes 1179656 | tf_op jit(solution)/shard_map/ppermute | solution.py:27
  50.4 11.7 %collective-permute-start.3 = (bf16[64,3072]{1,0:T(8,128)(2,1)S(1)}, bf16[64,3072]{1,0:T(8,128)(2,1)S(1)}, u32[]{:S(2)}, u32[]{:S(2)}) collective-permute-start(bf16[64,3072]{1,0:T(8,128)(2,1)S(1)} %get-tuple-element.14), channel_id=1, source_target_pairs={{0,24},{8,0},{16,8},{24,16},{1,25},{9,1},{17,9},{25,17},{2,26},{10... | collective-permute-start | bytes 1179656 | tf_op jit(solution)/shard_map/ppermute | solution.py:27
  117.0 29.7 %copy-start.1 = (bf16[64,3072]{1,0:T(8,128)(2,1)}, bf16[64,3072]{1,0:T(8,128)(2,1)S(1)}, u32[]{:S(2)}) copy-start(bf16[64,3072]{1,0:T(8,128)(2,1)S(1)} %get-tuple-element.12) | copy-start | bytes 1179652
  118.0 17.7 %collective-permute-start.4 = (bf16[128,3072]{1,0:T(8,128)(2,1)}, bf16[128,3072]{1,0:T(8,128)(2,1)}, u32[]{:S(2)}, u32[]{:S(2)}) collective-permute-start(bf16[128,3072]{1,0:T(8,128)(2,1)} %pad_maximum_fusion.4), channel_id=1, source_target_pairs={{0,24},{8,0},{16,8},{24,16},{1,25},{9,1},{17,9},{25,17},{2,26},{10... | collective-permute-start | bytes 2359304 | tf_op jit(solution)/shard_map/ppermute | solution.py:27
  118.0 19.7 %collective-permute-start.6 = (bf16[128,3072]{1,0:T(8,128)(2,1)}, bf16[128,3072]{1,0:T(8,128)(2,1)}, u32[]{:S(2)}, u32[]{:S(2)}) collective-permute-start(bf16[128,3072]{1,0:T(8,128)(2,1)} %pad_maximum_fusion.4), channel_id=1, source_target_pairs={{0,8},{8,16},{16,24},{24,0},{1,9},{9,17},{17,25},{25,1},{2,10},{10... | collective-permute-start | bytes 2359304 | tf_op jit(solution)/shard_map/ppermute | solution.py:27
  137.6 10.0 %copy-start.3 = (bf16[64,3072]{1,0:T(8,128)(2,1)}, bf16[64,3072]{1,0:T(8,128)(2,1)S(1)}, u32[]{:S(2)}) copy-start(bf16[64,3072]{1,0:T(8,128)(2,1)S(1)} %get-tuple-element.8) | copy-start | bytes 1179652
  137.6 9.0 %collective-permute-start.5 = (bf16[64,3072]{1,0:T(8,128)(2,1)S(1)}, bf16[64,3072]{1,0:T(8,128)(2,1)S(1)}, u32[]{:S(2)}, u32[]{:S(2)}) collective-permute-start(bf16[64,3072]{1,0:T(8,128)(2,1)S(1)} %get-tuple-element.8), channel_id=1, source_target_pairs={{0,24},{8,0},{16,8},{24,16},{1,25},{9,1},{17,9},{25,17},{2,26},{10... | collective-permute-start | bytes 1179656 | tf_op jit(solution)/shard_map/ppermute | solution.py:27
  139.7 7.9 %copy-start.4 = (bf16[64,3072]{1,0:T(8,128)(2,1)}, bf16[64,3072]{1,0:T(8,128)(2,1)S(1)}, u32[]{:S(2)}) copy-start(bf16[64,3072]{1,0:T(8,128)(2,1)S(1)} %get-tuple-element.10) | copy-start | bytes 1179652
  139.7 16.1 %collective-permute-start.7 = (bf16[64,3072]{1,0:T(8,128)(2,1)}, bf16[64,3072]{1,0:T(8,128)(2,1)}, u32[]{:S(2)}, u32[]{:S(2)}) collective-permute-start(bf16[64,3072]{1,0:T(8,128)(2,1)} %get-tuple-element.9), channel_id=1, source_target_pairs={{0,8},{8,16},{16,24},{24,0},{1,9},{9,17},{17,25},{25,1},{2,10},{10... | collective-permute-start | bytes 1179656 | tf_op jit(solution)/shard_map/ppermute | solution.py:27
  146.6 1.0 copy-start.5
  148.5 12.6 %all-to-all-start.1 = ((f32[8,32,384]{2,1,0:T(8,128)}), f32[8,32,384]{2,1,0:T(8,128)S(1)}, u32[]{:S(2)}, u32[]{:S(2)}) async-start(f32[8,32,384]{2,1,0:T(8,128)} %bitcast.2), calls=%async_computation.1 | async-start | bytes 786432 | tf_op jit(solution)/shard_map/all_to_all | solution.py:96
  152.2 3.6 %copy-start.2 = (bf16[64,3072]{1,0:T(8,128)(2,1)S(1)}, bf16[64,3072]{1,0:T(8,128)(2,1)}, u32[]{:S(2)}) copy-start(bf16[64,3072]{1,0:T(8,128)(2,1)} %get-tuple-element.7) | copy-start | bytes 1179652

commit v2 on v0

v2 whole, which is shorter than its diff:
```python
import jax
import jax.numpy as jnp
from jax import lax
from jax.sharding import Mesh, PartitionSpec as P

F32, BF16 = jnp.float32, jnp.bfloat16
COL, ROW = ("x", "core"), ("z", "y")
NZ, NY, NX, NCORE = 8, 4, 4, 2
SIZES = {"z": NZ, "y": NY, "x": NX, "core": NCORE}


def contract(left, right, left_dim, right_dim):
    return lax.dot_general(
        left, right, (((left_dim,), (right_dim,)), ((), ())), preferred_element_type=F32
    )


def gelu_tanh(values):
    return jax.nn.gelu(values, approximate=True)


def gelu_slope(values):
    return jax.jvp(gelu_tanh, (values,), (jnp.ones_like(values),))[1]


def shift(value, axis, by):
    n = SIZES[axis]
    return lax.ppermute(value, axis, [(i, (i + by) % n) for i in range(n)])


def shift_apart(value, axis, by):
    n = SIZES[axis]
    pairs = [
        (i * NCORE + core, (i + by * (1 - 2 * core)) % n * NCORE + core)
        for i in range(n)
        for core in range(NCORE)
    ]
    return lax.ppermute(value, (axis, "core"), pairs)


def swap_cores(value):
    return lax.ppermute(value, "core", [(0, 1), (1, 0)])


def tie(values):
    return lax.optimization_barrier(values)


def roll(value, axis, start):
    n = value.shape[axis]
    return lax.dynamic_slice_in_dim(
        jnp.concatenate([value, value], axis=axis), lax.rem(start + n, n), n, axis=axis
    )


def split_rows(value, n):
    rows = value.shape[0] // n
    return [value[i * rows : (i + 1) * rows] for i in range(n)]


def shards(tokens, grad_out, up_weight, down_weight):
    width = tokens.shape[1]
    z, y, x, core = (lax.axis_index(name) for name in ("z", "y", "x", "core"))
    way = 1 - 2 * core
    n_pair = NZ // 2
    half = n_pair // 2
    unit = tokens.shape[0] // half
    both = jnp.concatenate([tokens, grad_out], axis=1).reshape(half, unit, 2 * width)
    chip = jnp.concatenate([both, swap_cores(both)])
    next_x, far_x, last_x = (shift_apart(chip, "x", -1), shift(chip, "x", 2), shift_apart(chip, "x", 1))
    both = jnp.stack([chip, next_x, far_x, last_x])
    both = roll(roll(both, 0, way * (y - x)), 1, z // 2 - half * core)

    order = (2, 1, 3, 0)
    rows = jnp.concatenate([both[:, j] for j in order], axis=1).reshape(-1, 2 * width)
    pre = split_rows(jnp.dot(rows[:, :width], up_weight, preferred_element_type=F32), NY)
    back = split_rows(contract(rows[:, width:], down_weight, 1, 1), NY)

    def parts_of(first, last):
        at = slice(first * unit, last * unit)
        parts = [jnp.concatenate([p[at], b[at]]) for p, b in zip(pre, back, strict=True)]
        return [parts[0], parts[1], parts[2].astype(BF16), parts[3].astype(BF16)]

    def first_hops(parts):
        return shift_apart(parts[2], "y", 1), shift_apart(parts[3], "y", -1)

    def second_message(parts, relay):
        return (parts[1] + relay.astype(F32)).astype(BF16)

    def finish(parts, message, last):
        return parts[0] + shift_apart(message, "y", 1).astype(F32) + last.astype(F32)

    far, mid, own = parts_of(0, 1), parts_of(1, 3), parts_of(3, 4)
    relay, last_far = first_hops(far)
    message, mid[2], mid[3] = tie((second_message(far, relay), mid[2], mid[3]))
    sum_far = finish(far, message, last_far)
    relay, last_mid = first_hops(mid)
    sum_mid = finish(mid, second_message(mid, relay), last_mid)
    sum_mid, own[2], own[3] = tie((sum_mid.astype(BF16), own[2], own[3]))
    relay, last_own = first_hops(own)
    total = finish(own, second_message(own, relay), last_own)

    total = total + shift(sum_far.astype(BF16), "z", 4).astype(F32)
    pre_1, pre_3, back_1, back_3 = split_rows(sum_mid, 4)
    total = total + shift(jnp.concatenate([pre_1, back_1]), "z", 2).astype(F32)
    total = total + shift(jnp.concatenate([pre_3, back_3]), "z", -2).astype(F32)
    total = total + lax.ppermute(total.astype(BF16), "z", [(i, i ^ 1) for i in range(NZ)]).astype(F32)
    pre_act, grad_hidden = total[:unit], total[unit:]
    hidden = gelu_tanh(pre_act).astype(BF16)
    grad_pre = (grad_hidden * gelu_slope(pre_act)).astype(BF16)

    mine = jnp.concatenate([hidden, grad_pre])
    have_1, have_3 = shift(mine, "z", -2), shift(mine, "z", 2)
    have_2 = shift(mine, "z", 4)

    def neighbours(message):
        return shift_apart(message, "y", -1), shift_apart(message, "y", 1)

    next_own, last_own = neighbours(mine)
    have_1, have_3, next_own, last_own = tie((have_1, have_3, next_own, last_own))
    relay_own = shift_apart(next_own, "y", -1)
    have_mid, have_far = jnp.concatenate([have_1, have_3]), have_2
    next_mid, last_mid = neighbours(have_mid)
    next_far, last_far = neighbours(have_far)
    relay = shift_apart(jnp.concatenate([next_mid, next_far]), "y", -1)

    groups = (
        ((0,), (3, 0, 1, 2), (last_own, mine, next_own, relay_own)),
        ((1, 3), (3, 0, 1), (last_mid, have_mid, next_mid)),
        ((2,), (3, 0, 1), (last_far, have_far, next_far)),
        ((1, 3, 2), (2,), (relay,)),
    )
    in_blocks, up_sum, down_sum = {}, 0.0, 0.0
    for js, es, messages in groups:
        parts = [split_rows(message, 2 * len(js)) for message in messages]
        hidden = jnp.concatenate([row for p in parts for row in p[0::2]])
        grad_pre = jnp.concatenate([row for p in parts for row in p[1::2]])
        rows = jnp.concatenate([both[e, j] for e in es for j in js])
        in_part = contract(grad_pre, up_weight, 1, 1).reshape(len(es), len(js), unit, width)
        for i, j in enumerate(js):
            in_blocks.setdefault(j, []).append(in_part[:, i])
        up_sum = up_sum + contract(rows[:, :width], grad_pre, 0, 0)
        down_sum = down_sum + contract(hidden, rows[:, width:], 0, 0)

    in_total = jnp.stack([jnp.concatenate(in_blocks[j]) for j in range(n_pair)], axis=1)
    in_total = roll(roll(in_total, 0, way * (x - y) + 1), 1, half * core - z // 2)
    other = swap_cores(in_total[:, half:])
    in_chip = [in_total[e, :half] + other[-e % NX] for e in range(NX)]
    in_mine = in_chip[0] + shift(in_chip[2], "x", 2)
    in_mine = in_mine + shift_apart(in_chip[1], "x", 1) + shift_apart(in_chip[3], "x", -1)
    grad_in = in_mine.reshape(half * unit, width).astype(BF16)
    return grad_in, up_sum.astype(BF16), down_sum.astype(BF16)


def solution(mesh):
    grid = Mesh(mesh.devices.reshape(NZ, NY, NX, NCORE), ("z", "y", "x", "core"))
    return jax.shard_map(
        shards,
        mesh=grid,
        in_specs=(P(COL, ROW), P(COL, ROW), P(ROW, COL), P(COL, ROW)),
        out_specs=(P(COL, ROW), P(ROW, COL), P(COL, ROW)),
        check_vma=False,
    )
```

time: 466 us -> 134 us (0.29)
  waiting for transfers between devices: 400 us -> 47.6 us
  starting transfers between devices: 0.16 us -> 63.9 us
  blocking collectives: 26.5 us -> 0 us
  between operations: 13.8 us -> 1.3 us
    reduce_scatter x2 -> x0, waiting for transfers between devices: 257 us -> none  [the longest x1 226 us: shards(): lax.psum_scatter(jnp.concatenate([forward_part, backward_part], axis=1),...]
    all_gather x2 -> x0, waiting for transfers between devices: 143 us -> none  [the longest x1 76.3 us: shards(): pre_piece = lax.all_gather(grad_pre, 'row', axis=0, tiled=True)]
    ppermute x0 -> x32, starting transfers between devices: none -> 63.9 us  [the longest x21 43.2 us: shift_apart(): return lax.ppermute(value, (axis, 'core'), pairs)]
    ppermute x0 -> x32, waiting for transfers between devices: none -> 47.6 us  [the longest x21 32.2 us: shift_apart(): return lax.ppermute(value, (axis, 'core'), pairs)]
    all_gather x2 -> x0, blocking collectives: 26.5 us -> none  [the longest x1 13.5 us: shards(): lax.all_gather(tokens, 'col', axis=0, tiled=True)]
    dot_general x4 -> x13, matrix products: 13.5 us -> 13.6 us  [contract(): lax.dot_general(left, right, (((left_dim,), (right_dim,)), ((), ())), pre...]
  transfers between devices with their start and end apart: 4 -> 32, of which waited for: 4 -> 16; matrix products, arithmetic and copies ran while one was open for 3% -> 10% of each run, Pallas kernels for 0% -> 0%
where the time goes in v2:
time: 134 us; the launch traced here: 132 us
  starting transfers between devices  63.9 us (48%)
  waiting for transfers between devices  47.6 us (36%)
  matrix products  14.6 us (11%)
  other arithmetic  2.91 us (2%)
  local copies, waits for them, and re-layouts  1.47 us (1%)
    ppermute x21, starting transfers between devices, shift_apart(): return lax.ppermute(value, (axis, 'core'), pairs)  43.2 us
    ppermute x21, waiting for transfers between devices, shift_apart(): return lax.ppermute(value, (axis, 'core'), pairs)  32.2 us
    ppermute x8, starting transfers between devices, shift(): return lax.ppermute(value, axis, [(i, (i + by) % n) for i in range(n)])  19.4 us
    dot_general x13, matrix products, contract(): lax.dot_general(left, right, (((left_dim,), (right_dim,)), ((), ())), pre...  13.6 us
    ppermute x8, waiting for transfers between devices, shift(): return lax.ppermute(value, axis, [(i, (i + by) % n) for i in range(n)])  7.41 us
    ppermute x1, waiting for transfers between devices, shards(): lax.ppermute(total.astype(BF16), 'z', [(i, i ^ 1) for i in range(NZ)])  6.91 us
  transfers between devices with their start and end apart: 32, of which 16 were waited for; matrix products, arithmetic and copies ran while one was open for 10% of the time, Pallas kernels for 0%

profile of v2, /device:TPU:24, one launch (start us, length us, event | category | flops | bytes accessed | tf_op | source)
XLA Modules:
  0.0 131.8 jit_solution(894585116209950865)
XLA Ops:
  2.8 2.8 %collective-permute-start.1 = (bf16[4,16,768]{2,1,0:T(8,128)(2,1)S(1)}, bf16[4,16,768]{2,1,0:T(8,128)(2,1)S(1)}, u32[]{:S(2)}, u32[]{:S(2)}) collective-permute-start(bf16[4,16,768]{2,1,0:T(8,128)(2,1)S(1)} %pad_maximum_fusion.18), channel_id=1, source_target_pairs={{0,6},{1,3},{2,0},{3,5},{4,2},{5,7},{6,4},{7,1},{8,14},{9,11},{10,... | collective-permute-start | bytes 294920 | tf_op jit(solution)/shard_map/ppermute | solution.py:38
  7.3 2.8 %collective-permute-done.1 = bf16[4,16,768]{2,1,0:T(8,128)(2,1)S(1)} collective-permute-done((bf16[4,16,768]{2,1,0:T(8,128)(2,1)S(1)}, bf16[4,16,768]{2,1,0:T(8,128)(2,1)S(1)}, u32[]{:S(2)}, u32[]{:S(2)}) %collective-permute-start.1) | collective-permute-done | bytes 98336 | tf_op jit(solution)/shard_map/ppermute | solution.py:38
  18.6 3.4 %collective-permute-done.4 = bf16[32,3072]{1,0:T(8,128)(2,1)S(1)} collective-permute-done((bf16[32,3072]{1,0:T(8,128)(2,1)S(1)}, bf16[32,3072]{1,0:T(8,128)(2,1)S(1)}, u32[]{:S(2)}, u32[]{:S(2)}) %collective-permute-start.4) | collective-permute-done | bytes 196640 | tf_op jit(solution)/shard_map/ppermute | solution.py:38
  22.1 3.5 %collective-permute-start.5 = (bf16[64,3072]{1,0:T(8,128)(2,1)S(1)}, bf16[64,3072]{1,0:T(8,128)(2,1)S(1)}, u32[]{:S(2)}, u32[]{:S(2)}) collective-permute-start(bf16[64,3072]{1,0:T(8,128)(2,1)S(1)} %get-tuple-element.13), channel_id=1, source_target_pairs={{0,8},{1,25},{8,16},{9,1},{16,24},{17,9},{24,0},{25,17},{2,10},{3,... | collective-permute-start | bytes 1179656 | tf_op jit(solution)/shard_map/ppermute | solution.py:38
  25.7 3.2 %collective-permute-start.11 = (bf16[32,3072]{1,0:T(8,128)(2,1)S(1)}, bf16[32,3072]{1,0:T(8,128)(2,1)S(1)}, u32[]{:S(2)}, u32[]{:S(2)}) collective-permute-start(bf16[32,3072]{1,0:T(8,128)(2,1)S(1)} %fusion.17), channel_id=1, source_target_pairs={{0,8},{1,25},{8,16},{9,1},{16,24},{17,9},{24,0},{25,17},{2,10},{3,... | collective-permute-start | bytes 589832 | tf_op jit(solution)/shard_map/ppermute | solution.py:38
  29.0 3.2 %collective-permute-done.5 = bf16[64,3072]{1,0:T(8,128)(2,1)S(1)} collective-permute-done((bf16[64,3072]{1,0:T(8,128)(2,1)S(1)}, bf16[64,3072]{1,0:T(8,128)(2,1)S(1)}, u32[]{:S(2)}, u32[]{:S(2)}) %collective-permute-start.5) | collective-permute-done | bytes 393248 | tf_op jit(solution)/shard_map/ppermute | solution.py:38
  32.2 3.8 %collective-permute-start.6 = (bf16[64,3072]{1,0:T(8,128)(2,1)S(1)}, bf16[64,3072]{1,0:T(8,128)(2,1)S(1)}, u32[]{:S(2)}, u32[]{:S(2)}) collective-permute-start(bf16[64,3072]{1,0:T(8,128)(2,1)S(1)} %fusion.2), channel_id=1, source_target_pairs={{0,8},{1,25},{8,16},{9,1},{16,24},{17,9},{24,0},{25,17},{2,10},{3,... | collective-permute-start | bytes 1179656 | tf_op jit(solution)/shard_map/ppermute | solution.py:38
  36.1 7.3 %collective-permute-start.13 = (bf16[32,3072]{1,0:T(8,128)(2,1)S(1)}, bf16[32,3072]{1,0:T(8,128)(2,1)S(1)}, u32[]{:S(2)}, u32[]{:S(2)}) collective-permute-start(bf16[32,3072]{1,0:T(8,128)(2,1)S(1)} %fusion.19), channel_id=1, source_target_pairs={{0,128},{32,160},{64,192},{96,224},{128,0},{160,32},{192,64},{224,... | collective-permute-start | bytes 589832 | tf_op jit(solution)/shard_map/ppermute | solution.py:28
  43.5 4.3 %collective-permute-start.15 = (bf16[32,3072]{1,0:T(8,128)(2,1)S(1)}, bf16[32,3072]{1,0:T(8,128)(2,1)S(1)}, u32[]{:S(2)}, u32[]{:S(2)}) collective-permute-start(bf16[32,3072]{1,0:T(8,128)(2,1)S(1)} %pad_maximum_fusion.12), channel_id=1, source_target_pairs={{0,192},{32,224},{64,0},{96,32},{128,64},{160,96},{192,128},{224,1... | collective-permute-start | bytes 589832 | tf_op jit(solution)/shard_map/ppermute | solution.py:28
  47.8 3.7 %collective-permute-start.8 = (bf16[32,3072]{1,0:T(8,128)(2,1)S(1)}, bf16[32,3072]{1,0:T(8,128)(2,1)S(1)}, u32[]{:S(2)}, u32[]{:S(2)}) collective-permute-start(bf16[32,3072]{1,0:T(8,128)(2,1)S(1)} %get-tuple-element.15), channel_id=1, source_target_pairs={{0,8},{1,25},{8,16},{9,1},{16,24},{17,9},{24,0},{25,17},{2,10},{3,... | collective-permute-start | bytes 589832 | tf_op jit(solution)/shard_map/ppermute | solution.py:38
  51.7 3.0 %collective-permute-done.8 = bf16[32,3072]{1,0:T(8,128)(2,1)S(1)} collective-permute-done((bf16[32,3072]{1,0:T(8,128)(2,1)S(1)}, bf16[32,3072]{1,0:T(8,128)(2,1)S(1)}, u32[]{:S(2)}, u32[]{:S(2)}) %collective-permute-start.8) | collective-permute-done | bytes 196640 | tf_op jit(solution)/shard_map/ppermute | solution.py:38
  54.8 3.8 %collective-permute-start.9 = (bf16[32,3072]{1,0:T(8,128)(2,1)S(1)}, bf16[32,3072]{1,0:T(8,128)(2,1)S(1)}, u32[]{:S(2)}, u32[]{:S(2)}) collective-permute-start(bf16[32,3072]{1,0:T(8,128)(2,1)S(1)} %fusion.16), channel_id=1, source_target_pairs={{0,8},{1,25},{8,16},{9,1},{16,24},{17,9},{24,0},{25,17},{2,10},{3,... | collective-permute-start | bytes 589832 | tf_op jit(solution)/shard_map/ppermute | solution.py:38
  58.6 2.3 %collective-permute-done.14 = bf16[32,3072]{1,0:T(8,128)(2,1)S(1)} collective-permute-done((bf16[32,3072]{1,0:T(8,128)(2,1)S(1)}, bf16[32,3072]{1,0:T(8,128)(2,1)S(1)}, u32[]{:S(2)}, u32[]{:S(2)}) %collective-permute-start.14) | collective-permute-done | bytes 196640 | tf_op jit(solution)/shard_map/ppermute | solution.py:28
  63.0 6.9 %collective-permute-done.16 = bf16[32,3072]{1,0:T(8,128)(2,1)S(1)} collective-permute-done((bf16[32,3072]{1,0:T(8,128)(2,1)S(1)}, bf16[32,3072]{1,0:T(8,128)(2,1)S(1)}, u32[]{:S(2)}, u32[]{:S(2)}) %collective-permute-start.16) | collective-permute-done | bytes 196640 | tf_op jit(solution)/shard_map/ppermute | solution.py:107
  70.7 2.4 %collective-permute-start.18 = (bf16[32,3072]{1,0:T(8,128)(2,1)S(1)}, bf16[32,3072]{1,0:T(8,128)(2,1)S(1)}, u32[]{:S(2)}, u32[]{:S(2)}) collective-permute-start(bf16[32,3072]{1,0:T(8,128)(2,1)S(1)} %pad_maximum_fusion.13), channel_id=1, source_target_pairs={{0,64},{32,96},{64,128},{96,160},{128,192},{160,224},{192,0},{224,... | collective-permute-start | bytes 589832 | tf_op jit(solution)/shard_map/ppermute | solution.py:28
  73.1 4.0 %collective-permute-start.20 = (bf16[32,3072]{1,0:T(8,128)(2,1)S(1)}, bf16[32,3072]{1,0:T(8,128)(2,1)S(1)}, u32[]{:S(2)}, u32[]{:S(2)}) collective-permute-start(bf16[32,3072]{1,0:T(8,128)(2,1)S(1)} %pad_maximum_fusion.13), channel_id=1, source_target_pairs={{0,8},{1,25},{8,16},{9,1},{16,24},{17,9},{24,0},{25,17},{2,10},{3,... | collective-permute-start | bytes 589832 | tf_op jit(solution)/shard_map/ppermute | solution.py:38
  77.2 2.4 %collective-permute-start.24 = (bf16[32,3072]{1,0:T(8,128)(2,1)S(1)}, bf16[32,3072]{1,0:T(8,128)(2,1)S(1)}, u32[]{:S(2)}, u32[]{:S(2)}) collective-permute-start(bf16[32,3072]{1,0:T(8,128)(2,1)S(1)} %pad_maximum_fusion.13), channel_id=1, source_target_pairs={{0,128},{32,160},{64,192},{96,224},{128,0},{160,32},{192,64},{224,... | collective-permute-start | bytes 589832 | tf_op jit(solution)/shard_map/ppermute | solution.py:28
  79.6 2.8 %collective-permute-done.17 = bf16[32,3072]{1,0:T(8,128)(2,1)S(1)} collective-permute-done((bf16[32,3072]{1,0:T(8,128)(2,1)S(1)}, bf16[32,3072]{1,0:T(8,128)(2,1)S(1)}, u32[]{:S(2)}, u32[]{:S(2)}) %collective-permute-start.17) | collective-permute-done | bytes 196640 | tf_op jit(solution)/shard_map/ppermute | solution.py:28
  83.4 2.4 %collective-permute-start.23 = (bf16[64,3072]{1,0:T(8,128)(2,1)S(1)}, bf16[64,3072]{1,0:T(8,128)(2,1)S(1)}, u32[]{:S(2)}, u32[]{:S(2)}) collective-permute-start(bf16[64,3072]{1,0:T(8,128)(2,1)S(1)} %constant_dynamic-update-slice_fusion), channel_id=1, source_target_pairs={{0,24},{1,9},{8,0},{9,17},{16,8},{17,25},{24,16},{25,1},{2,26},{3,... | collective-permute-start | bytes 1179656 | tf_op jit(solution)/shard_map/ppermute | solution.py:38
  87.9 2.9 %collective-permute-start.27 = (bf16[32,3072]{1,0:T(8,128)(2,1)S(1)}, bf16[32,3072]{1,0:T(8,128)(2,1)S(1)}, u32[]{:S(2)}, u32[]{:S(2)}) collective-permute-start(bf16[32,3072]{1,0:T(8,128)(2,1)S(1)} %collective-permute-done.24), channel_id=1, source_target_pairs={{0,8},{1,25},{8,16},{9,1},{16,24},{17,9},{24,0},{25,17},{2,10},{3,... | collective-permute-start | bytes 589832 | tf_op jit(solution)/shard_map/ppermute | solution.py:38
  92.4 6.7 %collective-permute-done.25 = bf16[32,3072]{1,0:T(8,128)(2,1)S(1)} collective-permute-done((bf16[32,3072]{1,0:T(8,128)(2,1)S(1)}, bf16[32,3072]{1,0:T(8,128)(2,1)S(1)}, u32[]{:S(2)}, u32[]{:S(2)}) %collective-permute-start.25) | collective-permute-done | bytes 196640 | tf_op jit(solution)/shard_map/ppermute | solution.py:38
  104.3 8.5 %collective-permute-done.26 = bf16[96,3072]{1,0:T(8,128)(2,1)S(1)} collective-permute-done((bf16[96,3072]{1,0:T(8,128)(2,1)S(1)}, bf16[96,3072]{1,0:T(8,128)(2,1)S(1)}, u32[]{:S(2)}, u32[]{:S(2)}) %collective-permute-start.26) | collective-permute-done | bytes 589856 | tf_op jit(solution)/shard_map/ppermute | solution.py:38
  117.9 7.3 %collective-permute-start.31 = (f32[2,16,384]{2,1,0:T(8,128)S(1)}, f32[2,16,384]{2,1,0:T(8,128)S(1)}, u32[]{:S(2)}, u32[]{:S(2)}) collective-permute-start(f32[2,16,384]{2,1,0:T(8,128)S(1)} %fusion.67), channel_id=1, source_target_pairs={{0,6},{1,3},{2,0},{3,5},{4,2},{5,7},{6,4},{7,1},{8,14},{9,11},{10,... | collective-permute-start | bytes 147464 | tf_op jit(solution)/shard_map/ppermute | solution.py:38
  126.8 2.3 %add_convert_fusion = bf16[3072,384]{1,0:T(8,128)(2,1)} fusion(f32[3072,384]{1,0:T(8,128)S(1)} %fusion.33, f32[3072,384]{1,0:T(8,128)S(1)} %fusion.20, f32[3072,384]{1,0:T(8,128)S(1)} %fusion.58, bf16[16,3072]{1,0:T(8,128)(2,1)S(1)} %get-tuple-element.89, bf16[16,3072]{1,0:T(8,128)(2,1)S(1)} %get-tuple-element.87, bf16[16,3072]{1,0:T(8,128)(2,1)S(1)} %get-tuple-element.85, ...), kind=kOutput, calls=%fused_computation | convolution fusion | flops 118849536 | bytes 16846848 | tf_op jit(solution)/shard_map/dot_general | solution.py:13
  (132 shorter events, 34.8 us)
Async XLA Ops:
  2.8 7.3 %collective-permute-start.1 = (bf16[4,16,768]{2,1,0:T(8,128)(2,1)S(1)}, bf16[4,16,768]{2,1,0:T(8,128)(2,1)S(1)}, u32[]{:S(2)}, u32[]{:S(2)}) collective-permute-start(bf16[4,16,768]{2,1,0:T(8,128)(2,1)S(1)} %pad_maximum_fusion.18), channel_id=1, source_target_pairs={{0,6},{1,3},{2,0},{3,5},{4,2},{5,7},{6,4},{7,1},{8,14},{9,11},{10,... | collective-permute-start | bytes 294920 | tf_op jit(solution)/shard_map/ppermute | solution.py:38
  16.6 19.3 %collective-permute-start.12 = (bf16[32,3072]{1,0:T(8,128)(2,1)S(1)}, bf16[32,3072]{1,0:T(8,128)(2,1)S(1)}, u32[]{:S(2)}, u32[]{:S(2)}) collective-permute-start(bf16[32,3072]{1,0:T(8,128)(2,1)S(1)} %pad_maximum_fusion.10), channel_id=1, source_target_pairs={{0,24},{1,9},{8,0},{9,17},{16,8},{17,25},{24,16},{25,1},{2,26},{3,... | collective-permute-start | bytes 589832 | tf_op jit(solution)/shard_map/ppermute | solution.py:38
  22.1 10.0 %collective-permute-start.5 = (bf16[64,3072]{1,0:T(8,128)(2,1)S(1)}, bf16[64,3072]{1,0:T(8,128)(2,1)S(1)}, u32[]{:S(2)}, u32[]{:S(2)}) collective-permute-start(bf16[64,3072]{1,0:T(8,128)(2,1)S(1)} %get-tuple-element.13), channel_id=1, source_target_pairs={{0,8},{1,25},{8,16},{9,1},{16,24},{17,9},{24,0},{25,17},{2,10},{3,... | collective-permute-start | bytes 1179656 | tf_op jit(solution)/shard_map/ppermute | solution.py:38
  25.6 17.7 %collective-permute-start.7 = (bf16[64,3072]{1,0:T(8,128)(2,1)S(1)}, bf16[64,3072]{1,0:T(8,128)(2,1)S(1)}, u32[]{:S(2)}, u32[]{:S(2)}) collective-permute-start(bf16[64,3072]{1,0:T(8,128)(2,1)S(1)} %get-tuple-element.14), channel_id=1, source_target_pairs={{0,24},{1,9},{8,0},{9,17},{16,8},{17,25},{24,16},{25,1},{2,26},{3,... | collective-permute-start | bytes 1179656 | tf_op jit(solution)/shard_map/ppermute | solution.py:38
  25.7 10.3 %collective-permute-start.11 = (bf16[32,3072]{1,0:T(8,128)(2,1)S(1)}, bf16[32,3072]{1,0:T(8,128)(2,1)S(1)}, u32[]{:S(2)}, u32[]{:S(2)}) collective-permute-start(bf16[32,3072]{1,0:T(8,128)(2,1)S(1)} %fusion.17), channel_id=1, source_target_pairs={{0,8},{1,25},{8,16},{9,1},{16,24},{17,9},{24,0},{25,17},{2,10},{3,... | collective-permute-start | bytes 589832 | tf_op jit(solution)/shard_map/ppermute | solution.py:38
  32.2 11.1 %collective-permute-start.6 = (bf16[64,3072]{1,0:T(8,128)(2,1)S(1)}, bf16[64,3072]{1,0:T(8,128)(2,1)S(1)}, u32[]{:S(2)}, u32[]{:S(2)}) collective-permute-start(bf16[64,3072]{1,0:T(8,128)(2,1)S(1)} %fusion.2), channel_id=1, source_target_pairs={{0,8},{1,25},{8,16},{9,1},{16,24},{17,9},{24,0},{25,17},{2,10},{3,... | collective-permute-start | bytes 1179656 | tf_op jit(solution)/shard_map/ppermute | solution.py:38
  36.1 22.5 %collective-permute-start.13 = (bf16[32,3072]{1,0:T(8,128)(2,1)S(1)}, bf16[32,3072]{1,0:T(8,128)(2,1)S(1)}, u32[]{:S(2)}, u32[]{:S(2)}) collective-permute-start(bf16[32,3072]{1,0:T(8,128)(2,1)S(1)} %fusion.19), channel_id=1, source_target_pairs={{0,128},{32,160},{64,192},{96,224},{128,0},{160,32},{192,64},{224,... | collective-permute-start | bytes 589832 | tf_op jit(solution)/shard_map/ppermute | solution.py:28
  43.5 15.0 %collective-permute-start.15 = (bf16[32,3072]{1,0:T(8,128)(2,1)S(1)}, bf16[32,3072]{1,0:T(8,128)(2,1)S(1)}, u32[]{:S(2)}, u32[]{:S(2)}) collective-permute-start(bf16[32,3072]{1,0:T(8,128)(2,1)S(1)} %pad_maximum_fusion.12), channel_id=1, source_target_pairs={{0,192},{32,224},{64,0},{96,32},{128,64},{160,96},{192,128},{224,1... | collective-permute-start | bytes 589832 | tf_op jit(solution)/shard_map/ppermute | solution.py:28
  51.6 9.3 %collective-permute-start.14 = (bf16[32,3072]{1,0:T(8,128)(2,1)S(1)}, bf16[32,3072]{1,0:T(8,128)(2,1)S(1)}, u32[]{:S(2)}, u32[]{:S(2)}) collective-permute-start(bf16[32,3072]{1,0:T(8,128)(2,1)S(1)} %pad_maximum_fusion.11), channel_id=1, source_target_pairs={{0,64},{32,96},{64,128},{96,160},{128,192},{160,224},{192,0},{224,... | collective-permute-start | bytes 589832 | tf_op jit(solution)/shard_map/ppermute | solution.py:28
  51.6 9.2 %collective-permute-start.10 = (bf16[32,3072]{1,0:T(8,128)(2,1)S(1)}, bf16[32,3072]{1,0:T(8,128)(2,1)S(1)}, u32[]{:S(2)}, u32[]{:S(2)}) collective-permute-start(bf16[32,3072]{1,0:T(8,128)(2,1)S(1)} %get-tuple-element.16), channel_id=1, source_target_pairs={{0,24},{1,9},{8,0},{9,17},{16,8},{17,25},{24,16},{25,1},{2,26},{3,... | collective-permute-start | bytes 589832 | tf_op jit(solution)/shard_map/ppermute | solution.py:38
  54.8 7.0 %collective-permute-start.9 = (bf16[32,3072]{1,0:T(8,128)(2,1)S(1)}, bf16[32,3072]{1,0:T(8,128)(2,1)S(1)}, u32[]{:S(2)}, u32[]{:S(2)}) collective-permute-start(bf16[32,3072]{1,0:T(8,128)(2,1)S(1)} %fusion.16), channel_id=1, source_target_pairs={{0,8},{1,25},{8,16},{9,1},{16,24},{17,9},{24,0},{25,17},{2,10},{3,... | collective-permute-start | bytes 589832 | tf_op jit(solution)/shard_map/ppermute | solution.py:38
  61.9 8.0 %collective-permute-start.16 = (bf16[32,3072]{1,0:T(8,128)(2,1)S(1)}, bf16[32,3072]{1,0:T(8,128)(2,1)S(1)}, u32[]{:S(2)}, u32[]{:S(2)}) collective-permute-start(bf16[32,3072]{1,0:T(8,128)(2,1)S(1)} %get-tuple-element.23), channel_id=1, source_target_pairs={{0,32},{32,0},{64,96},{96,64},{128,160},{160,128},{192,224},{224,1... | collective-permute-start | bytes 589832 | tf_op jit(solution)/shard_map/ppermute | solution.py:107
  70.1 12.3 %collective-permute-start.17 = (bf16[32,3072]{1,0:T(8,128)(2,1)S(1)}, bf16[32,3072]{1,0:T(8,128)(2,1)S(1)}, u32[]{:S(2)}, u32[]{:S(2)}) collective-permute-start(bf16[32,3072]{1,0:T(8,128)(2,1)S(1)} %pad_maximum_fusion.13), channel_id=1, source_target_pairs={{0,192},{32,224},{64,0},{96,32},{128,64},{160,96},{192,128},{224,1... | collective-permute-start | bytes 589832 | tf_op jit(solution)/shard_map/ppermute | solution.py:28
  70.7 11.7 %collective-permute-start.18 = (bf16[32,3072]{1,0:T(8,128)(2,1)S(1)}, bf16[32,3072]{1,0:T(8,128)(2,1)S(1)}, u32[]{:S(2)}, u32[]{:S(2)}) collective-permute-start(bf16[32,3072]{1,0:T(8,128)(2,1)S(1)} %pad_maximum_fusion.13), channel_id=1, source_target_pairs={{0,64},{32,96},{64,128},{96,160},{128,192},{160,224},{192,0},{224,... | collective-permute-start | bytes 589832 | tf_op jit(solution)/shard_map/ppermute | solution.py:28
  73.1 9.3 %collective-permute-start.19 = (bf16[32,3072]{1,0:T(8,128)(2,1)S(1)}, bf16[32,3072]{1,0:T(8,128)(2,1)S(1)}, u32[]{:S(2)}, u32[]{:S(2)}) collective-permute-start(bf16[32,3072]{1,0:T(8,128)(2,1)S(1)} %pad_maximum_fusion.13), channel_id=1, source_target_pairs={{0,24},{1,9},{8,0},{9,17},{16,8},{17,25},{24,16},{25,1},{2,26},{3,... | collective-permute-start | bytes 589832 | tf_op jit(solution)/shard_map/ppermute | solution.py:38
  73.1 9.3 %collective-permute-start.20 = (bf16[32,3072]{1,0:T(8,128)(2,1)S(1)}, bf16[32,3072]{1,0:T(8,128)(2,1)S(1)}, u32[]{:S(2)}, u32[]{:S(2)}) collective-permute-start(bf16[32,3072]{1,0:T(8,128)(2,1)S(1)} %pad_maximum_fusion.13), channel_id=1, source_target_pairs={{0,8},{1,25},{8,16},{9,1},{16,24},{17,9},{24,0},{25,17},{2,10},{3,... | collective-permute-start | bytes 589832 | tf_op jit(solution)/shard_map/ppermute | solution.py:38
  77.2 10.1 %collective-permute-start.24 = (bf16[32,3072]{1,0:T(8,128)(2,1)S(1)}, bf16[32,3072]{1,0:T(8,128)(2,1)S(1)}, u32[]{:S(2)}, u32[]{:S(2)}) collective-permute-start(bf16[32,3072]{1,0:T(8,128)(2,1)S(1)} %pad_maximum_fusion.13), channel_id=1, source_target_pairs={{0,128},{32,160},{64,192},{96,224},{128,0},{160,32},{192,64},{224,... | collective-permute-start | bytes 589832 | tf_op jit(solution)/shard_map/ppermute | solution.py:28
  82.4 9.1 %collective-permute-start.21 = (bf16[32,3072]{1,0:T(8,128)(2,1)S(1)}, bf16[32,3072]{1,0:T(8,128)(2,1)S(1)}, u32[]{:S(2)}, u32[]{:S(2)}) collective-permute-start(bf16[32,3072]{1,0:T(8,128)(2,1)S(1)} %collective-permute-done.19), channel_id=1, source_target_pairs={{0,24},{1,9},{8,0},{9,17},{16,8},{17,25},{24,16},{25,1},{2,26},{3,... | collective-permute-start | bytes 589832 | tf_op jit(solution)/shard_map/ppermute | solution.py:38
  83.4 18.2 %collective-permute-start.23 = (bf16[64,3072]{1,0:T(8,128)(2,1)S(1)}, bf16[64,3072]{1,0:T(8,128)(2,1)S(1)}, u32[]{:S(2)}, u32[]{:S(2)}) collective-permute-start(bf16[64,3072]{1,0:T(8,128)(2,1)S(1)} %constant_dynamic-update-slice_fusion), channel_id=1, source_target_pairs={{0,24},{1,9},{8,0},{9,17},{16,8},{17,25},{24,16},{25,1},{2,26},{3,... | collective-permute-start | bytes 1179656 | tf_op jit(solution)/shard_map/ppermute | solution.py:38
  85.8 15.9 %collective-permute-start.22 = (bf16[64,3072]{1,0:T(8,128)(2,1)S(1)}, bf16[64,3072]{1,0:T(8,128)(2,1)S(1)}, u32[]{:S(2)}, u32[]{:S(2)}) collective-permute-start(bf16[64,3072]{1,0:T(8,128)(2,1)S(1)} %constant_dynamic-update-slice_fusion), channel_id=1, source_target_pairs={{0,8},{1,25},{8,16},{9,1},{16,24},{17,9},{24,0},{25,17},{2,10},{3,... | collective-permute-start | bytes 1179656 | tf_op jit(solution)/shard_map/ppermute | solution.py:38
  87.3 11.7 %collective-permute-start.25 = (bf16[32,3072]{1,0:T(8,128)(2,1)S(1)}, bf16[32,3072]{1,0:T(8,128)(2,1)S(1)}, u32[]{:S(2)}, u32[]{:S(2)}) collective-permute-start(bf16[32,3072]{1,0:T(8,128)(2,1)S(1)} %collective-permute-done.24), channel_id=1, source_target_pairs={{0,24},{1,9},{8,0},{9,17},{16,8},{17,25},{24,16},{25,1},{2,26},{3,... | collective-permute-start | bytes 589832 | tf_op jit(solution)/shard_map/ppermute | solution.py:38
  87.9 11.9 %collective-permute-start.27 = (bf16[32,3072]{1,0:T(8,128)(2,1)S(1)}, bf16[32,3072]{1,0:T(8,128)(2,1)S(1)}, u32[]{:S(2)}, u32[]{:S(2)}) collective-permute-start(bf16[32,3072]{1,0:T(8,128)(2,1)S(1)} %collective-permute-done.24), channel_id=1, source_target_pairs={{0,8},{1,25},{8,16},{9,1},{16,24},{17,9},{24,0},{25,17},{2,10},{3,... | collective-permute-start | bytes 589832 | tf_op jit(solution)/shard_map/ppermute | solution.py:38
  101.6 11.2 %collective-permute-start.26 = (bf16[96,3072]{1,0:T(8,128)(2,1)S(1)}, bf16[96,3072]{1,0:T(8,128)(2,1)S(1)}, u32[]{:S(2)}, u32[]{:S(2)}) collective-permute-start(bf16[96,3072]{1,0:T(8,128)(2,1)S(1)} %pad_maximum_fusion), channel_id=1, source_target_pairs={{0,24},{1,9},{8,0},{9,17},{16,8},{17,25},{24,16},{25,1},{2,26},{3,... | collective-permute-start | bytes 1769480 | tf_op jit(solution)/shard_map/ppermute | solution.py:38
  117.9 11.2 %collective-permute-start.31 = (f32[2,16,384]{2,1,0:T(8,128)S(1)}, f32[2,16,384]{2,1,0:T(8,128)S(1)}, u32[]{:S(2)}, u32[]{:S(2)}) collective-permute-start(f32[2,16,384]{2,1,0:T(8,128)S(1)} %fusion.67), channel_id=1, source_target_pairs={{0,6},{1,3},{2,0},{3,5},{4,2},{5,7},{6,4},{7,1},{8,14},{9,11},{10,... | collective-permute-start | bytes 147464 | tf_op jit(solution)/shard_map/ppermute | solution.py:38
  (10 other events, 56.5 us)

commit v3 on v2

--- a/solution.py
+++ b/solution.py
@@ -38,6 +38,14 @@
     return lax.ppermute(value, (axis, "core"), pairs)
 
 
+def shift_between_pairs(value, by):
+    return lax.ppermute(value, "z", [(i, (i + by * (2 * (i % 2) - 1)) % NZ) for i in range(NZ)])
+
+
+def swap_in_pair(value):
+    return lax.ppermute(value, "z", [(i, i ^ 1) for i in range(NZ)])
+
+
 def swap_cores(value):
     return lax.ppermute(value, "core", [(0, 1), (1, 0)])
 
@@ -69,7 +77,13 @@
     chip = jnp.concatenate([both, swap_cores(both)])
     next_x, far_x, last_x = (shift_apart(chip, "x", -1), shift(chip, "x", 2), shift_apart(chip, "x", 1))
     both = jnp.stack([chip, next_x, far_x, last_x])
-    both = roll(roll(both, 0, way * (y - x)), 1, z // 2 - half * core)
+    pair, odd = z // 2, z % 2 == 1
+    both = roll(both, 0, way * (y - x))
+    both = roll(
+        jnp.where(odd, both, both[:, ::-1]),
+        1,
+        jnp.where(odd, pair - half * core, half * core + n_pair - 1 - pair),
+    )
 
     order = (2, 1, 3, 0)
     rows = jnp.concatenate([both[:, j] for j in order], axis=1).reshape(-1, 2 * width)
@@ -93,57 +107,75 @@
     far, mid, own = parts_of(0, 1), parts_of(1, 3), parts_of(3, 4)
     relay, last_far = first_hops(far)
     message, mid[2], mid[3] = tie((second_message(far, relay), mid[2], mid[3]))
-    sum_far = finish(far, message, last_far)
+    sum_far = finish(far, message, last_far).astype(BF16)
     relay, last_mid = first_hops(mid)
-    sum_mid = finish(mid, second_message(mid, relay), last_mid)
-    sum_mid, own[2], own[3] = tie((sum_mid.astype(BF16), own[2], own[3]))
+    message = second_message(mid, relay)
+    sum_mid = finish(mid, message, last_mid).astype(BF16)
+    sum_mid, own[2], own[3] = tie((sum_mid, own[2], own[3]))
+
+    pre_1, pre_3, back_1, back_3 = split_rows(sum_mid, 4)
+    from_z = shift_between_pairs(jnp.concatenate([pre_3, back_3]), -2).astype(F32)
+    from_z = from_z + shift_between_pairs(jnp.concatenate([pre_1, back_1]), 1).astype(F32)
+    from_z = tie(from_z + shift_between_pairs(sum_far, 3).astype(F32))
     relay, last_own = first_hops(own)
     total = finish(own, second_message(own, relay), last_own)
-
-    total = total + shift(sum_far.astype(BF16), "z", 4).astype(F32)
-    pre_1, pre_3, back_1, back_3 = split_rows(sum_mid, 4)
-    total = total + shift(jnp.concatenate([pre_1, back_1]), "z", 2).astype(F32)
-    total = total + shift(jnp.concatenate([pre_3, back_3]), "z", -2).astype(F32)
-    total = total + lax.ppermute(total.astype(BF16), "z", [(i, i ^ 1) for i in range(NZ)]).astype(F32)
+    total = total + from_z
+    total = total + swap_in_pair(total.astype(BF16)).astype(F32)
     pre_act, grad_hidden = total[:unit], total[unit:]
     hidden = gelu_tanh(pre_act).astype(BF16)
     grad_pre = (grad_hidden * gelu_slope(pre_act)).astype(BF16)
 
-    mine = jnp.concatenate([hidden, grad_pre])
-    have_1, have_3 = shift(mine, "z", -2), shift(mine, "z", 2)
-    have_2 = shift(mine, "z", 4)
-
     def neighbours(message):
         return shift_apart(message, "y", -1), shift_apart(message, "y", 1)
 
-    next_own, last_own = neighbours(mine)
-    have_1, have_3, next_own, last_own = tie((have_1, have_3, next_own, last_own))
-    relay_own = shift_apart(next_own, "y", -1)
-    have_mid, have_far = jnp.concatenate([have_1, have_3]), have_2
-    next_mid, last_mid = neighbours(have_mid)
+    mine = jnp.concatenate([hidden, grad_pre])
+    have_1 = shift_between_pairs(mine, 1)
+    have_3 = swap_in_pair(have_1)
+    have_2 = shift_between_pairs(have_3, 1)
+    have_near = jnp.concatenate([mine, have_1])
+    next_near, last_near = neighbours(have_near)
+    next_near, have_2, have_3 = tie((next_near, have_2, have_3))
+    relay_near = shift_apart(next_near, "y", -1)
+    have_far = jnp.concatenate([have_3, have_2])
     next_far, last_far = neighbours(have_far)
-    relay = shift_apart(jnp.concatenate([next_mid, next_far]), "y", -1)
+    relay_near, relay_far = tie((relay_near, shift_apart(next_far, "y", -1)))
 
-    groups = (
-        ((0,), (3, 0, 1, 2), (last_own, mine, next_own, relay_own)),
-        ((1, 3), (3, 0, 1), (last_mid, have_mid, next_mid)),
-        ((2,), (3, 0, 1), (last_far, have_far, next_far)),
-        ((1, 3, 2), (2,), (relay,)),
+    stages = (
+        (((0, 1), (3, 0, 1), (last_near, have_near, next_near)),),
+        (
+            ((0, 1), (2,), (relay_near,)),
+            ((3, 2), (3, 0, 1), (last_far, have_far, next_far)),
+            ((3, 2), (2,), (relay_far,)),
+        ),
     )
-    in_blocks, up_sum, down_sum = {}, 0.0, 0.0
-    for js, es, messages in groups:
-        parts = [split_rows(message, 2 * len(js)) for message in messages]
-        hidden = jnp.concatenate([row for p in parts for row in p[0::2]])
-        grad_pre = jnp.concatenate([row for p in parts for row in p[1::2]])
-        rows = jnp.concatenate([both[e, j] for e in es for j in js])
-        in_part = contract(grad_pre, up_weight, 1, 1).reshape(len(es), len(js), unit, width)
-        for i, j in enumerate(js):
-            in_blocks.setdefault(j, []).append(in_part[:, i])
-        up_sum = up_sum + contract(rows[:, :width], grad_pre, 0, 0)
-        down_sum = down_sum + contract(hidden, rows[:, width:], 0, 0)
+    in_blocks, sums = {}, (0.0, 0.0)
+    for stage in stages:
+        hidden, grad_pre, rows = [], [], []
+        for js, es, messages in stage:
+            parts = [split_rows(message, 2 * len(js)) for message in messages]
+            hidden += [row for p in parts for row in p[0::2]]
+            grad_pre += [row for p in parts for row in p[1::2]]
+            rows += [both[e, j] for e in es for j in js]
+        hidden, grad_pre, rows = (jnp.concatenate(v) for v in (hidden, grad_pre, rows))
+        in_part = iter(split_rows(contract(grad_pre, up_weight, 1, 1), rows.shape[0] // unit))
+        for js, es, _ in stage:
+            for _ in es:
+                for j in js:
+                    in_blocks.setdefault(j, []).append(next(in_part))
+        sums = tie(sums)
+        sums = (
+            sums[0] + contract(rows[:, :width], grad_pre, 0, 0),
+            sums[1] + contract(hidden, rows[:, width:], 0, 0),
+        )
+    up_sum, down_sum = sums
 
-    in_total = jnp.stack([jnp.concatenate(in_blocks[j]) for j in range(n_pair)], axis=1)
-    in_total = roll(roll(in_total, 0, way * (x - y) + 1), 1, half * core - z // 2)
+    in_total = jnp.stack([jnp.stack(in_blocks[j]) for j in range(n_pair)], axis=1)
+    in_total = roll(in_total, 0, way * (x - y) + 1)
+    in_total = roll(
+        jnp.where(odd, in_total, in_total[:, ::-1]),
+        1,
+        jnp.where(odd, half * core - pair, half * core + n_pair - 1 - pair),
+    )
     other = swap_cores(in_total[:, half:])
     in_chip = [in_total[e, :half] + other[-e % NX] for e in range(NX)]
     in_mine = in_chip[0] + shift(in_chip[2], "x", 2)

time: 134 us -> 123 us (0.918); the launches traced: 132 us -> 122 us
  starting transfers between devices: 63.9 us -> 50.1 us
  waiting for transfers between devices: 47.6 us -> 55.7 us
  matrix products: 14.6 us -> 10 us
    ppermute x8 -> x2, starting transfers between devices: 19.4 us -> 3.83 us  [shift(): return lax.ppermute(value, axis, [(i, (i + by) % n) for i in range(n)])]
    ppermute x1 -> x7, starting transfers between devices: 1.1 us -> 16 us  [the longest x5 15.7 us: shift_between_pairs(): lax.ppermute(value, 'z', [(i, (i + by * (2 * (i % 2) - 1)) % NZ) for i in...]
    ppermute x1 -> x7, waiting for transfers between devices: 6.91 us -> 20.2 us  [the longest x2 11.1 us: swap_in_pair(): return lax.ppermute(value, 'z', [(i, i ^ 1) for i in range(NZ)])]
    ppermute x21 -> x19, starting transfers between devices: 43.2 us -> 30.2 us  [shift_apart(): return lax.ppermute(value, (axis, 'core'), pairs)]
    ppermute x8 -> x2, waiting for transfers between devices: 7.41 us -> 2.29 us  [shift(): return lax.ppermute(value, axis, [(i, (i + by) % n) for i in range(n)])]
    dot_general x13 -> x7, matrix products: 13.6 us -> 9.02 us  [contract(): lax.dot_general(left, right, (((left_dim,), (right_dim,)), ((), ())), pre...]
    ppermute x21 -> x19, waiting for transfers between devices: 32.2 us -> 32.1 us  [shift_apart(): return lax.ppermute(value, (axis, 'core'), pairs)]
  transfers between devices with their start and end apart: 32 -> 30, of which waited for: 16 -> 16; matrix products, arithmetic and copies ran while one was open for 10% -> 6% of each run, Pallas kernels for 0% -> 0%
where the time goes in v3:
time: 123 us; the launch traced here: 122 us
  waiting for transfers between devices  55.7 us (45%)
  starting transfers between devices  50.1 us (41%)
  matrix products  10 us (8%)
  other arithmetic  3.05 us (2%)
  local copies, waits for them, and re-layouts  2.1 us (2%)
  between operations  1.34 us (1%)
    ppermute x19, waiting for transfers between devices, shift_apart(): return lax.ppermute(value, (axis, 'core'), pairs)  32.1 us
    ppermute x19, starting transfers between devices, shift_apart(): return lax.ppermute(value, (axis, 'core'), pairs)  30.2 us
    ppermute x5, starting transfers between devices, shift_between_pairs(): lax.ppermute(value, 'z', [(i, (i + by * (2 * (i % 2) - 1)) % NZ) for i in...  15.7 us
    ppermute x2, waiting for transfers between devices, swap_in_pair(): return lax.ppermute(value, 'z', [(i, i ^ 1) for i in range(NZ)])  11.1 us
    ppermute x5, waiting for transfers between devices, shift_between_pairs(): lax.ppermute(value, 'z', [(i, (i + by * (2 * (i % 2) - 1)) % NZ) for i in...  9.11 us
    dot_general x7, matrix products, contract(): lax.dot_general(left, right, (((left_dim,), (right_dim,)), ((), ())), pre...  9.02 us
    ppermute x2, starting transfers between devices, shift(): return lax.ppermute(value, axis, [(i, (i + by) % n) for i in range(n)])  3.83 us
  transfers between devices with their start and end apart: 30, of which 16 were waited for; matrix products, arithmetic and copies ran while one was open for 6% of the time, Pallas kernels for 0%

profile of v3, /device:TPU:24, one launch (start us, length us, event | category | flops | bytes accessed | tf_op | source)
XLA Modules:
  0.0 122.3 jit_solution(9546224406599510636)
XLA Ops:
  2.8 3.1 %collective-permute-start.2 = (bf16[4,16,768]{2,1,0:T(8,128)(2,1)S(1)}, bf16[4,16,768]{2,1,0:T(8,128)(2,1)S(1)}, u32[]{:S(2)}, u32[]{:S(2)}) collective-permute-start(bf16[4,16,768]{2,1,0:T(8,128)(2,1)S(1)} %pad_maximum_fusion.11), channel_id=1, source_target_pairs={{0,4},{2,6},{4,0},{6,2},{1,5},{3,7},{5,1},{7,3},{8,12},{10,14},{12... | collective-permute-start | bytes 294920 | tf_op jit(solution)/shard_map/ppermute | solution.py:28
  7.9 3.5 %collective-permute-done.1 = bf16[4,16,768]{2,1,0:T(8,128)(2,1)S(1)} collective-permute-done((bf16[4,16,768]{2,1,0:T(8,128)(2,1)S(1)}, bf16[4,16,768]{2,1,0:T(8,128)(2,1)S(1)}, u32[]{:S(2)}, u32[]{:S(2)}) %collective-permute-start.1) | collective-permute-done | bytes 98336 | tf_op jit(solution)/shard_map/ppermute | solution.py:38
  19.3 3.5 %collective-permute-done.4 = bf16[32,3072]{1,0:T(8,128)(2,1)S(1)} collective-permute-done((bf16[32,3072]{1,0:T(8,128)(2,1)S(1)}, bf16[32,3072]{1,0:T(8,128)(2,1)S(1)}, u32[]{:S(2)}, u32[]{:S(2)}) %collective-permute-start.4) | collective-permute-done | bytes 196640 | tf_op jit(solution)/shard_map/ppermute | solution.py:38
  22.8 3.5 %collective-permute-start.5 = (bf16[64,3072]{1,0:T(8,128)(2,1)S(1)}, bf16[64,3072]{1,0:T(8,128)(2,1)S(1)}, u32[]{:S(2)}, u32[]{:S(2)}) collective-permute-start(bf16[64,3072]{1,0:T(8,128)(2,1)S(1)} %get-tuple-element.18), channel_id=1, source_target_pairs={{0,8},{1,25},{8,16},{9,1},{16,24},{17,9},{24,0},{25,17},{2,10},{3,... | collective-permute-start | bytes 1179656 | tf_op jit(solution)/shard_map/ppermute | solution.py:38
  28.4 4.2 %collective-permute-done.5 = bf16[64,3072]{1,0:T(8,128)(2,1)S(1)} collective-permute-done((bf16[64,3072]{1,0:T(8,128)(2,1)S(1)}, bf16[64,3072]{1,0:T(8,128)(2,1)S(1)}, u32[]{:S(2)}, u32[]{:S(2)}) %collective-permute-start.5) | collective-permute-done | bytes 393248 | tf_op jit(solution)/shard_map/ppermute | solution.py:38
  32.7 3.8 %collective-permute-start.6 = (bf16[64,3072]{1,0:T(8,128)(2,1)S(1)}, bf16[64,3072]{1,0:T(8,128)(2,1)S(1)}, u32[]{:S(2)}, u32[]{:S(2)}) collective-permute-start(bf16[64,3072]{1,0:T(8,128)(2,1)S(1)} %fusion.2), channel_id=1, source_target_pairs={{0,8},{1,25},{8,16},{9,1},{16,24},{17,9},{24,0},{25,17},{2,10},{3,... | collective-permute-start | bytes 1179656 | tf_op jit(solution)/shard_map/ppermute | solution.py:38
  36.6 6.8 %collective-permute-start.15 = (bf16[32,3072]{1,0:T(8,128)(2,1)S(1)}, bf16[32,3072]{1,0:T(8,128)(2,1)S(1)}, u32[]{:S(2)}, u32[]{:S(2)}) collective-permute-start(bf16[32,3072]{1,0:T(8,128)(2,1)S(1)} %fusion.17), channel_id=1, source_target_pairs={{0,160},{32,128},{64,224},{96,192},{128,32},{160,0},{192,96},{224,... | collective-permute-start | bytes 589832 | tf_op jit(solution)/shard_map/ppermute | solution.py:42
  43.5 2.2 %collective-permute-start.8 = (bf16[32,3072]{1,0:T(8,128)(2,1)S(1)}, bf16[32,3072]{1,0:T(8,128)(2,1)S(1)}, u32[]{:S(2)}, u32[]{:S(2)}) collective-permute-start(bf16[32,3072]{1,0:T(8,128)(2,1)S(1)} %get-tuple-element.20), channel_id=1, source_target_pairs={{0,8},{1,25},{8,16},{9,1},{16,24},{17,9},{24,0},{25,17},{2,10},{3,... | collective-permute-start | bytes 589832 | tf_op jit(solution)/shard_map/ppermute | solution.py:38
  45.8 5.9 %collective-permute-start.12 = (bf16[32,3072]{1,0:T(8,128)(2,1)S(1)}, bf16[32,3072]{1,0:T(8,128)(2,1)S(1)}, u32[]{:S(2)}, u32[]{:S(2)}) collective-permute-start(bf16[32,3072]{1,0:T(8,128)(2,1)S(1)} %pad_maximum_fusion.8), channel_id=1, source_target_pairs={{0,224},{32,64},{64,32},{96,128},{128,96},{160,192},{192,160},{224... | collective-permute-start | bytes 589832 | tf_op jit(solution)/shard_map/ppermute | solution.py:42
  51.9 3.3 %collective-permute-start.9 = (bf16[32,3072]{1,0:T(8,128)(2,1)S(1)}, bf16[32,3072]{1,0:T(8,128)(2,1)S(1)}, u32[]{:S(2)}, u32[]{:S(2)}) collective-permute-start(bf16[32,3072]{1,0:T(8,128)(2,1)S(1)} %fusion.14), channel_id=1, source_target_pairs={{0,8},{1,25},{8,16},{9,1},{16,24},{17,9},{24,0},{25,17},{2,10},{3,... | collective-permute-start | bytes 589832 | tf_op jit(solution)/shard_map/ppermute | solution.py:38
  55.2 2.8 %collective-permute-done.12 = bf16[32,3072]{1,0:T(8,128)(2,1)S(1)} collective-permute-done((bf16[32,3072]{1,0:T(8,128)(2,1)S(1)}, bf16[32,3072]{1,0:T(8,128)(2,1)S(1)}, u32[]{:S(2)}, u32[]{:S(2)}) %collective-permute-start.12) | collective-permute-done | bytes 196640 | tf_op jit(solution)/shard_map/ppermute | solution.py:42
  60.0 5.5 %collective-permute-done.16 = bf16[32,3072]{1,0:T(8,128)(2,1)S(1)} collective-permute-done((bf16[32,3072]{1,0:T(8,128)(2,1)S(1)}, bf16[32,3072]{1,0:T(8,128)(2,1)S(1)}, u32[]{:S(2)}, u32[]{:S(2)}) %collective-permute-start.16) | collective-permute-done | bytes 196640 | tf_op jit(solution)/shard_map/ppermute | solution.py:46
  65.8 2.3 %collective-permute-start.17 = (bf16[32,3072]{1,0:T(8,128)(2,1)S(1)}, bf16[32,3072]{1,0:T(8,128)(2,1)S(1)}, u32[]{:S(2)}, u32[]{:S(2)}) collective-permute-start(bf16[32,3072]{1,0:T(8,128)(2,1)S(1)} %pad_maximum_fusion.10), channel_id=1, source_target_pairs={{0,224},{32,64},{64,32},{96,128},{128,96},{160,192},{192,160},{224... | collective-permute-start | bytes 589832 | tf_op jit(solution)/shard_map/ppermute | solution.py:42
  68.1 4.7 %collective-permute-done.17 = bf16[32,3072]{1,0:T(8,128)(2,1)S(1)} collective-permute-done((bf16[32,3072]{1,0:T(8,128)(2,1)S(1)}, bf16[32,3072]{1,0:T(8,128)(2,1)S(1)}, u32[]{:S(2)}, u32[]{:S(2)}) %collective-permute-start.17) | collective-permute-done | bytes 196640 | tf_op jit(solution)/shard_map/ppermute | solution.py:42
  72.8 5.2 %collective-permute-start.18 = (bf16[64,3072]{1,0:T(8,128)(2,1)S(1)}, bf16[64,3072]{1,0:T(8,128)(2,1)S(1)}, u32[]{:S(2)}, u32[]{:S(2)}) collective-permute-start(bf16[64,3072]{1,0:T(8,128)(2,1)S(1)} %pad_maximum_fusion.3), channel_id=1, source_target_pairs={{0,8},{1,25},{8,16},{9,1},{16,24},{17,9},{24,0},{25,17},{2,10},{3,... | collective-permute-start | bytes 1179656 | tf_op jit(solution)/shard_map/ppermute | solution.py:38
  78.2 5.6 %collective-permute-done.20 = bf16[32,3072]{1,0:T(8,128)(2,1)S(1)} collective-permute-done((bf16[32,3072]{1,0:T(8,128)(2,1)S(1)}, bf16[32,3072]{1,0:T(8,128)(2,1)S(1)}, u32[]{:S(2)}, u32[]{:S(2)}) %collective-permute-start.20) | collective-permute-done | bytes 196640 | tf_op jit(solution)/shard_map/ppermute | solution.py:46
  84.4 6.2 %collective-permute-done.19 = bf16[64,3072]{1,0:T(8,128)(2,1)S(1)} collective-permute-done((bf16[64,3072]{1,0:T(8,128)(2,1)S(1)}, bf16[64,3072]{1,0:T(8,128)(2,1)S(1)}, u32[]{:S(2)}, u32[]{:S(2)}) %collective-permute-start.19) | collective-permute-done | bytes 393248 | tf_op jit(solution)/shard_map/ppermute | solution.py:38
  94.4 5.4 %collective-permute-done.23 = bf16[64,3072]{1,0:T(8,128)(2,1)S(1)} collective-permute-done((bf16[64,3072]{1,0:T(8,128)(2,1)S(1)}, bf16[64,3072]{1,0:T(8,128)(2,1)S(1)}, u32[]{:S(2)}, u32[]{:S(2)}) %collective-permute-start.23) | collective-permute-done | bytes 393248 | tf_op jit(solution)/shard_map/ppermute | solution.py:38
  101.4 2.7 %collective-permute-done.22 = bf16[64,3072]{1,0:T(8,128)(2,1)S(1)} collective-permute-done((bf16[64,3072]{1,0:T(8,128)(2,1)S(1)}, bf16[64,3072]{1,0:T(8,128)(2,1)S(1)}, u32[]{:S(2)}, u32[]{:S(2)}) %collective-permute-start.22) | collective-permute-done | bytes 393248 | tf_op jit(solution)/shard_map/ppermute | solution.py:38
  104.0 4.8 %collective-permute-done.24 = bf16[64,3072]{1,0:T(8,128)(2,1)S(1)} collective-permute-done((bf16[64,3072]{1,0:T(8,128)(2,1)S(1)}, bf16[64,3072]{1,0:T(8,128)(2,1)S(1)}, u32[]{:S(2)}, u32[]{:S(2)}) %collective-permute-start.24) | collective-permute-done | bytes 393248 | tf_op jit(solution)/shard_map/ppermute | solution.py:38
  110.5 2.2 %add_convert_fusion.1 = bf16[384,3072]{1,0:T(8,128)(2,1)} fusion(f32[384,3072]{1,0:T(8,128)S(1)} %convolution_add_fusion.1, bf16[160,3072]{1,0:T(8,128)(2,1)S(1)} %get-tuple-element.60, bf16[160,768]{1,0:T(8,128)(2,1)S(1)} %get-tuple-element.75), kind=kOutput, calls=%fused_computation.1 | convolution fusion | flops 379846656 | bytes 8183808 | tf_op jit(solution)/shard_map/dot_general | solution.py:13
  112.7 2.8 %collective-permute-start.29 = (f32[2,16,384]{2,1,0:T(8,128)S(1)}, f32[2,16,384]{2,1,0:T(8,128)S(1)}, u32[]{:S(2)}, u32[]{:S(2)}) collective-permute-start(f32[2,16,384]{2,1,0:T(8,128)S(1)} %fusion.39), channel_id=1, source_target_pairs={{0,6},{1,3},{2,0},{3,5},{4,2},{5,7},{6,4},{7,1},{8,14},{9,11},{10,... | collective-permute-start | bytes 147464 | tf_op jit(solution)/shard_map/ppermute | solution.py:38
  116.5 2.4 %add_convert_fusion = bf16[3072,384]{1,0:T(8,128)(2,1)} fusion(f32[3072,384]{1,0:T(8,128)S(1)} %convolution_add_fusion, bf16[160,3072]{1,0:T(8,128)(2,1)S(1)} %get-tuple-element.59, bf16[160,768]{1,0:T(8,128)(2,1)S(1)} %get-tuple-element.75), kind=kOutput, calls=%fused_computation | convolution fusion | flops 379846656 | bytes 8183808 | tf_op jit(solution)/shard_map/dot_general | solution.py:13
  118.9 2.3 %collective-permute-done.27 = f32[2,16,384]{2,1,0:T(8,128)S(1)} collective-permute-done((f32[2,16,384]{2,1,0:T(8,128)S(1)}, f32[2,16,384]{2,1,0:T(8,128)S(1)}, u32[]{:S(2)}, u32[]{:S(2)}) %collective-permute-start.27) | collective-permute-done | bytes 49184 | tf_op jit(solution)/shard_map/ppermute | solution.py:28
  (130 shorter events, 26.4 us)
Async XLA Ops:
  2.8 8.7 %collective-permute-start.2 = (bf16[4,16,768]{2,1,0:T(8,128)(2,1)S(1)}, bf16[4,16,768]{2,1,0:T(8,128)(2,1)S(1)}, u32[]{:S(2)}, u32[]{:S(2)}) collective-permute-start(bf16[4,16,768]{2,1,0:T(8,128)(2,1)S(1)} %pad_maximum_fusion.11), channel_id=1, source_target_pairs={{0,4},{2,6},{4,0},{6,2},{1,5},{3,7},{5,1},{7,3},{8,12},{10,14},{12... | collective-permute-start | bytes 294920 | tf_op jit(solution)/shard_map/ppermute | solution.py:28
  7.1 5.8 %collective-permute-start.3 = (bf16[4,16,768]{2,1,0:T(8,128)(2,1)S(1)}, bf16[4,16,768]{2,1,0:T(8,128)(2,1)S(1)}, u32[]{:S(2)}, u32[]{:S(2)}) collective-permute-start(bf16[4,16,768]{2,1,0:T(8,128)(2,1)S(1)} %pad_maximum_fusion.11), channel_id=1, source_target_pairs={{0,2},{1,7},{2,4},{3,1},{4,6},{5,3},{6,0},{7,5},{8,10},{9,15},{10,... | collective-permute-start | bytes 294920 | tf_op jit(solution)/shard_map/ppermute | solution.py:38
  17.0 5.7 %collective-permute-start.4 = (bf16[32,3072]{1,0:T(8,128)(2,1)S(1)}, bf16[32,3072]{1,0:T(8,128)(2,1)S(1)}, u32[]{:S(2)}, u32[]{:S(2)}) collective-permute-start(bf16[32,3072]{1,0:T(8,128)(2,1)S(1)} %pad_maximum_fusion.4), channel_id=1, source_target_pairs={{0,8},{1,25},{8,16},{9,1},{16,24},{17,9},{24,0},{25,17},{2,10},{3,... | collective-permute-start | bytes 589832 | tf_op jit(solution)/shard_map/ppermute | solution.py:38
  17.6 18.9 %collective-permute-start.14 = (bf16[32,3072]{1,0:T(8,128)(2,1)S(1)}, bf16[32,3072]{1,0:T(8,128)(2,1)S(1)}, u32[]{:S(2)}, u32[]{:S(2)}) collective-permute-start(bf16[32,3072]{1,0:T(8,128)(2,1)S(1)} %pad_maximum_fusion.9), channel_id=1, source_target_pairs={{0,24},{1,9},{8,0},{9,17},{16,8},{17,25},{24,16},{25,1},{2,26},{3,... | collective-permute-start | bytes 589832 | tf_op jit(solution)/shard_map/ppermute | solution.py:38
  22.8 9.8 %collective-permute-start.5 = (bf16[64,3072]{1,0:T(8,128)(2,1)S(1)}, bf16[64,3072]{1,0:T(8,128)(2,1)S(1)}, u32[]{:S(2)}, u32[]{:S(2)}) collective-permute-start(bf16[64,3072]{1,0:T(8,128)(2,1)S(1)} %get-tuple-element.18), channel_id=1, source_target_pairs={{0,8},{1,25},{8,16},{9,1},{16,24},{17,9},{24,0},{25,17},{2,10},{3,... | collective-permute-start | bytes 1179656 | tf_op jit(solution)/shard_map/ppermute | solution.py:38
  26.3 10.2 %collective-permute-start.13 = (bf16[32,3072]{1,0:T(8,128)(2,1)S(1)}, bf16[32,3072]{1,0:T(8,128)(2,1)S(1)}, u32[]{:S(2)}, u32[]{:S(2)}) collective-permute-start(bf16[32,3072]{1,0:T(8,128)(2,1)S(1)} %fusion.15), channel_id=1, source_target_pairs={{0,8},{1,25},{8,16},{9,1},{16,24},{17,9},{24,0},{25,17},{2,10},{3,... | collective-permute-start | bytes 589832 | tf_op jit(solution)/shard_map/ppermute | solution.py:38
  26.4 17.0 %collective-permute-start.7 = (bf16[64,3072]{1,0:T(8,128)(2,1)S(1)}, bf16[64,3072]{1,0:T(8,128)(2,1)S(1)}, u32[]{:S(2)}, u32[]{:S(2)}) collective-permute-start(bf16[64,3072]{1,0:T(8,128)(2,1)S(1)} %get-tuple-element.19), channel_id=1, source_target_pairs={{0,24},{1,9},{8,0},{9,17},{16,8},{17,25},{24,16},{25,1},{2,26},{3,... | collective-permute-start | bytes 1179656 | tf_op jit(solution)/shard_map/ppermute | solution.py:38
  32.7 10.7 %collective-permute-start.6 = (bf16[64,3072]{1,0:T(8,128)(2,1)S(1)}, bf16[64,3072]{1,0:T(8,128)(2,1)S(1)}, u32[]{:S(2)}, u32[]{:S(2)}) collective-permute-start(bf16[64,3072]{1,0:T(8,128)(2,1)S(1)} %fusion.2), channel_id=1, source_target_pairs={{0,8},{1,25},{8,16},{9,1},{16,24},{17,9},{24,0},{25,17},{2,10},{3,... | collective-permute-start | bytes 1179656 | tf_op jit(solution)/shard_map/ppermute | solution.py:38
  36.6 18.6 %collective-permute-start.15 = (bf16[32,3072]{1,0:T(8,128)(2,1)S(1)}, bf16[32,3072]{1,0:T(8,128)(2,1)S(1)}, u32[]{:S(2)}, u32[]{:S(2)}) collective-permute-start(bf16[32,3072]{1,0:T(8,128)(2,1)S(1)} %fusion.17), channel_id=1, source_target_pairs={{0,160},{32,128},{64,224},{96,192},{128,32},{160,0},{192,96},{224,... | collective-permute-start | bytes 589832 | tf_op jit(solution)/shard_map/ppermute | solution.py:42
  43.5 8.3 %collective-permute-start.8 = (bf16[32,3072]{1,0:T(8,128)(2,1)S(1)}, bf16[32,3072]{1,0:T(8,128)(2,1)S(1)}, u32[]{:S(2)}, u32[]{:S(2)}) collective-permute-start(bf16[32,3072]{1,0:T(8,128)(2,1)S(1)} %get-tuple-element.20), channel_id=1, source_target_pairs={{0,8},{1,25},{8,16},{9,1},{16,24},{17,9},{24,0},{25,17},{2,10},{3,... | collective-permute-start | bytes 589832 | tf_op jit(solution)/shard_map/ppermute | solution.py:38
  45.7 13.9 %collective-permute-start.10 = (bf16[32,3072]{1,0:T(8,128)(2,1)S(1)}, bf16[32,3072]{1,0:T(8,128)(2,1)S(1)}, u32[]{:S(2)}, u32[]{:S(2)}) collective-permute-start(bf16[32,3072]{1,0:T(8,128)(2,1)S(1)} %get-tuple-element.21), channel_id=1, source_target_pairs={{0,24},{1,9},{8,0},{9,17},{16,8},{17,25},{24,16},{25,1},{2,26},{3,... | collective-permute-start | bytes 589832 | tf_op jit(solution)/shard_map/ppermute | solution.py:38
  45.8 12.2 %collective-permute-start.12 = (bf16[32,3072]{1,0:T(8,128)(2,1)S(1)}, bf16[32,3072]{1,0:T(8,128)(2,1)S(1)}, u32[]{:S(2)}, u32[]{:S(2)}) collective-permute-start(bf16[32,3072]{1,0:T(8,128)(2,1)S(1)} %pad_maximum_fusion.8), channel_id=1, source_target_pairs={{0,224},{32,64},{64,32},{96,128},{128,96},{160,192},{192,160},{224... | collective-permute-start | bytes 589832 | tf_op jit(solution)/shard_map/ppermute | solution.py:42
  51.7 7.9 %collective-permute-start.11 = (bf16[32,3072]{1,0:T(8,128)(2,1)S(1)}, bf16[32,3072]{1,0:T(8,128)(2,1)S(1)}, u32[]{:S(2)}, u32[]{:S(2)}) collective-permute-start(bf16[32,3072]{1,0:T(8,128)(2,1)S(1)} %pad_maximum_fusion.7), channel_id=1, source_target_pairs={{0,64},{32,224},{64,128},{96,32},{128,192},{160,96},{192,0},{224,1... | collective-permute-start | bytes 589832 | tf_op jit(solution)/shard_map/ppermute | solution.py:42
  51.9 7.8 %collective-permute-start.9 = (bf16[32,3072]{1,0:T(8,128)(2,1)S(1)}, bf16[32,3072]{1,0:T(8,128)(2,1)S(1)}, u32[]{:S(2)}, u32[]{:S(2)}) collective-permute-start(bf16[32,3072]{1,0:T(8,128)(2,1)S(1)} %fusion.14), channel_id=1, source_target_pairs={{0,8},{1,25},{8,16},{9,1},{16,24},{17,9},{24,0},{25,17},{2,10},{3,... | collective-permute-start | bytes 589832 | tf_op jit(solution)/shard_map/ppermute | solution.py:38
  59.8 5.8 %collective-permute-start.16 = (bf16[32,3072]{1,0:T(8,128)(2,1)S(1)}, bf16[32,3072]{1,0:T(8,128)(2,1)S(1)}, u32[]{:S(2)}, u32[]{:S(2)}) collective-permute-start(bf16[32,3072]{1,0:T(8,128)(2,1)S(1)} %fusion.47), channel_id=1, source_target_pairs={{0,32},{32,0},{64,96},{96,64},{128,160},{160,128},{192,224},{224,1... | collective-permute-start | bytes 589832 | tf_op jit(solution)/shard_map/ppermute | solution.py:46
  65.8 7.0 %collective-permute-start.17 = (bf16[32,3072]{1,0:T(8,128)(2,1)S(1)}, bf16[32,3072]{1,0:T(8,128)(2,1)S(1)}, u32[]{:S(2)}, u32[]{:S(2)}) collective-permute-start(bf16[32,3072]{1,0:T(8,128)(2,1)S(1)} %pad_maximum_fusion.10), channel_id=1, source_target_pairs={{0,224},{32,64},{64,32},{96,128},{128,96},{160,192},{192,160},{224... | collective-permute-start | bytes 589832 | tf_op jit(solution)/shard_map/ppermute | solution.py:42
  72.8 11.5 %collective-permute-start.18 = (bf16[64,3072]{1,0:T(8,128)(2,1)S(1)}, bf16[64,3072]{1,0:T(8,128)(2,1)S(1)}, u32[]{:S(2)}, u32[]{:S(2)}) collective-permute-start(bf16[64,3072]{1,0:T(8,128)(2,1)S(1)} %pad_maximum_fusion.3), channel_id=1, source_target_pairs={{0,8},{1,25},{8,16},{9,1},{16,24},{17,9},{24,0},{25,17},{2,10},{3,... | collective-permute-start | bytes 1179656 | tf_op jit(solution)/shard_map/ppermute | solution.py:38
  78.1 12.5 %collective-permute-start.19 = (bf16[64,3072]{1,0:T(8,128)(2,1)S(1)}, bf16[64,3072]{1,0:T(8,128)(2,1)S(1)}, u32[]{:S(2)}, u32[]{:S(2)}) collective-permute-start(bf16[64,3072]{1,0:T(8,128)(2,1)S(1)} %pad_maximum_fusion.3), channel_id=1, source_target_pairs={{0,24},{1,9},{8,0},{9,17},{16,8},{17,25},{24,16},{25,1},{2,26},{3,... | collective-permute-start | bytes 1179656 | tf_op jit(solution)/shard_map/ppermute | solution.py:38
  83.7 6.9 %collective-permute-start.21 = (bf16[32,3072]{1,0:T(8,128)(2,1)S(1)}, bf16[32,3072]{1,0:T(8,128)(2,1)S(1)}, u32[]{:S(2)}, u32[]{:S(2)}) collective-permute-start(bf16[32,3072]{1,0:T(8,128)(2,1)S(1)} %collective-permute-done.20), channel_id=1, source_target_pairs={{0,224},{32,64},{64,32},{96,128},{128,96},{160,192},{192,160},{224... | collective-permute-start | bytes 589832 | tf_op jit(solution)/shard_map/ppermute | solution.py:42
  90.6 18.2 %collective-permute-start.25 = (bf16[64,3072]{1,0:T(8,128)(2,1)S(1)}, bf16[64,3072]{1,0:T(8,128)(2,1)S(1)}, u32[]{:S(2)}, u32[]{:S(2)}) collective-permute-start(bf16[64,3072]{1,0:T(8,128)(2,1)S(1)} %constant_dynamic-update-slice_fusion.14), channel_id=1, source_target_pairs={{0,8},{1,25},{8,16},{9,1},{16,24},{17,9},{24,0},{25,17},{2,10},{3,... | collective-permute-start | bytes 1179656 | tf_op jit(solution)/shard_map/ppermute | solution.py:38
  90.8 9.0 %collective-permute-start.23 = (bf16[64,3072]{1,0:T(8,128)(2,1)S(1)}, bf16[64,3072]{1,0:T(8,128)(2,1)S(1)}, u32[]{:S(2)}, u32[]{:S(2)}) collective-permute-start(bf16[64,3072]{1,0:T(8,128)(2,1)S(1)} %constant_dynamic-update-slice_fusion.14), channel_id=1, source_target_pairs={{0,24},{1,9},{8,0},{9,17},{16,8},{17,25},{24,16},{25,1},{2,26},{3,... | collective-permute-start | bytes 1179656 | tf_op jit(solution)/shard_map/ppermute | solution.py:38
  92.7 11.3 %collective-permute-start.22 = (bf16[64,3072]{1,0:T(8,128)(2,1)S(1)}, bf16[64,3072]{1,0:T(8,128)(2,1)S(1)}, u32[]{:S(2)}, u32[]{:S(2)}) collective-permute-start(bf16[64,3072]{1,0:T(8,128)(2,1)S(1)} %collective-permute-done.19), channel_id=1, source_target_pairs={{0,24},{1,9},{8,0},{9,17},{16,8},{17,25},{24,16},{25,1},{2,26},{3,... | collective-permute-start | bytes 1179656 | tf_op jit(solution)/shard_map/ppermute | solution.py:38
  99.8 9.0 %collective-permute-start.24 = (bf16[64,3072]{1,0:T(8,128)(2,1)S(1)}, bf16[64,3072]{1,0:T(8,128)(2,1)S(1)}, u32[]{:S(2)}, u32[]{:S(2)}) collective-permute-start(bf16[64,3072]{1,0:T(8,128)(2,1)S(1)} %collective-permute-done.23), channel_id=1, source_target_pairs={{0,24},{1,9},{8,0},{9,17},{16,8},{17,25},{24,16},{25,1},{2,26},{3,... | collective-permute-start | bytes 1179656 | tf_op jit(solution)/shard_map/ppermute | solution.py:38
  112.7 6.2 %collective-permute-start.29 = (f32[2,16,384]{2,1,0:T(8,128)S(1)}, f32[2,16,384]{2,1,0:T(8,128)S(1)}, u32[]{:S(2)}, u32[]{:S(2)}) collective-permute-start(f32[2,16,384]{2,1,0:T(8,128)S(1)} %fusion.39), channel_id=1, source_target_pairs={{0,6},{1,3},{2,0},{3,5},{4,2},{5,7},{6,4},{7,1},{8,14},{9,11},{10,... | collective-permute-start | bytes 147464 | tf_op jit(solution)/shard_map/ppermute | solution.py:38
  (8 other events, 42.6 us)

commit v4 on v3

--- a/solution.py
+++ b/solution.py
@@ -131,7 +131,7 @@
     mine = jnp.concatenate([hidden, grad_pre])
     have_1 = shift_between_pairs(mine, 1)
     have_3 = swap_in_pair(have_1)
-    have_2 = shift_between_pairs(have_3, 1)
+    have_2 = shift_between_pairs(have_1, -2)
     have_near = jnp.concatenate([mine, have_1])
     next_near, last_near = neighbours(have_near)
     next_near, have_2, have_3 = tie((next_near, have_2, have_3))

time: 123 us -> 120 us (0.976)
  waiting for transfers between devices: 55.7 us -> 51.5 us
  starting transfers between devices: 50.1 us -> 52.1 us
    ppermute x2, waiting for transfers between devices: 11.1 us -> 5.51 us  [swap_in_pair(): return lax.ppermute(value, 'z', [(i, i ^ 1) for i in range(NZ)])]
    ppermute x19, waiting for transfers between devices: 32.1 us -> 34.2 us  [shift_apart(): return lax.ppermute(value, (axis, 'core'), pairs)]
    ppermute x5, starting transfers between devices: 15.7 us -> 17.6 us  [shift_between_pairs(): lax.ppermute(value, 'z', [(i, (i + by * (2 * (i % 2) - 1)) % NZ) for i in...]
  transfers between devices with their start and end apart: 30 -> 30, of which waited for: 16 -> 15; matrix products, arithmetic and copies ran while one was open for 6% -> 7% of each run, Pallas kernels for 0% -> 0%
where the time goes in v4:
time: 120 us
  starting transfers between devices  52.1 us (43%)
  waiting for transfers between devices  51.5 us (43%)
  matrix products  10 us (8%)
  other arithmetic  3.05 us (3%)
  local copies, waits for them, and re-layouts  2.11 us (2%)
  between operations  1.35 us (1%)
    ppermute x19, waiting for transfers between devices, shift_apart(): return lax.ppermute(value, (axis, 'core'), pairs)  34.2 us
    ppermute x19, starting transfers between devices, shift_apart(): return lax.ppermute(value, (axis, 'core'), pairs)  30.2 us
    ppermute x5, starting transfers between devices, shift_between_pairs(): lax.ppermute(value, 'z', [(i, (i + by * (2 * (i % 2) - 1)) % NZ) for i in...  17.6 us
    ppermute x5, waiting for transfers between devices, shift_between_pairs(): lax.ppermute(value, 'z', [(i, (i + by * (2 * (i % 2) - 1)) % NZ) for i in...  9.1 us
    dot_general x7, matrix products, contract(): lax.dot_general(left, right, (((left_dim,), (right_dim,)), ((), ())), pre...  9.01 us
    ppermute x2, waiting for transfers between devices, swap_in_pair(): return lax.ppermute(value, 'z', [(i, i ^ 1) for i in range(NZ)])  5.51 us
    ppermute x2, starting transfers between devices, shift(): return lax.ppermute(value, axis, [(i, (i + by) % n) for i in range(n)])  3.97 us
  transfers between devices with their start and end apart: 30, of which 15 were waited for; matrix products, arithmetic and copies ran while one was open for 7% of the time, Pallas kernels for 0%

profile of v4, /device:TPU:24, one launch (start us, length us, event | category | flops | bytes accessed | tf_op | source)
XLA Modules:
  0.0 120.1 jit_solution(16492337513646659996)
XLA Ops:
  2.8 3.1 %collective-permute-start.2 = (bf16[4,16,768]{2,1,0:T(8,128)(2,1)S(1)}, bf16[4,16,768]{2,1,0:T(8,128)(2,1)S(1)}, u32[]{:S(2)}, u32[]{:S(2)}) collective-permute-start(bf16[4,16,768]{2,1,0:T(8,128)(2,1)S(1)} %pad_maximum_fusion.11), channel_id=1, source_target_pairs={{0,4},{2,6},{4,0},{6,2},{1,5},{3,7},{5,1},{7,3},{8,12},{10,14},{12... | collective-permute-start | bytes 294920 | tf_op jit(solution)/shard_map/ppermute | solution.py:28
  7.9 3.5 %collective-permute-done.1 = bf16[4,16,768]{2,1,0:T(8,128)(2,1)S(1)} collective-permute-done((bf16[4,16,768]{2,1,0:T(8,128)(2,1)S(1)}, bf16[4,16,768]{2,1,0:T(8,128)(2,1)S(1)}, u32[]{:S(2)}, u32[]{:S(2)}) %collective-permute-start.1) | collective-permute-done | bytes 98336 | tf_op jit(solution)/shard_map/ppermute | solution.py:38
  17.6 1.7 %collective-permute-start.14 = (bf16[32,3072]{1,0:T(8,128)(2,1)S(1)}, bf16[32,3072]{1,0:T(8,128)(2,1)S(1)}, u32[]{:S(2)}, u32[]{:S(2)}) collective-permute-start(bf16[32,3072]{1,0:T(8,128)(2,1)S(1)} %pad_maximum_fusion.9), channel_id=1, source_target_pairs={{0,24},{1,9},{8,0},{9,17},{16,8},{17,25},{24,16},{25,1},{2,26},{3,... | collective-permute-start | bytes 589832 | tf_op jit(solution)/shard_map/ppermute | solution.py:38
  19.3 3.5 %collective-permute-done.4 = bf16[32,3072]{1,0:T(8,128)(2,1)S(1)} collective-permute-done((bf16[32,3072]{1,0:T(8,128)(2,1)S(1)}, bf16[32,3072]{1,0:T(8,128)(2,1)S(1)}, u32[]{:S(2)}, u32[]{:S(2)}) %collective-permute-start.4) | collective-permute-done | bytes 196640 | tf_op jit(solution)/shard_map/ppermute | solution.py:38
  22.8 3.5 %collective-permute-start.5 = (bf16[64,3072]{1,0:T(8,128)(2,1)S(1)}, bf16[64,3072]{1,0:T(8,128)(2,1)S(1)}, u32[]{:S(2)}, u32[]{:S(2)}) collective-permute-start(bf16[64,3072]{1,0:T(8,128)(2,1)S(1)} %get-tuple-element.18), channel_id=1, source_target_pairs={{0,8},{1,25},{8,16},{9,1},{16,24},{17,9},{24,0},{25,17},{2,10},{3,... | collective-permute-start | bytes 1179656 | tf_op jit(solution)/shard_map/ppermute | solution.py:38
  26.4 2.0 %collective-permute-start.7 = (bf16[64,3072]{1,0:T(8,128)(2,1)S(1)}, bf16[64,3072]{1,0:T(8,128)(2,1)S(1)}, u32[]{:S(2)}, u32[]{:S(2)}) collective-permute-start(bf16[64,3072]{1,0:T(8,128)(2,1)S(1)} %get-tuple-element.19), channel_id=1, source_target_pairs={{0,24},{1,9},{8,0},{9,17},{16,8},{17,25},{24,16},{25,1},{2,26},{3,... | collective-permute-start | bytes 1179656 | tf_op jit(solution)/shard_map/ppermute | solution.py:38
  28.4 4.2 %collective-permute-done.5 = bf16[64,3072]{1,0:T(8,128)(2,1)S(1)} collective-permute-done((bf16[64,3072]{1,0:T(8,128)(2,1)S(1)}, bf16[64,3072]{1,0:T(8,128)(2,1)S(1)}, u32[]{:S(2)}, u32[]{:S(2)}) %collective-permute-start.5) | collective-permute-done | bytes 393248 | tf_op jit(solution)/shard_map/ppermute | solution.py:38
  32.7 3.8 %collective-permute-start.6 = (bf16[64,3072]{1,0:T(8,128)(2,1)S(1)}, bf16[64,3072]{1,0:T(8,128)(2,1)S(1)}, u32[]{:S(2)}, u32[]{:S(2)}) collective-permute-start(bf16[64,3072]{1,0:T(8,128)(2,1)S(1)} %fusion.2), channel_id=1, source_target_pairs={{0,8},{1,25},{8,16},{9,1},{16,24},{17,9},{24,0},{25,17},{2,10},{3,... | collective-permute-start | bytes 1179656 | tf_op jit(solution)/shard_map/ppermute | solution.py:38
  36.6 6.8 %collective-permute-start.15 = (bf16[32,3072]{1,0:T(8,128)(2,1)S(1)}, bf16[32,3072]{1,0:T(8,128)(2,1)S(1)}, u32[]{:S(2)}, u32[]{:S(2)}) collective-permute-start(bf16[32,3072]{1,0:T(8,128)(2,1)S(1)} %fusion.17), channel_id=1, source_target_pairs={{0,160},{32,128},{64,224},{96,192},{128,32},{160,0},{192,96},{224,... | collective-permute-start | bytes 589832 | tf_op jit(solution)/shard_map/ppermute | solution.py:42
  43.5 2.2 %collective-permute-start.8 = (bf16[32,3072]{1,0:T(8,128)(2,1)S(1)}, bf16[32,3072]{1,0:T(8,128)(2,1)S(1)}, u32[]{:S(2)}, u32[]{:S(2)}) collective-permute-start(bf16[32,3072]{1,0:T(8,128)(2,1)S(1)} %get-tuple-element.20), channel_id=1, source_target_pairs={{0,8},{1,25},{8,16},{9,1},{16,24},{17,9},{24,0},{25,17},{2,10},{3,... | collective-permute-start | bytes 589832 | tf_op jit(solution)/shard_map/ppermute | solution.py:38
  45.8 5.9 %collective-permute-start.12 = (bf16[32,3072]{1,0:T(8,128)(2,1)S(1)}, bf16[32,3072]{1,0:T(8,128)(2,1)S(1)}, u32[]{:S(2)}, u32[]{:S(2)}) collective-permute-start(bf16[32,3072]{1,0:T(8,128)(2,1)S(1)} %pad_maximum_fusion.8), channel_id=1, source_target_pairs={{0,224},{32,64},{64,32},{96,128},{128,96},{160,192},{192,160},{224... | collective-permute-start | bytes 589832 | tf_op jit(solution)/shard_map/ppermute | solution.py:42
  51.9 3.3 %collective-permute-start.9 = (bf16[32,3072]{1,0:T(8,128)(2,1)S(1)}, bf16[32,3072]{1,0:T(8,128)(2,1)S(1)}, u32[]{:S(2)}, u32[]{:S(2)}) collective-permute-start(bf16[32,3072]{1,0:T(8,128)(2,1)S(1)} %fusion.14), channel_id=1, source_target_pairs={{0,8},{1,25},{8,16},{9,1},{16,24},{17,9},{24,0},{25,17},{2,10},{3,... | collective-permute-start | bytes 589832 | tf_op jit(solution)/shard_map/ppermute | solution.py:38
  55.2 2.8 %collective-permute-done.12 = bf16[32,3072]{1,0:T(8,128)(2,1)S(1)} collective-permute-done((bf16[32,3072]{1,0:T(8,128)(2,1)S(1)}, bf16[32,3072]{1,0:T(8,128)(2,1)S(1)}, u32[]{:S(2)}, u32[]{:S(2)}) %collective-permute-start.12) | collective-permute-done | bytes 196640 | tf_op jit(solution)/shard_map/ppermute | solution.py:42
  60.0 5.5 %collective-permute-done.16 = bf16[32,3072]{1,0:T(8,128)(2,1)S(1)} collective-permute-done((bf16[32,3072]{1,0:T(8,128)(2,1)S(1)}, bf16[32,3072]{1,0:T(8,128)(2,1)S(1)}, u32[]{:S(2)}, u32[]{:S(2)}) %collective-permute-start.16) | collective-permute-done | bytes 196640 | tf_op jit(solution)/shard_map/ppermute | solution.py:46
  65.8 2.3 %collective-permute-start.17 = (bf16[32,3072]{1,0:T(8,128)(2,1)S(1)}, bf16[32,3072]{1,0:T(8,128)(2,1)S(1)}, u32[]{:S(2)}, u32[]{:S(2)}) collective-permute-start(bf16[32,3072]{1,0:T(8,128)(2,1)S(1)} %pad_maximum_fusion.10), channel_id=1, source_target_pairs={{0,224},{32,64},{64,32},{96,128},{128,96},{160,192},{192,160},{224... | collective-permute-start | bytes 589832 | tf_op jit(solution)/shard_map/ppermute | solution.py:42
  68.1 4.7 %collective-permute-done.17 = bf16[32,3072]{1,0:T(8,128)(2,1)S(1)} collective-permute-done((bf16[32,3072]{1,0:T(8,128)(2,1)S(1)}, bf16[32,3072]{1,0:T(8,128)(2,1)S(1)}, u32[]{:S(2)}, u32[]{:S(2)}) %collective-permute-start.17) | collective-permute-done | bytes 196640 | tf_op jit(solution)/shard_map/ppermute | solution.py:42
  73.0 2.4 %collective-permute-start.20 = (bf16[32,3072]{1,0:T(8,128)(2,1)S(1)}, bf16[32,3072]{1,0:T(8,128)(2,1)S(1)}, u32[]{:S(2)}, u32[]{:S(2)}) collective-permute-start(bf16[32,3072]{1,0:T(8,128)(2,1)S(1)} %collective-permute-done.17), channel_id=1, source_target_pairs={{0,64},{32,224},{64,128},{96,32},{128,192},{160,96},{192,0},{224,1... | collective-permute-start | bytes 589832 | tf_op jit(solution)/shard_map/ppermute | solution.py:42
  75.5 7.2 %collective-permute-start.18 = (bf16[64,3072]{1,0:T(8,128)(2,1)S(1)}, bf16[64,3072]{1,0:T(8,128)(2,1)S(1)}, u32[]{:S(2)}, u32[]{:S(2)}) collective-permute-start(bf16[64,3072]{1,0:T(8,128)(2,1)S(1)} %pad_maximum_fusion.3), channel_id=1, source_target_pairs={{0,8},{1,25},{8,16},{9,1},{16,24},{17,9},{24,0},{25,17},{2,10},{3,... | collective-permute-start | bytes 1179656 | tf_op jit(solution)/shard_map/ppermute | solution.py:38
  82.6 7.5 %collective-permute-done.19 = bf16[64,3072]{1,0:T(8,128)(2,1)S(1)} collective-permute-done((bf16[64,3072]{1,0:T(8,128)(2,1)S(1)}, bf16[64,3072]{1,0:T(8,128)(2,1)S(1)}, u32[]{:S(2)}, u32[]{:S(2)}) %collective-permute-start.19) | collective-permute-done | bytes 393248 | tf_op jit(solution)/shard_map/ppermute | solution.py:38
  94.0 5.6 %collective-permute-done.23 = bf16[64,3072]{1,0:T(8,128)(2,1)S(1)} collective-permute-done((bf16[64,3072]{1,0:T(8,128)(2,1)S(1)}, bf16[64,3072]{1,0:T(8,128)(2,1)S(1)}, u32[]{:S(2)}, u32[]{:S(2)}) %collective-permute-start.23) | collective-permute-done | bytes 393248 | tf_op jit(solution)/shard_map/ppermute | solution.py:38
  100.9 3.0 %collective-permute-done.22 = bf16[64,3072]{1,0:T(8,128)(2,1)S(1)} collective-permute-done((bf16[64,3072]{1,0:T(8,128)(2,1)S(1)}, bf16[64,3072]{1,0:T(8,128)(2,1)S(1)}, u32[]{:S(2)}, u32[]{:S(2)}) %collective-permute-start.22) | collective-permute-done | bytes 393248 | tf_op jit(solution)/shard_map/ppermute | solution.py:38
  103.9 4.8 %collective-permute-done.24 = bf16[64,3072]{1,0:T(8,128)(2,1)S(1)} collective-permute-done((bf16[64,3072]{1,0:T(8,128)(2,1)S(1)}, bf16[64,3072]{1,0:T(8,128)(2,1)S(1)}, u32[]{:S(2)}, u32[]{:S(2)}) %collective-permute-start.24) | collective-permute-done | bytes 393248 | tf_op jit(solution)/shard_map/ppermute | solution.py:38
  110.3 2.2 %add_convert_fusion.1 = bf16[384,3072]{1,0:T(8,128)(2,1)} fusion(f32[384,3072]{1,0:T(8,128)S(1)} %convolution_add_fusion.1, bf16[160,3072]{1,0:T(8,128)(2,1)S(1)} %get-tuple-element.60, bf16[160,768]{1,0:T(8,128)(2,1)S(1)} %get-tuple-element.75), kind=kOutput, calls=%fused_computation.1 | convolution fusion | flops 379846656 | bytes 8183808 | tf_op jit(solution)/shard_map/dot_general | solution.py:13
  114.8 2.4 %add_convert_fusion = bf16[3072,384]{1,0:T(8,128)(2,1)} fusion(f32[3072,384]{1,0:T(8,128)S(1)} %convolution_add_fusion, bf16[160,3072]{1,0:T(8,128)(2,1)S(1)} %get-tuple-element.59, bf16[160,768]{1,0:T(8,128)(2,1)S(1)} %get-tuple-element.75), kind=kOutput, calls=%fused_computation | convolution fusion | flops 379846656 | bytes 8183808 | tf_op jit(solution)/shard_map/dot_general | solution.py:13
  (130 shorter events, 24.9 us)
Async XLA Ops:
  2.8 8.7 %collective-permute-start.2 = (bf16[4,16,768]{2,1,0:T(8,128)(2,1)S(1)}, bf16[4,16,768]{2,1,0:T(8,128)(2,1)S(1)}, u32[]{:S(2)}, u32[]{:S(2)}) collective-permute-start(bf16[4,16,768]{2,1,0:T(8,128)(2,1)S(1)} %pad_maximum_fusion.11), channel_id=1, source_target_pairs={{0,4},{2,6},{4,0},{6,2},{1,5},{3,7},{5,1},{7,3},{8,12},{10,14},{12... | collective-permute-start | bytes 294920 | tf_op jit(solution)/shard_map/ppermute | solution.py:28
  7.1 5.8 %collective-permute-start.3 = (bf16[4,16,768]{2,1,0:T(8,128)(2,1)S(1)}, bf16[4,16,768]{2,1,0:T(8,128)(2,1)S(1)}, u32[]{:S(2)}, u32[]{:S(2)}) collective-permute-start(bf16[4,16,768]{2,1,0:T(8,128)(2,1)S(1)} %pad_maximum_fusion.11), channel_id=1, source_target_pairs={{0,2},{1,7},{2,4},{3,1},{4,6},{5,3},{6,0},{7,5},{8,10},{9,15},{10,... | collective-permute-start | bytes 294920 | tf_op jit(solution)/shard_map/ppermute | solution.py:38
  17.0 5.7 %collective-permute-start.4 = (bf16[32,3072]{1,0:T(8,128)(2,1)S(1)}, bf16[32,3072]{1,0:T(8,128)(2,1)S(1)}, u32[]{:S(2)}, u32[]{:S(2)}) collective-permute-start(bf16[32,3072]{1,0:T(8,128)(2,1)S(1)} %pad_maximum_fusion.4), channel_id=1, source_target_pairs={{0,8},{1,25},{8,16},{9,1},{16,24},{17,9},{24,0},{25,17},{2,10},{3,... | collective-permute-start | bytes 589832 | tf_op jit(solution)/shard_map/ppermute | solution.py:38
  17.6 18.9 %collective-permute-start.14 = (bf16[32,3072]{1,0:T(8,128)(2,1)S(1)}, bf16[32,3072]{1,0:T(8,128)(2,1)S(1)}, u32[]{:S(2)}, u32[]{:S(2)}) collective-permute-start(bf16[32,3072]{1,0:T(8,128)(2,1)S(1)} %pad_maximum_fusion.9), channel_id=1, source_target_pairs={{0,24},{1,9},{8,0},{9,17},{16,8},{17,25},{24,16},{25,1},{2,26},{3,... | collective-permute-start | bytes 589832 | tf_op jit(solution)/shard_map/ppermute | solution.py:38
  22.8 9.8 %collective-permute-start.5 = (bf16[64,3072]{1,0:T(8,128)(2,1)S(1)}, bf16[64,3072]{1,0:T(8,128)(2,1)S(1)}, u32[]{:S(2)}, u32[]{:S(2)}) collective-permute-start(bf16[64,3072]{1,0:T(8,128)(2,1)S(1)} %get-tuple-element.18), channel_id=1, source_target_pairs={{0,8},{1,25},{8,16},{9,1},{16,24},{17,9},{24,0},{25,17},{2,10},{3,... | collective-permute-start | bytes 1179656 | tf_op jit(solution)/shard_map/ppermute | solution.py:38
  26.3 10.2 %collective-permute-start.13 = (bf16[32,3072]{1,0:T(8,128)(2,1)S(1)}, bf16[32,3072]{1,0:T(8,128)(2,1)S(1)}, u32[]{:S(2)}, u32[]{:S(2)}) collective-permute-start(bf16[32,3072]{1,0:T(8,128)(2,1)S(1)} %fusion.15), channel_id=1, source_target_pairs={{0,8},{1,25},{8,16},{9,1},{16,24},{17,9},{24,0},{25,17},{2,10},{3,... | collective-permute-start | bytes 589832 | tf_op jit(solution)/shard_map/ppermute | solution.py:38
  26.4 17.0 %collective-permute-start.7 = (bf16[64,3072]{1,0:T(8,128)(2,1)S(1)}, bf16[64,3072]{1,0:T(8,128)(2,1)S(1)}, u32[]{:S(2)}, u32[]{:S(2)}) collective-permute-start(bf16[64,3072]{1,0:T(8,128)(2,1)S(1)} %get-tuple-element.19), channel_id=1, source_target_pairs={{0,24},{1,9},{8,0},{9,17},{16,8},{17,25},{24,16},{25,1},{2,26},{3,... | collective-permute-start | bytes 1179656 | tf_op jit(solution)/shard_map/ppermute | solution.py:38
  32.7 10.7 %collective-permute-start.6 = (bf16[64,3072]{1,0:T(8,128)(2,1)S(1)}, bf16[64,3072]{1,0:T(8,128)(2,1)S(1)}, u32[]{:S(2)}, u32[]{:S(2)}) collective-permute-start(bf16[64,3072]{1,0:T(8,128)(2,1)S(1)} %fusion.2), channel_id=1, source_target_pairs={{0,8},{1,25},{8,16},{9,1},{16,24},{17,9},{24,0},{25,17},{2,10},{3,... | collective-permute-start | bytes 1179656 | tf_op jit(solution)/shard_map/ppermute | solution.py:38
  36.6 18.6 %collective-permute-start.15 = (bf16[32,3072]{1,0:T(8,128)(2,1)S(1)}, bf16[32,3072]{1,0:T(8,128)(2,1)S(1)}, u32[]{:S(2)}, u32[]{:S(2)}) collective-permute-start(bf16[32,3072]{1,0:T(8,128)(2,1)S(1)} %fusion.17), channel_id=1, source_target_pairs={{0,160},{32,128},{64,224},{96,192},{128,32},{160,0},{192,96},{224,... | collective-permute-start | bytes 589832 | tf_op jit(solution)/shard_map/ppermute | solution.py:42
  43.5 8.3 %collective-permute-start.8 = (bf16[32,3072]{1,0:T(8,128)(2,1)S(1)}, bf16[32,3072]{1,0:T(8,128)(2,1)S(1)}, u32[]{:S(2)}, u32[]{:S(2)}) collective-permute-start(bf16[32,3072]{1,0:T(8,128)(2,1)S(1)} %get-tuple-element.20), channel_id=1, source_target_pairs={{0,8},{1,25},{8,16},{9,1},{16,24},{17,9},{24,0},{25,17},{2,10},{3,... | collective-permute-start | bytes 589832 | tf_op jit(solution)/shard_map/ppermute | solution.py:38
  45.7 13.9 %collective-permute-start.10 = (bf16[32,3072]{1,0:T(8,128)(2,1)S(1)}, bf16[32,3072]{1,0:T(8,128)(2,1)S(1)}, u32[]{:S(2)}, u32[]{:S(2)}) collective-permute-start(bf16[32,3072]{1,0:T(8,128)(2,1)S(1)} %get-tuple-element.21), channel_id=1, source_target_pairs={{0,24},{1,9},{8,0},{9,17},{16,8},{17,25},{24,16},{25,1},{2,26},{3,... | collective-permute-start | bytes 589832 | tf_op jit(solution)/shard_map/ppermute | solution.py:38
  45.8 12.2 %collective-permute-start.12 = (bf16[32,3072]{1,0:T(8,128)(2,1)S(1)}, bf16[32,3072]{1,0:T(8,128)(2,1)S(1)}, u32[]{:S(2)}, u32[]{:S(2)}) collective-permute-start(bf16[32,3072]{1,0:T(8,128)(2,1)S(1)} %pad_maximum_fusion.8), channel_id=1, source_target_pairs={{0,224},{32,64},{64,32},{96,128},{128,96},{160,192},{192,160},{224... | collective-permute-start | bytes 589832 | tf_op jit(solution)/shard_map/ppermute | solution.py:42
  51.7 7.9 %collective-permute-start.11 = (bf16[32,3072]{1,0:T(8,128)(2,1)S(1)}, bf16[32,3072]{1,0:T(8,128)(2,1)S(1)}, u32[]{:S(2)}, u32[]{:S(2)}) collective-permute-start(bf16[32,3072]{1,0:T(8,128)(2,1)S(1)} %pad_maximum_fusion.7), channel_id=1, source_target_pairs={{0,64},{32,224},{64,128},{96,32},{128,192},{160,96},{192,0},{224,1... | collective-permute-start | bytes 589832 | tf_op jit(solution)/shard_map/ppermute | solution.py:42
  51.9 7.8 %collective-permute-start.9 = (bf16[32,3072]{1,0:T(8,128)(2,1)S(1)}, bf16[32,3072]{1,0:T(8,128)(2,1)S(1)}, u32[]{:S(2)}, u32[]{:S(2)}) collective-permute-start(bf16[32,3072]{1,0:T(8,128)(2,1)S(1)} %fusion.14), channel_id=1, source_target_pairs={{0,8},{1,25},{8,16},{9,1},{16,24},{17,9},{24,0},{25,17},{2,10},{3,... | collective-permute-start | bytes 589832 | tf_op jit(solution)/shard_map/ppermute | solution.py:38
  59.8 5.8 %collective-permute-start.16 = (bf16[32,3072]{1,0:T(8,128)(2,1)S(1)}, bf16[32,3072]{1,0:T(8,128)(2,1)S(1)}, u32[]{:S(2)}, u32[]{:S(2)}) collective-permute-start(bf16[32,3072]{1,0:T(8,128)(2,1)S(1)} %fusion.47), channel_id=1, source_target_pairs={{0,32},{32,0},{64,96},{96,64},{128,160},{160,128},{192,224},{224,1... | collective-permute-start | bytes 589832 | tf_op jit(solution)/shard_map/ppermute | solution.py:46
  65.8 7.0 %collective-permute-start.17 = (bf16[32,3072]{1,0:T(8,128)(2,1)S(1)}, bf16[32,3072]{1,0:T(8,128)(2,1)S(1)}, u32[]{:S(2)}, u32[]{:S(2)}) collective-permute-start(bf16[32,3072]{1,0:T(8,128)(2,1)S(1)} %pad_maximum_fusion.10), channel_id=1, source_target_pairs={{0,224},{32,64},{64,32},{96,128},{128,96},{160,192},{192,160},{224... | collective-permute-start | bytes 589832 | tf_op jit(solution)/shard_map/ppermute | solution.py:42
  72.8 17.3 %collective-permute-start.19 = (bf16[64,3072]{1,0:T(8,128)(2,1)S(1)}, bf16[64,3072]{1,0:T(8,128)(2,1)S(1)}, u32[]{:S(2)}, u32[]{:S(2)}) collective-permute-start(bf16[64,3072]{1,0:T(8,128)(2,1)S(1)} %pad_maximum_fusion.3), channel_id=1, source_target_pairs={{0,24},{1,9},{8,0},{9,17},{16,8},{17,25},{24,16},{25,1},{2,26},{3,... | collective-permute-start | bytes 1179656 | tf_op jit(solution)/shard_map/ppermute | solution.py:38
  72.9 9.7 %collective-permute-start.21 = (bf16[32,3072]{1,0:T(8,128)(2,1)S(1)}, bf16[32,3072]{1,0:T(8,128)(2,1)S(1)}, u32[]{:S(2)}, u32[]{:S(2)}) collective-permute-start(bf16[32,3072]{1,0:T(8,128)(2,1)S(1)} %collective-permute-done.17), channel_id=1, source_target_pairs={{0,32},{32,0},{64,96},{96,64},{128,160},{160,128},{192,224},{224,1... | collective-permute-start | bytes 589832 | tf_op jit(solution)/shard_map/ppermute | solution.py:46
  73.0 9.6 %collective-permute-start.20 = (bf16[32,3072]{1,0:T(8,128)(2,1)S(1)}, bf16[32,3072]{1,0:T(8,128)(2,1)S(1)}, u32[]{:S(2)}, u32[]{:S(2)}) collective-permute-start(bf16[32,3072]{1,0:T(8,128)(2,1)S(1)} %collective-permute-done.17), channel_id=1, source_target_pairs={{0,64},{32,224},{64,128},{96,32},{128,192},{160,96},{192,0},{224,1... | collective-permute-start | bytes 589832 | tf_op jit(solution)/shard_map/ppermute | solution.py:42
  75.5 16.8 %collective-permute-start.18 = (bf16[64,3072]{1,0:T(8,128)(2,1)S(1)}, bf16[64,3072]{1,0:T(8,128)(2,1)S(1)}, u32[]{:S(2)}, u32[]{:S(2)}) collective-permute-start(bf16[64,3072]{1,0:T(8,128)(2,1)S(1)} %pad_maximum_fusion.3), channel_id=1, source_target_pairs={{0,8},{1,25},{8,16},{9,1},{16,24},{17,9},{24,0},{25,17},{2,10},{3,... | collective-permute-start | bytes 1179656 | tf_op jit(solution)/shard_map/ppermute | solution.py:38
  90.1 18.6 %collective-permute-start.25 = (bf16[64,3072]{1,0:T(8,128)(2,1)S(1)}, bf16[64,3072]{1,0:T(8,128)(2,1)S(1)}, u32[]{:S(2)}, u32[]{:S(2)}) collective-permute-start(bf16[64,3072]{1,0:T(8,128)(2,1)S(1)} %constant_dynamic-update-slice_fusion.14), channel_id=1, source_target_pairs={{0,8},{1,25},{8,16},{9,1},{16,24},{17,9},{24,0},{25,17},{2,10},{3,... | collective-permute-start | bytes 1179656 | tf_op jit(solution)/shard_map/ppermute | solution.py:38
  90.7 9.0 %collective-permute-start.23 = (bf16[64,3072]{1,0:T(8,128)(2,1)S(1)}, bf16[64,3072]{1,0:T(8,128)(2,1)S(1)}, u32[]{:S(2)}, u32[]{:S(2)}) collective-permute-start(bf16[64,3072]{1,0:T(8,128)(2,1)S(1)} %constant_dynamic-update-slice_fusion.14), channel_id=1, source_target_pairs={{0,24},{1,9},{8,0},{9,17},{16,8},{17,25},{24,16},{25,1},{2,26},{3,... | collective-permute-start | bytes 1179656 | tf_op jit(solution)/shard_map/ppermute | solution.py:38
  92.2 11.6 %collective-permute-start.22 = (bf16[64,3072]{1,0:T(8,128)(2,1)S(1)}, bf16[64,3072]{1,0:T(8,128)(2,1)S(1)}, u32[]{:S(2)}, u32[]{:S(2)}) collective-permute-start(bf16[64,3072]{1,0:T(8,128)(2,1)S(1)} %collective-permute-done.19), channel_id=1, source_target_pairs={{0,24},{1,9},{8,0},{9,17},{16,8},{17,25},{24,16},{25,1},{2,26},{3,... | collective-permute-start | bytes 1179656 | tf_op jit(solution)/shard_map/ppermute | solution.py:38
  99.7 9.0 %collective-permute-start.24 = (bf16[64,3072]{1,0:T(8,128)(2,1)S(1)}, bf16[64,3072]{1,0:T(8,128)(2,1)S(1)}, u32[]{:S(2)}, u32[]{:S(2)}) collective-permute-start(bf16[64,3072]{1,0:T(8,128)(2,1)S(1)} %collective-permute-done.23), channel_id=1, source_target_pairs={{0,24},{1,9},{8,0},{9,17},{16,8},{17,25},{24,16},{25,1},{2,26},{3,... | collective-permute-start | bytes 1179656 | tf_op jit(solution)/shard_map/ppermute | solution.py:38
  (8 other events, 41.7 us)

commit v5 on v4

--- a/solution.py
+++ b/solution.py
@@ -106,7 +106,7 @@
 
     far, mid, own = parts_of(0, 1), parts_of(1, 3), parts_of(3, 4)
     relay, last_far = first_hops(far)
-    message, mid[2], mid[3] = tie((second_message(far, relay), mid[2], mid[3]))
+    message = second_message(far, relay)
     sum_far = finish(far, message, last_far).astype(BF16)
     relay, last_mid = first_hops(mid)
     message = second_message(mid, relay)
@@ -134,7 +134,6 @@
     have_2 = shift_between_pairs(have_1, -2)
     have_near = jnp.concatenate([mine, have_1])
     next_near, last_near = neighbours(have_near)
-    next_near, have_2, have_3 = tie((next_near, have_2, have_3))
     relay_near = shift_apart(next_near, "y", -1)
     have_far = jnp.concatenate([have_3, have_2])
     next_far, last_far = neighbours(have_far)

time: 120 us -> 117 us (0.975)
  waiting for transfers between devices: 51.5 us -> 46.7 us
  starting transfers between devices: 52.1 us -> 53.8 us
    ppermute x19, waiting for transfers between devices: 34.2 us -> 23.8 us  [shift_apart(): return lax.ppermute(value, (axis, 'core'), pairs)]
    ppermute x5, waiting for transfers between devices: 9.1 us -> 13.9 us  [shift_between_pairs(): lax.ppermute(value, 'z', [(i, (i + by * (2 * (i % 2) - 1)) % NZ) for i in...]
    ppermute x2, starting transfers between devices: 0.34 us -> 2.37 us  [swap_in_pair(): return lax.ppermute(value, 'z', [(i, i ^ 1) for i in range(NZ)])]
  transfers between devices with their start and end apart: 30 -> 30, of which waited for: 15 -> 16; matrix products, arithmetic and copies ran while one was open for 7% -> 7% of each run, Pallas kernels for 0% -> 0%
where the time goes in v5:
time: 117 us
  starting transfers between devices  53.8 us (46%)
  waiting for transfers between devices  46.7 us (40%)
  matrix products  10 us (9%)
  other arithmetic  3.08 us (3%)
  local copies, waits for them, and re-layouts  2.12 us (2%)
  between operations  1.36 us (1%)
    ppermute x19, starting transfers between devices, shift_apart(): return lax.ppermute(value, (axis, 'core'), pairs)  29.8 us
    ppermute x19, waiting for transfers between devices, shift_apart(): return lax.ppermute(value, (axis, 'core'), pairs)  23.8 us
    ppermute x5, starting transfers between devices, shift_between_pairs(): lax.ppermute(value, 'z', [(i, (i + by * (2 * (i % 2) - 1)) % NZ) for i in...  17.6 us
    ppermute x5, waiting for transfers between devices, shift_between_pairs(): lax.ppermute(value, 'z', [(i, (i + by * (2 * (i % 2) - 1)) % NZ) for i in...  13.9 us
    dot_general x7, matrix products, contract(): lax.dot_general(left, right, (((left_dim,), (right_dim,)), ((), ())), pre...  9.02 us
    ppermute x2, waiting for transfers between devices, swap_in_pair(): return lax.ppermute(value, 'z', [(i, i ^ 1) for i in range(NZ)])  5.53 us
    ppermute x2, starting transfers between devices, shift(): return lax.ppermute(value, axis, [(i, (i + by) % n) for i in range(n)])  3.93 us
    ppermute x2, starting transfers between devices, swap_in_pair(): return lax.ppermute(value, 'z', [(i, i ^ 1) for i in range(NZ)])  2.37 us
  transfers between devices with their start and end apart: 30, of which 16 were waited for; matrix products, arithmetic and copies ran while one was open for 7% of the time, Pallas kernels for 0%

profile of v5, /device:TPU:24, one launch (start us, length us, event | category | flops | bytes accessed | tf_op | source)
XLA Modules:
  0.0 117.1 jit_solution(7419207816201329829)
XLA Ops:
  2.8 3.1 %collective-permute-start.2 = (bf16[4,16,768]{2,1,0:T(8,128)(2,1)S(1)}, bf16[4,16,768]{2,1,0:T(8,128)(2,1)S(1)}, u32[]{:S(2)}, u32[]{:S(2)}) collective-permute-start(bf16[4,16,768]{2,1,0:T(8,128)(2,1)S(1)} %pad_maximum_fusion.11), channel_id=1, source_target_pairs={{0,4},{2,6},{4,0},{6,2},{1,5},{3,7},{5,1},{7,3},{8,12},{10,14},{12... | collective-permute-start | bytes 294920 | tf_op jit(solution)/shard_map/ppermute | solution.py:28
  7.9 3.5 %collective-permute-done.1 = bf16[4,16,768]{2,1,0:T(8,128)(2,1)S(1)} collective-permute-done((bf16[4,16,768]{2,1,0:T(8,128)(2,1)S(1)}, bf16[4,16,768]{2,1,0:T(8,128)(2,1)S(1)}, u32[]{:S(2)}, u32[]{:S(2)}) %collective-permute-start.1) | collective-permute-done | bytes 98336 | tf_op jit(solution)/shard_map/ppermute | solution.py:38
  20.1 2.6 %collective-permute-start.4 = (bf16[64,3072]{1,0:T(8,128)(2,1)S(1)}, bf16[64,3072]{1,0:T(8,128)(2,1)S(1)}, u32[]{:S(2)}, u32[]{:S(2)}) collective-permute-start(bf16[64,3072]{1,0:T(8,128)(2,1)S(1)} %pad_maximum_fusion.1), channel_id=1, source_target_pairs={{0,8},{1,25},{8,16},{9,1},{16,24},{17,9},{24,0},{25,17},{2,10},{3,... | collective-permute-start | bytes 1179656 | tf_op jit(solution)/shard_map/ppermute | solution.py:38
  22.8 2.1 %collective-permute-done.12 = bf16[32,3072]{1,0:T(8,128)(2,1)S(1)} collective-permute-done((bf16[32,3072]{1,0:T(8,128)(2,1)S(1)}, bf16[32,3072]{1,0:T(8,128)(2,1)S(1)}, u32[]{:S(2)}, u32[]{:S(2)}) %collective-permute-start.12) | collective-permute-done | bytes 196640 | tf_op jit(solution)/shard_map/ppermute | solution.py:38
  26.6 4.5 %collective-permute-done.4 = bf16[64,3072]{1,0:T(8,128)(2,1)S(1)} collective-permute-done((bf16[64,3072]{1,0:T(8,128)(2,1)S(1)}, bf16[64,3072]{1,0:T(8,128)(2,1)S(1)}, u32[]{:S(2)}, u32[]{:S(2)}) %collective-permute-start.4) | collective-permute-done | bytes 393248 | tf_op jit(solution)/shard_map/ppermute | solution.py:38
  31.2 3.6 %collective-permute-start.5 = (bf16[64,3072]{1,0:T(8,128)(2,1)S(1)}, bf16[64,3072]{1,0:T(8,128)(2,1)S(1)}, u32[]{:S(2)}, u32[]{:S(2)}) collective-permute-start(bf16[64,3072]{1,0:T(8,128)(2,1)S(1)} %fusion.2), channel_id=1, source_target_pairs={{0,8},{1,25},{8,16},{9,1},{16,24},{17,9},{24,0},{25,17},{2,10},{3,... | collective-permute-start | bytes 1179656 | tf_op jit(solution)/shard_map/ppermute | solution.py:38
  34.9 6.8 %collective-permute-start.15 = (bf16[32,3072]{1,0:T(8,128)(2,1)S(1)}, bf16[32,3072]{1,0:T(8,128)(2,1)S(1)}, u32[]{:S(2)}, u32[]{:S(2)}) collective-permute-start(bf16[32,3072]{1,0:T(8,128)(2,1)S(1)} %fusion.16), channel_id=1, source_target_pairs={{0,160},{32,128},{64,224},{96,192},{128,32},{160,0},{192,96},{224,... | collective-permute-start | bytes 589832 | tf_op jit(solution)/shard_map/ppermute | solution.py:42
  41.9 2.1 %collective-permute-start.7 = (bf16[32,3072]{1,0:T(8,128)(2,1)S(1)}, bf16[32,3072]{1,0:T(8,128)(2,1)S(1)}, u32[]{:S(2)}, u32[]{:S(2)}) collective-permute-start(bf16[32,3072]{1,0:T(8,128)(2,1)S(1)} %get-tuple-element.12), channel_id=1, source_target_pairs={{0,8},{1,25},{8,16},{9,1},{16,24},{17,9},{24,0},{25,17},{2,10},{3,... | collective-permute-start | bytes 589832 | tf_op jit(solution)/shard_map/ppermute | solution.py:38
  44.1 5.9 %collective-permute-start.11 = (bf16[32,3072]{1,0:T(8,128)(2,1)S(1)}, bf16[32,3072]{1,0:T(8,128)(2,1)S(1)}, u32[]{:S(2)}, u32[]{:S(2)}) collective-permute-start(bf16[32,3072]{1,0:T(8,128)(2,1)S(1)} %pad_maximum_fusion.7), channel_id=1, source_target_pairs={{0,224},{32,64},{64,32},{96,128},{128,96},{160,192},{192,160},{224... | collective-permute-start | bytes 589832 | tf_op jit(solution)/shard_map/ppermute | solution.py:42
  50.2 3.3 %collective-permute-start.8 = (bf16[32,3072]{1,0:T(8,128)(2,1)S(1)}, bf16[32,3072]{1,0:T(8,128)(2,1)S(1)}, u32[]{:S(2)}, u32[]{:S(2)}) collective-permute-start(bf16[32,3072]{1,0:T(8,128)(2,1)S(1)} %fusion.14), channel_id=1, source_target_pairs={{0,8},{1,25},{8,16},{9,1},{16,24},{17,9},{24,0},{25,17},{2,10},{3,... | collective-permute-start | bytes 589832 | tf_op jit(solution)/shard_map/ppermute | solution.py:38
  55.1 3.2 %collective-permute-done.11 = bf16[32,3072]{1,0:T(8,128)(2,1)S(1)} collective-permute-done((bf16[32,3072]{1,0:T(8,128)(2,1)S(1)}, bf16[32,3072]{1,0:T(8,128)(2,1)S(1)}, u32[]{:S(2)}, u32[]{:S(2)}) %collective-permute-start.11) | collective-permute-done | bytes 196640 | tf_op jit(solution)/shard_map/ppermute | solution.py:42
  58.5 1.8 %collective-permute-start.16 = (bf16[32,3072]{1,0:T(8,128)(2,1)S(1)}, bf16[32,3072]{1,0:T(8,128)(2,1)S(1)}, u32[]{:S(2)}, u32[]{:S(2)}) collective-permute-start(bf16[32,3072]{1,0:T(8,128)(2,1)S(1)} %fusion.47), channel_id=1, source_target_pairs={{0,32},{32,0},{64,96},{96,64},{128,160},{160,128},{192,224},{224,1... | collective-permute-start | bytes 589832 | tf_op jit(solution)/shard_map/ppermute | solution.py:46
  60.3 4.7 %collective-permute-done.16 = bf16[32,3072]{1,0:T(8,128)(2,1)S(1)} collective-permute-done((bf16[32,3072]{1,0:T(8,128)(2,1)S(1)}, bf16[32,3072]{1,0:T(8,128)(2,1)S(1)}, u32[]{:S(2)}, u32[]{:S(2)}) %collective-permute-start.16) | collective-permute-done | bytes 196640 | tf_op jit(solution)/shard_map/ppermute | solution.py:46
  65.3 3.0 %collective-permute-start.17 = (bf16[32,3072]{1,0:T(8,128)(2,1)S(1)}, bf16[32,3072]{1,0:T(8,128)(2,1)S(1)}, u32[]{:S(2)}, u32[]{:S(2)}) collective-permute-start(bf16[32,3072]{1,0:T(8,128)(2,1)S(1)} %pad_maximum_fusion.10), channel_id=1, source_target_pairs={{0,224},{32,64},{64,32},{96,128},{128,96},{160,192},{192,160},{224... | collective-permute-start | bytes 589832 | tf_op jit(solution)/shard_map/ppermute | solution.py:42
  68.4 3.9 %collective-permute-done.17 = bf16[32,3072]{1,0:T(8,128)(2,1)S(1)} collective-permute-done((bf16[32,3072]{1,0:T(8,128)(2,1)S(1)}, bf16[32,3072]{1,0:T(8,128)(2,1)S(1)}, u32[]{:S(2)}, u32[]{:S(2)}) %collective-permute-start.17) | collective-permute-done | bytes 196640 | tf_op jit(solution)/shard_map/ppermute | solution.py:42
  73.9 2.3 %collective-permute-start.18 = (bf16[64,3072]{1,0:T(8,128)(2,1)S(1)}, bf16[64,3072]{1,0:T(8,128)(2,1)S(1)}, u32[]{:S(2)}, u32[]{:S(2)}) collective-permute-start(bf16[64,3072]{1,0:T(8,128)(2,1)S(1)} %pad_maximum_fusion.3), channel_id=1, source_target_pairs={{0,8},{1,25},{8,16},{9,1},{16,24},{17,9},{24,0},{25,17},{2,10},{3,... | collective-permute-start | bytes 1179656 | tf_op jit(solution)/shard_map/ppermute | solution.py:38
  78.7 5.2 %collective-permute-done.22 = bf16[32,3072]{1,0:T(8,128)(2,1)S(1)} collective-permute-done((bf16[32,3072]{1,0:T(8,128)(2,1)S(1)}, bf16[32,3072]{1,0:T(8,128)(2,1)S(1)}, u32[]{:S(2)}, u32[]{:S(2)}) %collective-permute-start.22) | collective-permute-done | bytes 196640 | tf_op jit(solution)/shard_map/ppermute | solution.py:42
  89.6 4.0 %collective-permute-done.23 = bf16[64,3072]{1,0:T(8,128)(2,1)S(1)} collective-permute-done((bf16[64,3072]{1,0:T(8,128)(2,1)S(1)}, bf16[64,3072]{1,0:T(8,128)(2,1)S(1)}, u32[]{:S(2)}, u32[]{:S(2)}) %collective-permute-start.23) | collective-permute-done | bytes 393248 | tf_op jit(solution)/shard_map/ppermute | solution.py:38
  94.9 2.9 %collective-permute-done.20 = bf16[64,3072]{1,0:T(8,128)(2,1)S(1)} collective-permute-done((bf16[64,3072]{1,0:T(8,128)(2,1)S(1)}, bf16[64,3072]{1,0:T(8,128)(2,1)S(1)}, u32[]{:S(2)}, u32[]{:S(2)}) %collective-permute-start.20) | collective-permute-done | bytes 393248 | tf_op jit(solution)/shard_map/ppermute | solution.py:38
  97.8 4.8 %collective-permute-done.24 = bf16[64,3072]{1,0:T(8,128)(2,1)S(1)} collective-permute-done((bf16[64,3072]{1,0:T(8,128)(2,1)S(1)}, bf16[64,3072]{1,0:T(8,128)(2,1)S(1)}, u32[]{:S(2)}, u32[]{:S(2)}) %collective-permute-start.24) | collective-permute-done | bytes 393248 | tf_op jit(solution)/shard_map/ppermute | solution.py:38
  104.3 2.2 %add_convert_fusion.1 = bf16[384,3072]{1,0:T(8,128)(2,1)} fusion(f32[384,3072]{1,0:T(8,128)S(1)} %convolution_add_fusion.1, bf16[160,3072]{1,0:T(8,128)(2,1)S(1)} %get-tuple-element.48, bf16[160,768]{1,0:T(8,128)(2,1)S(1)} %get-tuple-element.63), kind=kOutput, calls=%fused_computation.1 | convolution fusion | flops 379846656 | bytes 8183808 | tf_op jit(solution)/shard_map/dot_general | solution.py:13
  106.5 3.8 %collective-permute-start.29 = (f32[2,16,384]{2,1,0:T(8,128)S(1)}, f32[2,16,384]{2,1,0:T(8,128)S(1)}, u32[]{:S(2)}, u32[]{:S(2)}) collective-permute-start(f32[2,16,384]{2,1,0:T(8,128)S(1)} %fusion.39), channel_id=1, source_target_pairs={{0,6},{1,3},{2,0},{3,5},{4,2},{5,7},{6,4},{7,1},{8,14},{9,11},{10,... | collective-permute-start | bytes 147464 | tf_op jit(solution)/shard_map/ppermute | solution.py:38
  111.3 2.4 %add_convert_fusion = bf16[3072,384]{1,0:T(8,128)(2,1)} fusion(f32[3072,384]{1,0:T(8,128)S(1)} %convolution_add_fusion, bf16[160,3072]{1,0:T(8,128)(2,1)S(1)} %get-tuple-element.47, bf16[160,768]{1,0:T(8,128)(2,1)S(1)} %get-tuple-element.63), kind=kOutput, calls=%fused_computation | convolution fusion | flops 379846656 | bytes 8183808 | tf_op jit(solution)/shard_map/dot_general | solution.py:13
  113.7 2.3 %collective-permute-done.27 = f32[2,16,384]{2,1,0:T(8,128)S(1)} collective-permute-done((f32[2,16,384]{2,1,0:T(8,128)S(1)}, f32[2,16,384]{2,1,0:T(8,128)S(1)}, u32[]{:S(2)}, u32[]{:S(2)}) %collective-permute-start.27) | collective-permute-done | bytes 49184 | tf_op jit(solution)/shard_map/ppermute | solution.py:28
  (130 shorter events, 31.5 us)
Async XLA Ops:
  2.8 8.7 %collective-permute-start.2 = (bf16[4,16,768]{2,1,0:T(8,128)(2,1)S(1)}, bf16[4,16,768]{2,1,0:T(8,128)(2,1)S(1)}, u32[]{:S(2)}, u32[]{:S(2)}) collective-permute-start(bf16[4,16,768]{2,1,0:T(8,128)(2,1)S(1)} %pad_maximum_fusion.11), channel_id=1, source_target_pairs={{0,4},{2,6},{4,0},{6,2},{1,5},{3,7},{5,1},{7,3},{8,12},{10,14},{12... | collective-permute-start | bytes 294920 | tf_op jit(solution)/shard_map/ppermute | solution.py:28
  17.1 7.9 %collective-permute-start.12 = (bf16[32,3072]{1,0:T(8,128)(2,1)S(1)}, bf16[32,3072]{1,0:T(8,128)(2,1)S(1)}, u32[]{:S(2)}, u32[]{:S(2)}) collective-permute-start(bf16[32,3072]{1,0:T(8,128)(2,1)S(1)} %pad_maximum_fusion.8), channel_id=1, source_target_pairs={{0,8},{1,25},{8,16},{9,1},{16,24},{17,9},{24,0},{25,17},{2,10},{3,... | collective-permute-start | bytes 589832 | tf_op jit(solution)/shard_map/ppermute | solution.py:38
  17.6 17.2 %collective-permute-start.14 = (bf16[32,3072]{1,0:T(8,128)(2,1)S(1)}, bf16[32,3072]{1,0:T(8,128)(2,1)S(1)}, u32[]{:S(2)}, u32[]{:S(2)}) collective-permute-start(bf16[32,3072]{1,0:T(8,128)(2,1)S(1)} %pad_maximum_fusion.9), channel_id=1, source_target_pairs={{0,24},{1,9},{8,0},{9,17},{16,8},{17,25},{24,16},{25,1},{2,26},{3,... | collective-permute-start | bytes 589832 | tf_op jit(solution)/shard_map/ppermute | solution.py:38
  19.3 22.4 %collective-permute-start.6 = (bf16[64,3072]{1,0:T(8,128)(2,1)S(1)}, bf16[64,3072]{1,0:T(8,128)(2,1)S(1)}, u32[]{:S(2)}, u32[]{:S(2)}) collective-permute-start(bf16[64,3072]{1,0:T(8,128)(2,1)S(1)} %pad_maximum_fusion.2), channel_id=1, source_target_pairs={{0,24},{1,9},{8,0},{9,17},{16,8},{17,25},{24,16},{25,1},{2,26},{3,... | collective-permute-start | bytes 1179656 | tf_op jit(solution)/shard_map/ppermute | solution.py:38
  20.1 11.0 %collective-permute-start.4 = (bf16[64,3072]{1,0:T(8,128)(2,1)S(1)}, bf16[64,3072]{1,0:T(8,128)(2,1)S(1)}, u32[]{:S(2)}, u32[]{:S(2)}) collective-permute-start(bf16[64,3072]{1,0:T(8,128)(2,1)S(1)} %pad_maximum_fusion.1), channel_id=1, source_target_pairs={{0,8},{1,25},{8,16},{9,1},{16,24},{17,9},{24,0},{25,17},{2,10},{3,... | collective-permute-start | bytes 1179656 | tf_op jit(solution)/shard_map/ppermute | solution.py:38
  25.0 9.8 %collective-permute-start.13 = (bf16[32,3072]{1,0:T(8,128)(2,1)S(1)}, bf16[32,3072]{1,0:T(8,128)(2,1)S(1)}, u32[]{:S(2)}, u32[]{:S(2)}) collective-permute-start(bf16[32,3072]{1,0:T(8,128)(2,1)S(1)} %fusion.17), channel_id=1, source_target_pairs={{0,8},{1,25},{8,16},{9,1},{16,24},{17,9},{24,0},{25,17},{2,10},{3,... | collective-permute-start | bytes 589832 | tf_op jit(solution)/shard_map/ppermute | solution.py:38
  31.2 10.5 %collective-permute-start.5 = (bf16[64,3072]{1,0:T(8,128)(2,1)S(1)}, bf16[64,3072]{1,0:T(8,128)(2,1)S(1)}, u32[]{:S(2)}, u32[]{:S(2)}) collective-permute-start(bf16[64,3072]{1,0:T(8,128)(2,1)S(1)} %fusion.2), channel_id=1, source_target_pairs={{0,8},{1,25},{8,16},{9,1},{16,24},{17,9},{24,0},{25,17},{2,10},{3,... | collective-permute-start | bytes 1179656 | tf_op jit(solution)/shard_map/ppermute | solution.py:38
  34.9 20.2 %collective-permute-start.15 = (bf16[32,3072]{1,0:T(8,128)(2,1)S(1)}, bf16[32,3072]{1,0:T(8,128)(2,1)S(1)}, u32[]{:S(2)}, u32[]{:S(2)}) collective-permute-start(bf16[32,3072]{1,0:T(8,128)(2,1)S(1)} %fusion.16), channel_id=1, source_target_pairs={{0,160},{32,128},{64,224},{96,192},{128,32},{160,0},{192,96},{224,... | collective-permute-start | bytes 589832 | tf_op jit(solution)/shard_map/ppermute | solution.py:42
  41.9 8.2 %collective-permute-start.7 = (bf16[32,3072]{1,0:T(8,128)(2,1)S(1)}, bf16[32,3072]{1,0:T(8,128)(2,1)S(1)}, u32[]{:S(2)}, u32[]{:S(2)}) collective-permute-start(bf16[32,3072]{1,0:T(8,128)(2,1)S(1)} %get-tuple-element.12), channel_id=1, source_target_pairs={{0,8},{1,25},{8,16},{9,1},{16,24},{17,9},{24,0},{25,17},{2,10},{3,... | collective-permute-start | bytes 589832 | tf_op jit(solution)/shard_map/ppermute | solution.py:38
  44.0 14.4 %collective-permute-start.9 = (bf16[32,3072]{1,0:T(8,128)(2,1)S(1)}, bf16[32,3072]{1,0:T(8,128)(2,1)S(1)}, u32[]{:S(2)}, u32[]{:S(2)}) collective-permute-start(bf16[32,3072]{1,0:T(8,128)(2,1)S(1)} %get-tuple-element.13), channel_id=1, source_target_pairs={{0,24},{1,9},{8,0},{9,17},{16,8},{17,25},{24,16},{25,1},{2,26},{3,... | collective-permute-start | bytes 589832 | tf_op jit(solution)/shard_map/ppermute | solution.py:38
  44.1 14.2 %collective-permute-start.11 = (bf16[32,3072]{1,0:T(8,128)(2,1)S(1)}, bf16[32,3072]{1,0:T(8,128)(2,1)S(1)}, u32[]{:S(2)}, u32[]{:S(2)}) collective-permute-start(bf16[32,3072]{1,0:T(8,128)(2,1)S(1)} %pad_maximum_fusion.7), channel_id=1, source_target_pairs={{0,224},{32,64},{64,32},{96,128},{128,96},{160,192},{192,160},{224... | collective-permute-start | bytes 589832 | tf_op jit(solution)/shard_map/ppermute | solution.py:42
  50.0 8.3 %collective-permute-start.10 = (bf16[32,3072]{1,0:T(8,128)(2,1)S(1)}, bf16[32,3072]{1,0:T(8,128)(2,1)S(1)}, u32[]{:S(2)}, u32[]{:S(2)}) collective-permute-start(bf16[32,3072]{1,0:T(8,128)(2,1)S(1)} %pad_maximum_fusion.6), channel_id=1, source_target_pairs={{0,64},{32,224},{64,128},{96,32},{128,192},{160,96},{192,0},{224,1... | collective-permute-start | bytes 589832 | tf_op jit(solution)/shard_map/ppermute | solution.py:42
  50.2 8.2 %collective-permute-start.8 = (bf16[32,3072]{1,0:T(8,128)(2,1)S(1)}, bf16[32,3072]{1,0:T(8,128)(2,1)S(1)}, u32[]{:S(2)}, u32[]{:S(2)}) collective-permute-start(bf16[32,3072]{1,0:T(8,128)(2,1)S(1)} %fusion.14), channel_id=1, source_target_pairs={{0,8},{1,25},{8,16},{9,1},{16,24},{17,9},{24,0},{25,17},{2,10},{3,... | collective-permute-start | bytes 589832 | tf_op jit(solution)/shard_map/ppermute | solution.py:38
  58.5 6.6 %collective-permute-start.16 = (bf16[32,3072]{1,0:T(8,128)(2,1)S(1)}, bf16[32,3072]{1,0:T(8,128)(2,1)S(1)}, u32[]{:S(2)}, u32[]{:S(2)}) collective-permute-start(bf16[32,3072]{1,0:T(8,128)(2,1)S(1)} %fusion.47), channel_id=1, source_target_pairs={{0,32},{32,0},{64,96},{96,64},{128,160},{160,128},{192,224},{224,1... | collective-permute-start | bytes 589832 | tf_op jit(solution)/shard_map/ppermute | solution.py:46
  65.3 7.0 %collective-permute-start.17 = (bf16[32,3072]{1,0:T(8,128)(2,1)S(1)}, bf16[32,3072]{1,0:T(8,128)(2,1)S(1)}, u32[]{:S(2)}, u32[]{:S(2)}) collective-permute-start(bf16[32,3072]{1,0:T(8,128)(2,1)S(1)} %pad_maximum_fusion.10), channel_id=1, source_target_pairs={{0,224},{32,64},{64,32},{96,128},{128,96},{160,192},{192,160},{224... | collective-permute-start | bytes 589832 | tf_op jit(solution)/shard_map/ppermute | solution.py:42
  72.3 6.4 %collective-permute-start.21 = (bf16[32,3072]{1,0:T(8,128)(2,1)S(1)}, bf16[32,3072]{1,0:T(8,128)(2,1)S(1)}, u32[]{:S(2)}, u32[]{:S(2)}) collective-permute-start(bf16[32,3072]{1,0:T(8,128)(2,1)S(1)} %collective-permute-done.17), channel_id=1, source_target_pairs={{0,32},{32,0},{64,96},{96,64},{128,160},{160,128},{192,224},{224,1... | collective-permute-start | bytes 589832 | tf_op jit(solution)/shard_map/ppermute | solution.py:46
  72.9 13.3 %collective-permute-start.19 = (bf16[64,3072]{1,0:T(8,128)(2,1)S(1)}, bf16[64,3072]{1,0:T(8,128)(2,1)S(1)}, u32[]{:S(2)}, u32[]{:S(2)}) collective-permute-start(bf16[64,3072]{1,0:T(8,128)(2,1)S(1)} %pad_maximum_fusion.3), channel_id=1, source_target_pairs={{0,24},{1,9},{8,0},{9,17},{16,8},{17,25},{24,16},{25,1},{2,26},{3,... | collective-permute-start | bytes 1179656 | tf_op jit(solution)/shard_map/ppermute | solution.py:38
  73.9 12.2 %collective-permute-start.18 = (bf16[64,3072]{1,0:T(8,128)(2,1)S(1)}, bf16[64,3072]{1,0:T(8,128)(2,1)S(1)}, u32[]{:S(2)}, u32[]{:S(2)}) collective-permute-start(bf16[64,3072]{1,0:T(8,128)(2,1)S(1)} %pad_maximum_fusion.3), channel_id=1, source_target_pairs={{0,8},{1,25},{8,16},{9,1},{16,24},{17,9},{24,0},{25,17},{2,10},{3,... | collective-permute-start | bytes 1179656 | tf_op jit(solution)/shard_map/ppermute | solution.py:38
  76.2 7.8 %collective-permute-start.22 = (bf16[32,3072]{1,0:T(8,128)(2,1)S(1)}, bf16[32,3072]{1,0:T(8,128)(2,1)S(1)}, u32[]{:S(2)}, u32[]{:S(2)}) collective-permute-start(bf16[32,3072]{1,0:T(8,128)(2,1)S(1)} %collective-permute-done.17), channel_id=1, source_target_pairs={{0,64},{32,224},{64,128},{96,32},{128,192},{160,96},{192,0},{224,1... | collective-permute-start | bytes 589832 | tf_op jit(solution)/shard_map/ppermute | solution.py:42
  84.0 18.7 %collective-permute-start.25 = (bf16[64,3072]{1,0:T(8,128)(2,1)S(1)}, bf16[64,3072]{1,0:T(8,128)(2,1)S(1)}, u32[]{:S(2)}, u32[]{:S(2)}) collective-permute-start(bf16[64,3072]{1,0:T(8,128)(2,1)S(1)} %constant_dynamic-update-slice_fusion.14), channel_id=1, source_target_pairs={{0,8},{1,25},{8,16},{9,1},{16,24},{17,9},{24,0},{25,17},{2,10},{3,... | collective-permute-start | bytes 1179656 | tf_op jit(solution)/shard_map/ppermute | solution.py:38
  84.6 9.0 %collective-permute-start.23 = (bf16[64,3072]{1,0:T(8,128)(2,1)S(1)}, bf16[64,3072]{1,0:T(8,128)(2,1)S(1)}, u32[]{:S(2)}, u32[]{:S(2)}) collective-permute-start(bf16[64,3072]{1,0:T(8,128)(2,1)S(1)} %constant_dynamic-update-slice_fusion.14), channel_id=1, source_target_pairs={{0,24},{1,9},{8,0},{9,17},{16,8},{17,25},{24,16},{25,1},{2,26},{3,... | collective-permute-start | bytes 1179656 | tf_op jit(solution)/shard_map/ppermute | solution.py:38
  87.8 10.0 %collective-permute-start.20 = (bf16[64,3072]{1,0:T(8,128)(2,1)S(1)}, bf16[64,3072]{1,0:T(8,128)(2,1)S(1)}, u32[]{:S(2)}, u32[]{:S(2)}) collective-permute-start(bf16[64,3072]{1,0:T(8,128)(2,1)S(1)} %collective-permute-done.19), channel_id=1, source_target_pairs={{0,24},{1,9},{8,0},{9,17},{16,8},{17,25},{24,16},{25,1},{2,26},{3,... | collective-permute-start | bytes 1179656 | tf_op jit(solution)/shard_map/ppermute | solution.py:38
  93.6 9.0 %collective-permute-start.24 = (bf16[64,3072]{1,0:T(8,128)(2,1)S(1)}, bf16[64,3072]{1,0:T(8,128)(2,1)S(1)}, u32[]{:S(2)}, u32[]{:S(2)}) collective-permute-start(bf16[64,3072]{1,0:T(8,128)(2,1)S(1)} %collective-permute-done.23), channel_id=1, source_target_pairs={{0,24},{1,9},{8,0},{9,17},{16,8},{17,25},{24,16},{25,1},{2,26},{3,... | collective-permute-start | bytes 1179656 | tf_op jit(solution)/shard_map/ppermute | solution.py:38
  106.5 7.2 %collective-permute-start.29 = (f32[2,16,384]{2,1,0:T(8,128)S(1)}, f32[2,16,384]{2,1,0:T(8,128)S(1)}, u32[]{:S(2)}, u32[]{:S(2)}) collective-permute-start(f32[2,16,384]{2,1,0:T(8,128)S(1)} %fusion.39), channel_id=1, source_target_pairs={{0,6},{1,3},{2,0},{3,5},{4,2},{5,7},{6,4},{7,1},{8,14},{9,11},{10,... | collective-permute-start | bytes 147464 | tf_op jit(solution)/shard_map/ppermute | solution.py:38
  (8 other events, 42.6 us)

commit v6 on v5

--- a/solution.py
+++ b/solution.py
@@ -111,14 +111,15 @@
     relay, last_mid = first_hops(mid)
     message = second_message(mid, relay)
     sum_mid = finish(mid, message, last_mid).astype(BF16)
-    sum_mid, own[2], own[3] = tie((sum_mid, own[2], own[3]))
+    sum_mid, own[2] = tie((sum_mid, own[2]))
 
     pre_1, pre_3, back_1, back_3 = split_rows(sum_mid, 4)
     from_z = shift_between_pairs(jnp.concatenate([pre_3, back_3]), -2).astype(F32)
     from_z = from_z + shift_between_pairs(jnp.concatenate([pre_1, back_1]), 1).astype(F32)
     from_z = tie(from_z + shift_between_pairs(sum_far, 3).astype(F32))
-    relay, last_own = first_hops(own)
-    total = finish(own, second_message(own, relay), last_own)
+    relay = shift_apart(own[2], "y", 1)
+    message, own[3] = tie((second_message(own, relay), own[3]))
+    total = finish(own, message, shift_apart(own[3], "y", -1))
     total = total + from_z
     total = total + swap_in_pair(total.astype(BF16)).astype(F32)
     pre_act, grad_hidden = total[:unit], total[unit:]

time: 117 us -> 117 us (level)
  starting transfers between devices: 53.8 us -> 52 us
  waiting for transfers between devices: 46.7 us -> 48.1 us
    ppermute x19, starting transfers between devices: 29.8 us -> 25.9 us  [shift_apart(): return lax.ppermute(value, (axis, 'core'), pairs)]
    ppermute x5, starting transfers between devices: 17.6 us -> 20.2 us  [shift_between_pairs(): lax.ppermute(value, 'z', [(i, (i + by * (2 * (i % 2) - 1)) % NZ) for i in...]
where the time goes in v6:
time: 117 us
  starting transfers between devices  52 us (44%)
  waiting for transfers between devices  48.1 us (41%)
  matrix products  10 us (9%)
  other arithmetic  3.09 us (3%)
  local copies, waits for them, and re-layouts  2.12 us (2%)
  between operations  1.38 us (1%)
    ppermute x19, starting transfers between devices, shift_apart(): return lax.ppermute(value, (axis, 'core'), pairs)  25.9 us
    ppermute x19, waiting for transfers between devices, shift_apart(): return lax.ppermute(value, (axis, 'core'), pairs)  24.7 us
    ppermute x5, starting transfers between devices, shift_between_pairs(): lax.ppermute(value, 'z', [(i, (i + by * (2 * (i % 2) - 1)) % NZ) for i in...  20.2 us
    ppermute x5, waiting for transfers between devices, shift_between_pairs(): lax.ppermute(value, 'z', [(i, (i + by * (2 * (i % 2) - 1)) % NZ) for i in...  15.1 us
    dot_general x7, matrix products, contract(): lax.dot_general(left, right, (((left_dim,), (right_dim,)), ((), ())), pre...  9.02 us
    ppermute x2, waiting for transfers between devices, swap_in_pair(): return lax.ppermute(value, 'z', [(i, i ^ 1) for i in range(NZ)])  4.86 us
    ppermute x2, starting transfers between devices, shift(): return lax.ppermute(value, axis, [(i, (i + by) % n) for i in range(n)])  3.95 us
  transfers between devices with their start and end apart: 30, of which 16 were waited for; matrix products, arithmetic and copies ran while one was open for 7% of the time, Pallas kernels for 0%

profile of v6, /device:TPU:24, one launch (start us, length us, event | category | flops | bytes accessed | tf_op | source)
XLA Modules:
  0.0 116.7 jit_solution(6376066997668664523)
XLA Ops:
  2.8 3.1 %collective-permute-start.2 = (bf16[4,16,768]{2,1,0:T(8,128)(2,1)S(1)}, bf16[4,16,768]{2,1,0:T(8,128)(2,1)S(1)}, u32[]{:S(2)}, u32[]{:S(2)}) collective-permute-start(bf16[4,16,768]{2,1,0:T(8,128)(2,1)S(1)} %pad_maximum_fusion.11), channel_id=1, source_target_pairs={{0,4},{2,6},{4,0},{6,2},{1,5},{3,7},{5,1},{7,3},{8,12},{10,14},{12... | collective-permute-start | bytes 294920 | tf_op jit(solution)/shard_map/ppermute | solution.py:28
  7.9 3.5 %collective-permute-done.1 = bf16[4,16,768]{2,1,0:T(8,128)(2,1)S(1)} collective-permute-done((bf16[4,16,768]{2,1,0:T(8,128)(2,1)S(1)}, bf16[4,16,768]{2,1,0:T(8,128)(2,1)S(1)}, u32[]{:S(2)}, u32[]{:S(2)}) %collective-permute-start.1) | collective-permute-done | bytes 98336 | tf_op jit(solution)/shard_map/ppermute | solution.py:38
  20.1 2.6 %collective-permute-start.4 = (bf16[64,3072]{1,0:T(8,128)(2,1)S(1)}, bf16[64,3072]{1,0:T(8,128)(2,1)S(1)}, u32[]{:S(2)}, u32[]{:S(2)}) collective-permute-start(bf16[64,3072]{1,0:T(8,128)(2,1)S(1)} %pad_maximum_fusion.1), channel_id=1, source_target_pairs={{0,8},{1,25},{8,16},{9,1},{16,24},{17,9},{24,0},{25,17},{2,10},{3,... | collective-permute-start | bytes 1179656 | tf_op jit(solution)/shard_map/ppermute | solution.py:38
  22.8 2.1 %collective-permute-done.12 = bf16[32,3072]{1,0:T(8,128)(2,1)S(1)} collective-permute-done((bf16[32,3072]{1,0:T(8,128)(2,1)S(1)}, bf16[32,3072]{1,0:T(8,128)(2,1)S(1)}, u32[]{:S(2)}, u32[]{:S(2)}) %collective-permute-start.12) | collective-permute-done | bytes 196640 | tf_op jit(solution)/shard_map/ppermute | solution.py:38
  26.6 4.5 %collective-permute-done.4 = bf16[64,3072]{1,0:T(8,128)(2,1)S(1)} collective-permute-done((bf16[64,3072]{1,0:T(8,128)(2,1)S(1)}, bf16[64,3072]{1,0:T(8,128)(2,1)S(1)}, u32[]{:S(2)}, u32[]{:S(2)}) %collective-permute-start.4) | collective-permute-done | bytes 393248 | tf_op jit(solution)/shard_map/ppermute | solution.py:38
  31.2 3.6 %collective-permute-start.5 = (bf16[64,3072]{1,0:T(8,128)(2,1)S(1)}, bf16[64,3072]{1,0:T(8,128)(2,1)S(1)}, u32[]{:S(2)}, u32[]{:S(2)}) collective-permute-start(bf16[64,3072]{1,0:T(8,128)(2,1)S(1)} %fusion.2), channel_id=1, source_target_pairs={{0,8},{1,25},{8,16},{9,1},{16,24},{17,9},{24,0},{25,17},{2,10},{3,... | collective-permute-start | bytes 1179656 | tf_op jit(solution)/shard_map/ppermute | solution.py:38
  34.9 6.8 %collective-permute-start.15 = (bf16[32,3072]{1,0:T(8,128)(2,1)S(1)}, bf16[32,3072]{1,0:T(8,128)(2,1)S(1)}, u32[]{:S(2)}, u32[]{:S(2)}) collective-permute-start(bf16[32,3072]{1,0:T(8,128)(2,1)S(1)} %fusion.16), channel_id=1, source_target_pairs={{0,160},{32,128},{64,224},{96,192},{128,32},{160,0},{192,96},{224,... | collective-permute-start | bytes 589832 | tf_op jit(solution)/shard_map/ppermute | solution.py:42
  41.9 2.1 %collective-permute-start.7 = (bf16[32,3072]{1,0:T(8,128)(2,1)S(1)}, bf16[32,3072]{1,0:T(8,128)(2,1)S(1)}, u32[]{:S(2)}, u32[]{:S(2)}) collective-permute-start(bf16[32,3072]{1,0:T(8,128)(2,1)S(1)} %pad_maximum_fusion.4), channel_id=1, source_target_pairs={{0,8},{1,25},{8,16},{9,1},{16,24},{17,9},{24,0},{25,17},{2,10},{3,... | collective-permute-start | bytes 589832 | tf_op jit(solution)/shard_map/ppermute | solution.py:38
  44.1 5.9 %collective-permute-start.11 = (bf16[32,3072]{1,0:T(8,128)(2,1)S(1)}, bf16[32,3072]{1,0:T(8,128)(2,1)S(1)}, u32[]{:S(2)}, u32[]{:S(2)}) collective-permute-start(bf16[32,3072]{1,0:T(8,128)(2,1)S(1)} %pad_maximum_fusion.7), channel_id=1, source_target_pairs={{0,224},{32,64},{64,32},{96,128},{128,96},{160,192},{192,160},{224... | collective-permute-start | bytes 589832 | tf_op jit(solution)/shard_map/ppermute | solution.py:42
  52.5 2.8 %collective-permute-done.15 = bf16[32,3072]{1,0:T(8,128)(2,1)S(1)} collective-permute-done((bf16[32,3072]{1,0:T(8,128)(2,1)S(1)}, bf16[32,3072]{1,0:T(8,128)(2,1)S(1)}, u32[]{:S(2)}, u32[]{:S(2)}) %collective-permute-start.15) | collective-permute-done | bytes 196640 | tf_op jit(solution)/shard_map/ppermute | solution.py:42
  55.3 3.0 %collective-permute-done.11 = bf16[32,3072]{1,0:T(8,128)(2,1)S(1)} collective-permute-done((bf16[32,3072]{1,0:T(8,128)(2,1)S(1)}, bf16[32,3072]{1,0:T(8,128)(2,1)S(1)}, u32[]{:S(2)}, u32[]{:S(2)}) %collective-permute-start.11) | collective-permute-done | bytes 196640 | tf_op jit(solution)/shard_map/ppermute | solution.py:42
  60.3 4.7 %collective-permute-done.16 = bf16[32,3072]{1,0:T(8,128)(2,1)S(1)} collective-permute-done((bf16[32,3072]{1,0:T(8,128)(2,1)S(1)}, bf16[32,3072]{1,0:T(8,128)(2,1)S(1)}, u32[]{:S(2)}, u32[]{:S(2)}) %collective-permute-start.16) | collective-permute-done | bytes 196640 | tf_op jit(solution)/shard_map/ppermute | solution.py:46
  65.3 4.6 %collective-permute-start.17 = (bf16[32,3072]{1,0:T(8,128)(2,1)S(1)}, bf16[32,3072]{1,0:T(8,128)(2,1)S(1)}, u32[]{:S(2)}, u32[]{:S(2)}) collective-permute-start(bf16[32,3072]{1,0:T(8,128)(2,1)S(1)} %pad_maximum_fusion.10), channel_id=1, source_target_pairs={{0,224},{32,64},{64,32},{96,128},{128,96},{160,192},{192,160},{224... | collective-permute-start | bytes 589832 | tf_op jit(solution)/shard_map/ppermute | solution.py:42
  70.0 3.6 %collective-permute-done.17 = bf16[32,3072]{1,0:T(8,128)(2,1)S(1)} collective-permute-done((bf16[32,3072]{1,0:T(8,128)(2,1)S(1)}, bf16[32,3072]{1,0:T(8,128)(2,1)S(1)}, u32[]{:S(2)}, u32[]{:S(2)}) %collective-permute-start.17) | collective-permute-done | bytes 196640 | tf_op jit(solution)/shard_map/ppermute | solution.py:42
  73.7 3.2 %collective-permute-start.18 = (bf16[64,3072]{1,0:T(8,128)(2,1)S(1)}, bf16[64,3072]{1,0:T(8,128)(2,1)S(1)}, u32[]{:S(2)}, u32[]{:S(2)}) collective-permute-start(bf16[64,3072]{1,0:T(8,128)(2,1)S(1)} %pad_maximum_fusion.3), channel_id=1, source_target_pairs={{0,8},{1,25},{8,16},{9,1},{16,24},{17,9},{24,0},{25,17},{2,10},{3,... | collective-permute-start | bytes 1179656 | tf_op jit(solution)/shard_map/ppermute | solution.py:38
  77.0 2.6 %collective-permute-start.22 = (bf16[32,3072]{1,0:T(8,128)(2,1)S(1)}, bf16[32,3072]{1,0:T(8,128)(2,1)S(1)}, u32[]{:S(2)}, u32[]{:S(2)}) collective-permute-start(bf16[32,3072]{1,0:T(8,128)(2,1)S(1)} %collective-permute-done.17), channel_id=1, source_target_pairs={{0,64},{32,224},{64,128},{96,32},{128,192},{160,96},{192,0},{224,1... | collective-permute-start | bytes 589832 | tf_op jit(solution)/shard_map/ppermute | solution.py:42
  79.7 5.6 %collective-permute-done.22 = bf16[32,3072]{1,0:T(8,128)(2,1)S(1)} collective-permute-done((bf16[32,3072]{1,0:T(8,128)(2,1)S(1)}, bf16[32,3072]{1,0:T(8,128)(2,1)S(1)}, u32[]{:S(2)}, u32[]{:S(2)}) %collective-permute-start.22) | collective-permute-done | bytes 196640 | tf_op jit(solution)/shard_map/ppermute | solution.py:42
  89.3 5.2 %collective-permute-done.23 = bf16[64,3072]{1,0:T(8,128)(2,1)S(1)} collective-permute-done((bf16[64,3072]{1,0:T(8,128)(2,1)S(1)}, bf16[64,3072]{1,0:T(8,128)(2,1)S(1)}, u32[]{:S(2)}, u32[]{:S(2)}) %collective-permute-start.23) | collective-permute-done | bytes 393248 | tf_op jit(solution)/shard_map/ppermute | solution.py:38
  96.0 2.6 %collective-permute-done.20 = bf16[64,3072]{1,0:T(8,128)(2,1)S(1)} collective-permute-done((bf16[64,3072]{1,0:T(8,128)(2,1)S(1)}, bf16[64,3072]{1,0:T(8,128)(2,1)S(1)}, u32[]{:S(2)}, u32[]{:S(2)}) %collective-permute-start.20) | collective-permute-done | bytes 393248 | tf_op jit(solution)/shard_map/ppermute | solution.py:38
  98.7 4.8 %collective-permute-done.24 = bf16[64,3072]{1,0:T(8,128)(2,1)S(1)} collective-permute-done((bf16[64,3072]{1,0:T(8,128)(2,1)S(1)}, bf16[64,3072]{1,0:T(8,128)(2,1)S(1)}, u32[]{:S(2)}, u32[]{:S(2)}) %collective-permute-start.24) | collective-permute-done | bytes 393248 | tf_op jit(solution)/shard_map/ppermute | solution.py:38
  105.1 2.2 %add_convert_fusion.1 = bf16[384,3072]{1,0:T(8,128)(2,1)} fusion(f32[384,3072]{1,0:T(8,128)S(1)} %convolution_add_fusion.1, bf16[160,3072]{1,0:T(8,128)(2,1)S(1)} %get-tuple-element.50, bf16[160,768]{1,0:T(8,128)(2,1)S(1)} %get-tuple-element.65), kind=kOutput, calls=%fused_computation.1 | convolution fusion | flops 379846656 | bytes 8183808 | tf_op jit(solution)/shard_map/dot_general | solution.py:13
  107.3 2.5 %collective-permute-start.29 = (f32[2,16,384]{2,1,0:T(8,128)S(1)}, f32[2,16,384]{2,1,0:T(8,128)S(1)}, u32[]{:S(2)}, u32[]{:S(2)}) collective-permute-start(f32[2,16,384]{2,1,0:T(8,128)S(1)} %fusion.39), channel_id=1, source_target_pairs={{0,6},{1,3},{2,0},{3,5},{4,2},{5,7},{6,4},{7,1},{8,14},{9,11},{10,... | collective-permute-start | bytes 147464 | tf_op jit(solution)/shard_map/ppermute | solution.py:38
  110.8 2.4 %add_convert_fusion = bf16[3072,384]{1,0:T(8,128)(2,1)} fusion(f32[3072,384]{1,0:T(8,128)S(1)} %convolution_add_fusion, bf16[160,3072]{1,0:T(8,128)(2,1)S(1)} %get-tuple-element.49, bf16[160,768]{1,0:T(8,128)(2,1)S(1)} %get-tuple-element.65), kind=kOutput, calls=%fused_computation | convolution fusion | flops 379846656 | bytes 8183808 | tf_op jit(solution)/shard_map/dot_general | solution.py:13
  113.3 2.3 %collective-permute-done.27 = f32[2,16,384]{2,1,0:T(8,128)S(1)} collective-permute-done((f32[2,16,384]{2,1,0:T(8,128)S(1)}, f32[2,16,384]{2,1,0:T(8,128)S(1)}, u32[]{:S(2)}, u32[]{:S(2)}) %collective-permute-start.27) | collective-permute-done | bytes 49184 | tf_op jit(solution)/shard_map/ppermute | solution.py:28
  (130 shorter events, 28.7 us)
Async XLA Ops:
  2.8 8.7 %collective-permute-start.2 = (bf16[4,16,768]{2,1,0:T(8,128)(2,1)S(1)}, bf16[4,16,768]{2,1,0:T(8,128)(2,1)S(1)}, u32[]{:S(2)}, u32[]{:S(2)}) collective-permute-start(bf16[4,16,768]{2,1,0:T(8,128)(2,1)S(1)} %pad_maximum_fusion.11), channel_id=1, source_target_pairs={{0,4},{2,6},{4,0},{6,2},{1,5},{3,7},{5,1},{7,3},{8,12},{10,14},{12... | collective-permute-start | bytes 294920 | tf_op jit(solution)/shard_map/ppermute | solution.py:28
  17.1 7.9 %collective-permute-start.12 = (bf16[32,3072]{1,0:T(8,128)(2,1)S(1)}, bf16[32,3072]{1,0:T(8,128)(2,1)S(1)}, u32[]{:S(2)}, u32[]{:S(2)}) collective-permute-start(bf16[32,3072]{1,0:T(8,128)(2,1)S(1)} %pad_maximum_fusion.8), channel_id=1, source_target_pairs={{0,8},{1,25},{8,16},{9,1},{16,24},{17,9},{24,0},{25,17},{2,10},{3,... | collective-permute-start | bytes 589832 | tf_op jit(solution)/shard_map/ppermute | solution.py:38
  17.6 17.2 %collective-permute-start.14 = (bf16[32,3072]{1,0:T(8,128)(2,1)S(1)}, bf16[32,3072]{1,0:T(8,128)(2,1)S(1)}, u32[]{:S(2)}, u32[]{:S(2)}) collective-permute-start(bf16[32,3072]{1,0:T(8,128)(2,1)S(1)} %pad_maximum_fusion.9), channel_id=1, source_target_pairs={{0,24},{1,9},{8,0},{9,17},{16,8},{17,25},{24,16},{25,1},{2,26},{3,... | collective-permute-start | bytes 589832 | tf_op jit(solution)/shard_map/ppermute | solution.py:38
  19.3 22.4 %collective-permute-start.6 = (bf16[64,3072]{1,0:T(8,128)(2,1)S(1)}, bf16[64,3072]{1,0:T(8,128)(2,1)S(1)}, u32[]{:S(2)}, u32[]{:S(2)}) collective-permute-start(bf16[64,3072]{1,0:T(8,128)(2,1)S(1)} %pad_maximum_fusion.2), channel_id=1, source_target_pairs={{0,24},{1,9},{8,0},{9,17},{16,8},{17,25},{24,16},{25,1},{2,26},{3,... | collective-permute-start | bytes 1179656 | tf_op jit(solution)/shard_map/ppermute | solution.py:38
  20.1 11.0 %collective-permute-start.4 = (bf16[64,3072]{1,0:T(8,128)(2,1)S(1)}, bf16[64,3072]{1,0:T(8,128)(2,1)S(1)}, u32[]{:S(2)}, u32[]{:S(2)}) collective-permute-start(bf16[64,3072]{1,0:T(8,128)(2,1)S(1)} %pad_maximum_fusion.1), channel_id=1, source_target_pairs={{0,8},{1,25},{8,16},{9,1},{16,24},{17,9},{24,0},{25,17},{2,10},{3,... | collective-permute-start | bytes 1179656 | tf_op jit(solution)/shard_map/ppermute | solution.py:38
  25.0 9.8 %collective-permute-start.13 = (bf16[32,3072]{1,0:T(8,128)(2,1)S(1)}, bf16[32,3072]{1,0:T(8,128)(2,1)S(1)}, u32[]{:S(2)}, u32[]{:S(2)}) collective-permute-start(bf16[32,3072]{1,0:T(8,128)(2,1)S(1)} %fusion.17), channel_id=1, source_target_pairs={{0,8},{1,25},{8,16},{9,1},{16,24},{17,9},{24,0},{25,17},{2,10},{3,... | collective-permute-start | bytes 589832 | tf_op jit(solution)/shard_map/ppermute | solution.py:38
  31.2 10.5 %collective-permute-start.5 = (bf16[64,3072]{1,0:T(8,128)(2,1)S(1)}, bf16[64,3072]{1,0:T(8,128)(2,1)S(1)}, u32[]{:S(2)}, u32[]{:S(2)}) collective-permute-start(bf16[64,3072]{1,0:T(8,128)(2,1)S(1)} %fusion.2), channel_id=1, source_target_pairs={{0,8},{1,25},{8,16},{9,1},{16,24},{17,9},{24,0},{25,17},{2,10},{3,... | collective-permute-start | bytes 1179656 | tf_op jit(solution)/shard_map/ppermute | solution.py:38
  34.9 20.4 %collective-permute-start.15 = (bf16[32,3072]{1,0:T(8,128)(2,1)S(1)}, bf16[32,3072]{1,0:T(8,128)(2,1)S(1)}, u32[]{:S(2)}, u32[]{:S(2)}) collective-permute-start(bf16[32,3072]{1,0:T(8,128)(2,1)S(1)} %fusion.16), channel_id=1, source_target_pairs={{0,160},{32,128},{64,224},{96,192},{128,32},{160,0},{192,96},{224,... | collective-permute-start | bytes 589832 | tf_op jit(solution)/shard_map/ppermute | solution.py:42
  41.9 8.4 %collective-permute-start.7 = (bf16[32,3072]{1,0:T(8,128)(2,1)S(1)}, bf16[32,3072]{1,0:T(8,128)(2,1)S(1)}, u32[]{:S(2)}, u32[]{:S(2)}) collective-permute-start(bf16[32,3072]{1,0:T(8,128)(2,1)S(1)} %pad_maximum_fusion.4), channel_id=1, source_target_pairs={{0,8},{1,25},{8,16},{9,1},{16,24},{17,9},{24,0},{25,17},{2,10},{3,... | collective-permute-start | bytes 589832 | tf_op jit(solution)/shard_map/ppermute | solution.py:38
  44.1 14.2 %collective-permute-start.11 = (bf16[32,3072]{1,0:T(8,128)(2,1)S(1)}, bf16[32,3072]{1,0:T(8,128)(2,1)S(1)}, u32[]{:S(2)}, u32[]{:S(2)}) collective-permute-start(bf16[32,3072]{1,0:T(8,128)(2,1)S(1)} %pad_maximum_fusion.7), channel_id=1, source_target_pairs={{0,224},{32,64},{64,32},{96,128},{128,96},{160,192},{192,160},{224... | collective-permute-start | bytes 589832 | tf_op jit(solution)/shard_map/ppermute | solution.py:42
  50.0 8.3 %collective-permute-start.10 = (bf16[32,3072]{1,0:T(8,128)(2,1)S(1)}, bf16[32,3072]{1,0:T(8,128)(2,1)S(1)}, u32[]{:S(2)}, u32[]{:S(2)}) collective-permute-start(bf16[32,3072]{1,0:T(8,128)(2,1)S(1)} %pad_maximum_fusion.6), channel_id=1, source_target_pairs={{0,64},{32,224},{64,128},{96,32},{128,192},{160,96},{192,0},{224,1... | collective-permute-start | bytes 589832 | tf_op jit(solution)/shard_map/ppermute | solution.py:42
  50.3 8.0 %collective-permute-start.8 = (bf16[32,3072]{1,0:T(8,128)(2,1)S(1)}, bf16[32,3072]{1,0:T(8,128)(2,1)S(1)}, u32[]{:S(2)}, u32[]{:S(2)}) collective-permute-start(bf16[32,3072]{1,0:T(8,128)(2,1)S(1)} %fusion.14), channel_id=1, source_target_pairs={{0,8},{1,25},{8,16},{9,1},{16,24},{17,9},{24,0},{25,17},{2,10},{3,... | collective-permute-start | bytes 589832 | tf_op jit(solution)/shard_map/ppermute | solution.py:38
  51.0 7.4 %collective-permute-start.9 = (bf16[32,3072]{1,0:T(8,128)(2,1)S(1)}, bf16[32,3072]{1,0:T(8,128)(2,1)S(1)}, u32[]{:S(2)}, u32[]{:S(2)}) collective-permute-start(bf16[32,3072]{1,0:T(8,128)(2,1)S(1)} %pad_maximum_fusion.5), channel_id=1, source_target_pairs={{0,24},{1,9},{8,0},{9,17},{16,8},{17,25},{24,16},{25,1},{2,26},{3,... | collective-permute-start | bytes 589832 | tf_op jit(solution)/shard_map/ppermute | solution.py:38
  58.5 6.6 %collective-permute-start.16 = (bf16[32,3072]{1,0:T(8,128)(2,1)S(1)}, bf16[32,3072]{1,0:T(8,128)(2,1)S(1)}, u32[]{:S(2)}, u32[]{:S(2)}) collective-permute-start(bf16[32,3072]{1,0:T(8,128)(2,1)S(1)} %fusion.47), channel_id=1, source_target_pairs={{0,32},{32,0},{64,96},{96,64},{128,160},{160,128},{192,224},{224,1... | collective-permute-start | bytes 589832 | tf_op jit(solution)/shard_map/ppermute | solution.py:46
  65.3 8.3 %collective-permute-start.17 = (bf16[32,3072]{1,0:T(8,128)(2,1)S(1)}, bf16[32,3072]{1,0:T(8,128)(2,1)S(1)}, u32[]{:S(2)}, u32[]{:S(2)}) collective-permute-start(bf16[32,3072]{1,0:T(8,128)(2,1)S(1)} %pad_maximum_fusion.10), channel_id=1, source_target_pairs={{0,224},{32,64},{64,32},{96,128},{128,96},{160,192},{192,160},{224... | collective-permute-start | bytes 589832 | tf_op jit(solution)/shard_map/ppermute | solution.py:42
  73.6 6.0 %collective-permute-start.21 = (bf16[32,3072]{1,0:T(8,128)(2,1)S(1)}, bf16[32,3072]{1,0:T(8,128)(2,1)S(1)}, u32[]{:S(2)}, u32[]{:S(2)}) collective-permute-start(bf16[32,3072]{1,0:T(8,128)(2,1)S(1)} %collective-permute-done.17), channel_id=1, source_target_pairs={{0,32},{32,0},{64,96},{96,64},{128,160},{160,128},{192,224},{224,1... | collective-permute-start | bytes 589832 | tf_op jit(solution)/shard_map/ppermute | solution.py:46
  73.6 13.9 %collective-permute-start.19 = (bf16[64,3072]{1,0:T(8,128)(2,1)S(1)}, bf16[64,3072]{1,0:T(8,128)(2,1)S(1)}, u32[]{:S(2)}, u32[]{:S(2)}) collective-permute-start(bf16[64,3072]{1,0:T(8,128)(2,1)S(1)} %pad_maximum_fusion.3), channel_id=1, source_target_pairs={{0,24},{1,9},{8,0},{9,17},{16,8},{17,25},{24,16},{25,1},{2,26},{3,... | collective-permute-start | bytes 1179656 | tf_op jit(solution)/shard_map/ppermute | solution.py:38
  73.7 13.7 %collective-permute-start.18 = (bf16[64,3072]{1,0:T(8,128)(2,1)S(1)}, bf16[64,3072]{1,0:T(8,128)(2,1)S(1)}, u32[]{:S(2)}, u32[]{:S(2)}) collective-permute-start(bf16[64,3072]{1,0:T(8,128)(2,1)S(1)} %pad_maximum_fusion.3), channel_id=1, source_target_pairs={{0,8},{1,25},{8,16},{9,1},{16,24},{17,9},{24,0},{25,17},{2,10},{3,... | collective-permute-start | bytes 1179656 | tf_op jit(solution)/shard_map/ppermute | solution.py:38
  77.0 8.3 %collective-permute-start.22 = (bf16[32,3072]{1,0:T(8,128)(2,1)S(1)}, bf16[32,3072]{1,0:T(8,128)(2,1)S(1)}, u32[]{:S(2)}, u32[]{:S(2)}) collective-permute-start(bf16[32,3072]{1,0:T(8,128)(2,1)S(1)} %collective-permute-done.17), channel_id=1, source_target_pairs={{0,64},{32,224},{64,128},{96,32},{128,192},{160,96},{192,0},{224,1... | collective-permute-start | bytes 589832 | tf_op jit(solution)/shard_map/ppermute | solution.py:42
  85.3 18.2 %collective-permute-start.25 = (bf16[64,3072]{1,0:T(8,128)(2,1)S(1)}, bf16[64,3072]{1,0:T(8,128)(2,1)S(1)}, u32[]{:S(2)}, u32[]{:S(2)}) collective-permute-start(bf16[64,3072]{1,0:T(8,128)(2,1)S(1)} %constant_dynamic-update-slice_fusion.14), channel_id=1, source_target_pairs={{0,8},{1,25},{8,16},{9,1},{16,24},{17,9},{24,0},{25,17},{2,10},{3,... | collective-permute-start | bytes 1179656 | tf_op jit(solution)/shard_map/ppermute | solution.py:38
  85.4 9.1 %collective-permute-start.23 = (bf16[64,3072]{1,0:T(8,128)(2,1)S(1)}, bf16[64,3072]{1,0:T(8,128)(2,1)S(1)}, u32[]{:S(2)}, u32[]{:S(2)}) collective-permute-start(bf16[64,3072]{1,0:T(8,128)(2,1)S(1)} %constant_dynamic-update-slice_fusion.14), channel_id=1, source_target_pairs={{0,24},{1,9},{8,0},{9,17},{16,8},{17,25},{24,16},{25,1},{2,26},{3,... | collective-permute-start | bytes 1179656 | tf_op jit(solution)/shard_map/ppermute | solution.py:38
  89.2 9.5 %collective-permute-start.20 = (bf16[64,3072]{1,0:T(8,128)(2,1)S(1)}, bf16[64,3072]{1,0:T(8,128)(2,1)S(1)}, u32[]{:S(2)}, u32[]{:S(2)}) collective-permute-start(bf16[64,3072]{1,0:T(8,128)(2,1)S(1)} %collective-permute-done.19), channel_id=1, source_target_pairs={{0,24},{1,9},{8,0},{9,17},{16,8},{17,25},{24,16},{25,1},{2,26},{3,... | collective-permute-start | bytes 1179656 | tf_op jit(solution)/shard_map/ppermute | solution.py:38
  94.5 9.0 %collective-permute-start.24 = (bf16[64,3072]{1,0:T(8,128)(2,1)S(1)}, bf16[64,3072]{1,0:T(8,128)(2,1)S(1)}, u32[]{:S(2)}, u32[]{:S(2)}) collective-permute-start(bf16[64,3072]{1,0:T(8,128)(2,1)S(1)} %collective-permute-done.23), channel_id=1, source_target_pairs={{0,24},{1,9},{8,0},{9,17},{16,8},{17,25},{24,16},{25,1},{2,26},{3,... | collective-permute-start | bytes 1179656 | tf_op jit(solution)/shard_map/ppermute | solution.py:38
  107.3 5.9 %collective-permute-start.29 = (f32[2,16,384]{2,1,0:T(8,128)S(1)}, f32[2,16,384]{2,1,0:T(8,128)S(1)}, u32[]{:S(2)}, u32[]{:S(2)}) collective-permute-start(f32[2,16,384]{2,1,0:T(8,128)S(1)} %fusion.39), channel_id=1, source_target_pairs={{0,6},{1,3},{2,0},{3,5},{4,2},{5,7},{6,4},{7,1},{8,14},{9,11},{10,... | collective-permute-start | bytes 147464 | tf_op jit(solution)/shard_map/ppermute | solution.py:38
  (8 other events, 42.6 us)
